TPU v7x, 32 devices: a whole 2x2x4 slice. The times are simulated.
32 devices in a mesh: seq: 4 (over y, x), fsdp: 8 (over z, core).
Axes of the slice: x: 2, y: 2, z: 4, core: 2. Of those that a mesh axis runs over, the one named last changes fastest.
Arguments:
- tokens: bfloat16 [2, 2048, 2304], P(None, ('seq', 'fsdp')), may hold values from -6 to 6
- attn_weight: bfloat16 [6144, 2304], P('fsdp'), may hold values from -0.23570226 to 0.23570226
- norm_gains: bfloat16 [4, 2304], P(None, 'fsdp'), may hold values from 0.25 to 1.75
- ffn_weight: bfloat16 [9216, 3, 2304], P('fsdp'), may hold values from -0.125 to 0.125
- out_grad: bfloat16 [2, 2048, 2304], P(None, ('seq', 'fsdp')), may hold values from -6 to 6
Outputs:
- block_out: bfloat16 [2, 2048, 2304], P(None, ('seq', 'fsdp'))
- token_grad: float32 [2, 2048, 2304], P(None, ('seq', 'fsdp'))
- attn_weight_grad: float32 [6144, 2304], P('fsdp')
- gain_grad: float32 [4, 2304], P(None, 'fsdp')
- ffn_weight_grad: float32 [9216, 3, 2304], P('fsdp')
All inputs are finite; a program needn't handle non-finite values.
Results may differ from a plain program's by a relative error of at most 0.025.
The roundings to bfloat16 on the way count: a program that leaves them out, or rounds other values in their place, can miss the bound.
Values may be sent and summed in bfloat16 or wider, within the bound.
No kernel may reach another device: no remote copies, remote signals or barrier semaphores. Data moves between devices by JAX's collectives and lax.ppermute only.
A program may use at most 320 MiB of HBM per device.

v0:
```python
import jax
import jax.numpy as jnp
from jax import lax
from jax.sharding import PartitionSpec as P

HQ = 8
KVH = 4
HD = 256


soft_cap = 50.0
norm_eps = 1e-06


def rms_scale(values, gain_row):
    return (
        values * lax.rsqrt(jnp.mean(values * values, axis=-1, keepdims=True) + norm_eps) * gain_row
    )


def norm_back(values, gain_row, cotangent):
    inverse = lax.rsqrt(jnp.mean(values * values, axis=-1, keepdims=True) + norm_eps)
    unit_rows = values * inverse
    scaled = cotangent * gain_row
    grad_values = inverse * (
        scaled - unit_rows * jnp.mean(scaled * unit_rows, axis=-1, keepdims=True)
    )
    return (grad_values, cotangent * unit_rows)


def gated_units(gate_proj, up_proj):
    return jax.nn.gelu(gate_proj, approximate=True) * up_proj


def own_rows(group_rows, fsdp_index, seq_count, fsdp_count, row_count):
    feature_count = group_rows.shape[-1]
    shaped = group_rows.reshape(seq_count, fsdp_count, row_count, feature_count)
    picked = lax.dynamic_index_in_dim(shaped, fsdp_index, 1, keepdims=False)
    return picked.reshape(seq_count * row_count, feature_count)


def local(tokens, attn_weight, norm_gains, ffn_weight, out_grad):
    seq_count, row_count, model_width = tokens.shape
    seq_devices = lax.axis_size("seq")
    fsdp_count = lax.axis_size("fsdp")
    fsdp_index = lax.axis_index("fsdp")
    heads_local = HQ // seq_devices
    block_rows = row_count * fsdp_count
    key_count = block_rows * seq_devices
    query_width = HQ * HD
    kv_width = KVH * HD
    group_size = HQ // KVH
    score_scale = HD ** (-0.5)
    attn_full, gain_full = (
        lax.all_gather(attn_weight, "fsdp", axis=0, tiled=True),
        lax.all_gather(norm_gains, "fsdp", axis=1, tiled=True),
    )
    gain_rows = gain_full.astype(jnp.float32)
    proj_in = attn_full[: query_width + 2 * kv_width]
    proj_out = attn_full[query_width + 2 * kv_width :]
    flat_tokens = tokens.reshape(-1, model_width).astype(jnp.float32)
    flat_cot = out_grad.reshape(-1, model_width).astype(jnp.float32)
    normed = rms_scale(flat_tokens, gain_rows[0]).astype(jnp.bfloat16)
    projected = jnp.einsum("td,rd->tr", normed, proj_in, preferred_element_type=jnp.float32).astype(
        jnp.bfloat16
    )
    queries = projected[:, :query_width].reshape(seq_count, 1, row_count, query_width)

    def copied(part_rows):
        spread = jnp.broadcast_to(
            part_rows.reshape(seq_count, row_count, KVH, 1, HD),
            (seq_count, row_count, KVH, group_size, HD),
        )
        return spread.reshape(seq_count, 1, row_count, query_width)

    key_rows = copied(projected[:, query_width : query_width + kv_width])
    value_rows = copied(projected[:, query_width + kv_width :])
    query_heads, key_heads, value_heads = (
        lax.all_to_all(queries, "seq", split_axis=3, concat_axis=1, tiled=True),
        lax.all_to_all(key_rows, "seq", split_axis=3, concat_axis=1, tiled=True),
        lax.all_to_all(value_rows, "seq", split_axis=3, concat_axis=1, tiled=True),
    )
    key_all, value_all = (
        lax.all_gather(key_heads, "fsdp", axis=2, tiled=True),
        lax.all_gather(value_heads, "fsdp", axis=2, tiled=True),
    )
    head_shape = (seq_count, -1, heads_local, HD)
    query_seqs = query_heads.reshape(head_shape)
    key_seqs = key_all.reshape(head_shape)
    value_seqs = value_all.reshape(head_shape)
    query_pos = (
        jnp.arange(seq_devices, dtype=jnp.int32)[:, None] * block_rows
        + fsdp_index * row_count
        + jnp.arange(row_count, dtype=jnp.int32)[None, :]
    ).reshape(-1)
    causal = jnp.arange(key_count, dtype=jnp.int32)[None, :] <= query_pos[:, None]

    def scores_of(query_block, key_block):
        raw_scores = (
            jnp.einsum("qhd,khd->hqk", query_block, key_block, preferred_element_type=jnp.float32)
            * score_scale
        )
        bounded = jnp.tanh(raw_scores / soft_cap)
        return (bounded, jnp.where(causal[None], soft_cap * bounded, -1e30))

    def forward_seq(block_item):
        query_block, key_block, value_block = block_item
        bounded, capped = scores_of(query_block, key_block)
        row_max = jnp.max(capped, axis=-1, keepdims=True)
        expanded = jnp.exp(capped - row_max)
        row_total = jnp.sum(expanded, axis=-1, keepdims=True)
        softmax_weights = (expanded / row_total).astype(jnp.bfloat16)
        mixed_block = jnp.einsum(
            "hqk,khd->qhd", softmax_weights, value_block, preferred_element_type=jnp.float32
        )
        return (mixed_block.astype(jnp.bfloat16), (row_max + jnp.log(row_total))[..., 0])

    mixed_seqs, log_total = lax.map(forward_seq, (query_seqs, key_seqs, value_seqs))
    local_shape = (seq_count, seq_devices, row_count, heads_local * HD)
    mixed = lax.all_to_all(
        mixed_seqs.reshape(local_shape), "seq", split_axis=1, concat_axis=3, tiled=True
    ).reshape(-1, query_width)
    attn_out = jnp.dot(mixed, proj_out, preferred_element_type=jnp.float32)
    residual = flat_tokens + rms_scale(attn_out, gain_rows[1])
    normed_ffn = rms_scale(residual, gain_rows[2]).astype(jnp.bfloat16)
    group_in, group_grad = (
        lax.all_gather(
            normed_ffn.reshape(seq_count, row_count, model_width), "fsdp", axis=1, tiled=True
        ),
        lax.all_gather(out_grad, "fsdp", axis=1, tiled=True),
    )
    ffn_in = group_in.reshape(-1, model_width)
    gate_up = jnp.einsum(
        "td,fgd->tgf", ffn_in, ffn_weight[:, :2], preferred_element_type=jnp.float32
    )
    hidden = gated_units(gate_up[:, 0], gate_up[:, 1]).astype(jnp.bfloat16)
    branch = jnp.dot(hidden, ffn_weight[:, 2], preferred_element_type=jnp.float32)
    branch_rows = lax.psum(branch.astype(jnp.bfloat16), "fsdp").astype(jnp.float32)
    branch_cot = group_grad.reshape(-1, model_width).astype(jnp.float32)
    ffn_out = own_rows(branch_rows, fsdp_index, seq_count, fsdp_count, row_count)
    result = residual + rms_scale(ffn_out, gain_rows[3])
    block_out = result.astype(jnp.bfloat16).reshape(seq_count, row_count, model_width)
    grad_ffn, gain_terms = norm_back(branch_rows, gain_rows[3], branch_cot)
    grad_ffn_low = grad_ffn.astype(jnp.bfloat16)
    grad_hidden = jnp.einsum(
        "td,fd->tf", grad_ffn_low, ffn_weight[:, 2], preferred_element_type=jnp.float32
    )
    unused, gated_pull = jax.vjp(gated_units, gate_up[:, 0], gate_up[:, 1])
    grad_gate, grad_up = gated_pull(grad_hidden)
    grad_gate_up = jnp.stack([grad_gate, grad_up], axis=1).astype(jnp.bfloat16)
    grad_in = jnp.einsum(
        "tgf,fgd->td", grad_gate_up, ffn_weight[:, :2], preferred_element_type=jnp.float32
    )
    gain_last = jnp.sum(own_rows(gain_terms, fsdp_index, seq_count, fsdp_count, row_count), axis=0)
    grad_normed_ffn = (
        lax.psum_scatter(
            grad_in.reshape(seq_count, block_rows, model_width).astype(jnp.bfloat16),
            "fsdp",
            scatter_dimension=1,
            tiled=True,
        )
        .astype(jnp.float32)
        .reshape(-1, model_width)
    )
    upper = jnp.einsum("tgf,td->fgd", grad_gate_up, ffn_in, preferred_element_type=jnp.float32)
    lower = jnp.einsum("tf,td->fd", hidden, grad_ffn_low, preferred_element_type=jnp.float32)
    ffn_grad = jnp.concatenate([upper, lower[:, None]], axis=1)
    grad_mid, gain_pre_ffn = norm_back(residual, gain_rows[2], grad_normed_ffn)
    grad_residual = flat_cot + grad_mid
    grad_attn, gain_post_attn = norm_back(attn_out, gain_rows[1], grad_residual)
    grad_attn_low = grad_attn.astype(jnp.bfloat16)
    out_proj_grad = jnp.einsum(
        "tr,td->rd", mixed, grad_attn_low, preferred_element_type=jnp.float32
    )
    grad_mixed = jnp.einsum(
        "td,rd->tr", grad_attn_low, proj_out, preferred_element_type=jnp.float32
    ).astype(jnp.bfloat16)
    grad_heads = lax.all_to_all(
        grad_mixed.reshape(seq_count, 1, row_count, query_width),
        "seq",
        split_axis=3,
        concat_axis=1,
        tiled=True,
    )
    grad_head_seqs = grad_heads.reshape(head_shape)

    def backward_seq(block_item):
        query_block, key_block, value_block, grad_block, log_block = block_item
        bounded, capped = scores_of(query_block, key_block)
        softmax_weights = jnp.exp(capped - log_block[..., None])
        grad_weights = jnp.einsum(
            "qhd,khd->hqk", grad_block, value_block, preferred_element_type=jnp.float32
        )
        grad_values = jnp.einsum(
            "hqk,qhd->khd",
            softmax_weights.astype(jnp.bfloat16),
            grad_block,
            preferred_element_type=jnp.float32,
        )
        row_dot = jnp.sum(softmax_weights * grad_weights, axis=-1, keepdims=True)
        grad_raw = (softmax_weights * (grad_weights - row_dot) * (1.0 - bounded * bounded)).astype(
            jnp.bfloat16
        )
        grad_query = (
            jnp.einsum("hqk,khd->qhd", grad_raw, key_block, preferred_element_type=jnp.float32)
            * score_scale
        )
        grad_key = (
            jnp.einsum("hqk,qhd->khd", grad_raw, query_block, preferred_element_type=jnp.float32)
            * score_scale
        )
        return (grad_query, grad_key, grad_values)

    grad_q, grad_k, grad_v = lax.map(
        backward_seq, (query_seqs, key_seqs, value_seqs, grad_head_seqs, log_total)
    )
    kv_shape = (seq_count, seq_devices, block_rows, heads_local * HD)
    grad_k_own, grad_v_own = (
        lax.psum_scatter(
            grad_k.reshape(kv_shape).astype(jnp.bfloat16), "fsdp", scatter_dimension=2, tiled=True
        ).astype(jnp.float32),
        lax.psum_scatter(
            grad_v.reshape(kv_shape).astype(jnp.bfloat16), "fsdp", scatter_dimension=2, tiled=True
        ).astype(jnp.float32),
    )
    back_q, back_k, back_v = (
        lax.all_to_all(
            grad_q.reshape(local_shape).astype(jnp.bfloat16),
            "seq",
            split_axis=1,
            concat_axis=3,
            tiled=True,
        ).astype(jnp.float32),
        lax.all_to_all(
            grad_k_own.astype(jnp.bfloat16), "seq", split_axis=1, concat_axis=3, tiled=True
        ).astype(grad_k_own.dtype),
        lax.all_to_all(
            grad_v_own.astype(jnp.bfloat16), "seq", split_axis=1, concat_axis=3, tiled=True
        ).astype(grad_v_own.dtype),
    )

    def summed_copies(part_rows):
        return (
            part_rows.reshape(seq_count * row_count, KVH, group_size, HD)
            .sum(axis=2)
            .reshape(-1, kv_width)
        )

    grad_proj = jnp.concatenate(
        [back_q.reshape(-1, query_width), summed_copies(back_k), summed_copies(back_v)], axis=1
    ).astype(jnp.bfloat16)
    grad_normed = jnp.einsum("tr,rd->td", grad_proj, proj_in, preferred_element_type=jnp.float32)
    in_proj_grad = jnp.einsum("tr,td->rd", grad_proj, normed, preferred_element_type=jnp.float32)
    grad_tokens, gain_pre_attn = norm_back(flat_tokens, gain_rows[0], grad_normed)
    token_grad = (grad_residual + grad_tokens).reshape(seq_count, row_count, model_width)
    gain_grad = jnp.stack(
        [
            jnp.sum(gain_pre_attn, axis=0),
            jnp.sum(gain_post_attn, axis=0),
            jnp.sum(gain_pre_ffn, axis=0),
            gain_last,
        ]
    )
    attn_grad_full = jnp.concatenate([in_proj_grad, out_proj_grad], axis=0)
    attn_shard, gain_shard = (
        lax.psum_scatter(
            attn_grad_full.astype(jnp.bfloat16), "fsdp", scatter_dimension=0, tiled=True
        ).astype(jnp.float32),
        lax.psum_scatter(
            gain_grad.astype(jnp.bfloat16), "fsdp", scatter_dimension=1, tiled=True
        ).astype(jnp.float32),
    )
    attn_total, gain_total, ffn_total = (
        lax.psum(attn_shard.astype(jnp.bfloat16), "seq").astype(jnp.float32),
        lax.psum(gain_shard.astype(jnp.bfloat16), "seq").astype(jnp.float32),
        lax.psum(ffn_grad.astype(jnp.bfloat16), "seq").astype(jnp.float32),
    )
    return (block_out, token_grad, attn_total, gain_total, ffn_total)


def solution(mesh):
    in_specs = (
        P(None, ("seq", "fsdp"), None),
        P("fsdp", None),
        P(None, "fsdp"),
        P("fsdp", None, None),
        P(None, ("seq", "fsdp"), None),
    )
    out_specs = (
        P(None, ("seq", "fsdp"), None),
        P(None, ("seq", "fsdp"), None),
        P("fsdp", None),
        P(None, "fsdp"),
        P("fsdp", None, None),
    )
    return jax.shard_map(local, mesh=mesh, in_specs=in_specs, out_specs=out_specs, check_vma=False)
```

profile of v0, /device:TPU:0, one launch (start us, length us, event | category | flops | bytes accessed | tf_op | source)
XLA Modules:
  0.0 1752.8 jit_solution(18150564379613219699)
XLA Ops:
  9.3 15.7 all-gather.2
  25.8 232.2 %all-gather.9.cloned.1.call-done = bf16[6144,2304]{1,0:T(8,128)(2,1)} async-done(((bf16[768,2304]{1,0:T(8,128)(2,1)}), bf16[6144,2304]{1,0:T(8,128)(2,1)}) %all-gather.9.cloned.1.call-update) | async-done | bytes 28311568 | tf_op jit(solution)/shard_map/all_gather | solution.py:55
  258.0 12.5 fusion.126
  318.7 13.9 all-gather.15.cloned.1.call-done
  344.7 35.5 %all-gather.17.cloned.1.call-done = bf16[2,4,1,512,512]{4,1,3,0,2:T(4,128)(2,1)} async-done(((bf16[2,4,1,64,512]{4,1,3,0,2:T(4,128)(2,1)}), bf16[2,4,1,512,512]{4,1,3,0,2:T(4,128)(2,1)}) %all-gather.17.cloned.1.call-update) | async-done | bytes 4194320 | tf_op jit(solution)/shard_map/all_gather | solution.py:84
  396.9 30.1 %while.32 = (s32[]{:T(128)}, bf16[2,256,2,256]{1,3,2,0:T(8,128)(2,1)}, f32[2,2,256]{2,1,0:T(2,128)S(1)}, bf16[2,2048,2,256]{3,2,1,0:T(2,128)(2,1)}, bf16[2,256,2...) while((s32[]{:T(128)}, ...), condition=%wide.region_4.5_spmd.clone, body=%wide.region_1.4_spmd.clone.sunk | while | flops 1083833856 | bytes 39340220 | solution.py:118
  449.6 48.9 %all-gather.11.cloned.1.call-done = bf16[2,512,2304]{2,1,0:T(8,128)(2,1)} async-done(((bf16[2,64,2304]{2,1,0:T(8,128)(2,1)}), bf16[2,512,2304]{2,1,0:T(8,128)(2,1)}) %all-gather.11.cloned.1.call-update) | async-done | bytes 4718608 | tf_op jit(solution)/shard_map/all_gather | solution.py:127
  498.5 16.6 fusion.118
  530.5 104.8 %all-reduce.4.cloned.1.call-done = bf16[1024,2304]{1,0:T(8,128)(2,1)} async-done(((bf16[1024,2304]{1,0:T(8,128)(2,1)}), bf16[1024,2304]{1,0:T(8,128)(2,1)}) %all-reduce.4.cloned.1.call-update) | async-done | bytes 4718608 | tf_op jit(solution)/shard_map/psum | solution.py:138
  638.7 49.8 %all-gather.13.cloned.1.call-done = bf16[2,512,2304]{2,1,0:T(8,128)(2,1)} async-done(((bf16[2,64,2304]{2,1,0:T(8,128)(2,1)}), bf16[2,512,2304]{2,1,0:T(8,128)(2,1)}) %all-gather.13.cloned.1.call-update) | async-done | bytes 4718608 | tf_op jit(solution)/shard_map/all_gather | solution.py:130
  701.5 14.7 fusion.160
  716.2 16.4 bitcast_convert_fusion
  737.2 49.4 %reduce-scatter.8.cloned.1.call-done = bf16[2,64,2304]{2,1,0:T(8,128)(2,1)} async-done(((bf16[2,512,2304]{2,1,0:T(8,128)(2,1)}), bf16[2,64,2304]{2,1,0:T(8,128)(2,1)}) %reduce-scatter.8.cloned.1.call-update) | async-done | bytes 589840 | tf_op jit(solution)/shard_map/reduce_scatter | solution.py:156
  815.5 73.9 %while.33 = (s32[]{:T(128)}, bf16[2,256,2,256]{1,3,2,0:T(8,128)(2,1)}, bf16[2,2048,2,256]{1,3,2,0:T(8,128)(2,1)}, bf16[2,2048,2,256]{1,3,2,0:T(8,128)(2,1)}, bf1...) while((s32[]{:T(128)}, ...), condition=%wide.region_16.17_spmd.clone, body=%wide.region_14.16_spmd.clone.sunk | while | flops 2718569472 | bytes 91244752 | solution.py:214
  932.0 21.9 %reduce-scatter.12.cloned.1.call-done = bf16[2,4,64,512]{3,2,0,1:T(8,128)(2,1)} async-done(((bf16[2,4,512,512]{3,2,0,1:T(8,128)(2,1)}), bf16[2,4,64,512]{3,2,0,1:T(8,128)(2,1)}) %reduce-scatter.12.cloned.1.call-update) | async-done | bytes 524304 | tf_op jit(solution)/shard_map/reduce_scatter | solution.py:222
  957.5 47.4 %reduce-scatter.10.cloned.1.call-done = bf16[2,4,64,512]{3,2,0,1:T(8,128)(2,1)} async-done(((bf16[2,4,512,512]{3,2,0,1:T(8,128)(2,1)}), bf16[2,4,64,512]{3,2,0,1:T(8,128)(2,1)}) %reduce-scatter.10.cloned.1.call-update) | async-done | bytes 524304 | tf_op jit(solution)/shard_map/reduce_scatter | solution.py:219
  1028.6 25.3 %pad_maximum_fusion = bf16[6144,2304]{1,0:T(8,128)(2,1)} fusion(bf16[2048,2304]{1,0:T(8,128)(2,1)} %convolution_convert_fusion.3, bf16[4096,2304]{1,0:T(8,128)(2,1)} %convolution_convert_fusion), kind=kLoop, calls=%fused_computation.76 | loop fusion | flops 56623104 | bytes 56623104 | tf_op jit(solution)/shard_map/concatenate | solution.py:264
  1055.5 14.4 fusion.106
  1070.0 13.7 fusion.103
  1093.2 13.5 pad_maximum_fusion.1
  1106.6 222.9 %reduce-scatter.14.cloned.1.call-done = bf16[768,2304]{1,0:T(8,128)(2,1)} async-done(((bf16[6144,2304]{1,0:T(8,128)(2,1)}), bf16[768,2304]{1,0:T(8,128)(2,1)}) %reduce-scatter.14.cloned.1.call-update) | async-done | bytes 3538960 | tf_op jit(solution)/shard_map/reduce_scatter | solution.py:266
  1332.2 29.2 %reduce-scatter.16.cloned.1.call-done = bf16[288,4]{1,0:T(8,128)(2,1)} async-done(((bf16[2304,4]{1,0:T(8,128)(2,1)}), bf16[288,4]{1,0:T(8,128)(2,1)}) %reduce-scatter.16.cloned.1.call-update) | async-done | bytes 2320
  1373.0 342.5 %all-reduce.6.cloned.1.call-done = (bf16[1152,3,2304]{0,2,1:T(8,128)(2,1)}, bf16[768,2304]{1,0:T(8,128)(2,1)}) async-done(((bf16[1152,3,2304]{0,2,1:T(8,128)(2,1)}, bf16[768,2304]{1,0:T(8,128)(2,1)}), (bf16[1152,3,2304]{0,2,1:T(8,128)(2,1)}, bf16[768,2304]{1,0:T(8,128)(2,1)})) %all-reduce.6.cloned.1.call-update) | async-done | bytes 19464208 | tf_op jit(solution)/shard_map/psum | solution.py:276
  1720.9 24.8 %copy.176 = f32[1152,3,2304]{2,0,1:T(8,128)} copy(bf16[1152,3,2304]{0,2,1:T(8,128)(2,1)} %get-tuple-element.433) | data formatting | bytes 47775744
  (257 shorter events, 371.5 us)
Async XLA Ops:
  7.2 18.1 %copy-start.5 = (bf16[2,64,2304]{2,1,0:T(8,128)(2,1)S(1)}, bf16[2,64,2304]{2,1,0:T(8,128)(2,1)}, u32[]{:S(2)}) copy-start(bf16[2,64,2304]{2,1,0:T(8,128)(2,1)} %param.9) | copy-start | bytes 1769476
  7.2 250.9 %all-gather.9.cloned.1.call-start = ((), (), s32[]{:S(2)}) async-start(), calls=%async_computation.13 | async-start | bytes 31850496 | tf_op jit(solution)/shard_map/all_gather | solution.py:55
  7.9 324.8 %all-gather.15.cloned.1.call-start = ((), (), s32[]{:S(2)}) async-start(), calls=%async_computation.21 | async-start | bytes 4718592 | tf_op jit(solution)/shard_map/all_gather | solution.py:85
  9.3 16.1 copy-start.24
  25.8 244.7 %copy-start.12 = (bf16[128,2304]{1,0:T(8,128)(2,1)}, bf16[128,2304]{1,0:T(8,128)(2,1)S(1)}, u32[]{:S(2)}) copy-start(bf16[128,2304]{1,0:T(8,128)(2,1)S(1)} %fusion.175) | copy-start | bytes 1769476
  288.7 91.5 %all-gather.17.cloned.1.call-start = ((), (), s32[]{:S(2)}) async-start(), calls=%async_computation.22 | async-start | bytes 4718592 | tf_op jit(solution)/shard_map/all_gather | solution.py:84
  306.0 10.0 all-to-all-start.1
  309.5 189.0 %all-gather.11.cloned.1.call-start = ((), (), s32[]{:S(2)}) async-start(), calls=%async_computation.14 | async-start | bytes 5308416 | tf_op jit(solution)/shard_map/all_gather | solution.py:127
  449.4 185.9 %all-reduce.4.cloned.1.call-start = ((), (), s32[]{:S(2)}) async-start(), calls=%async_computation.15 | async-start | bytes 9437184 | tf_op jit(solution)/shard_map/psum | solution.py:138
  529.9 158.6 %all-gather.13.cloned.1.call-start = ((), (), s32[]{:S(2)}) async-start(), calls=%async_computation.16 | async-start | bytes 5308416 | tf_op jit(solution)/shard_map/all_gather | solution.py:130
  530.5 256.1 %reduce-scatter.8.cloned.1.call-start = ((), (), s32[]{:S(2)}) async-start(), calls=%async_computation.17 | async-start | bytes 5308416 | tf_op jit(solution)/shard_map/reduce_scatter | solution.py:156
  635.3 63.0 %slice-start = ((s8[4718592]{0:T(1024)(128)(4,1)}), s8[524288]{0:T(1024)(128)(4,1)S(1)}, s32[]{:S(2)}) async-start(s8[4718592]{0:T(1024)(128)(4,1)} %bitcast.316), calls=%async_computation.25 | async-start | bytes 1048576
  716.2 16.4 copy-start.27
  716.2 16.4 copy-start.29
  736.0 52.7 %copy-start.11 = (bf16[2,64,2304]{2,1,0:T(8,128)(2,1)S(1)}, bf16[2,64,2304]{2,1,0:T(8,128)(2,1)}, u32[]{:S(2)}) copy-start(bf16[2,64,2304]{2,1,0:T(8,128)(2,1)} %param.13) | copy-start | bytes 1769476
  802.9 10.7 all-to-all-start.4
  807.0 146.8 %reduce-scatter.12.cloned.1.call-start = ((), (), s32[]{:S(2)}) async-start(), calls=%async_computation.19 | async-start | bytes 4718592 | tf_op jit(solution)/shard_map/reduce_scatter | solution.py:222
  904.7 100.2 %reduce-scatter.10.cloned.1.call-start = ((), (), s32[]{:S(2)}) async-start(), calls=%async_computation.18 | async-start | bytes 4718592 | tf_op jit(solution)/shard_map/reduce_scatter | solution.py:219
  920.1 89.0 %copy-start.10 = (bf16[16,8,4,512]{3,1,2,0:T(8,128)(2,1)S(1)}, bf16[16,8,4,512]{3,1,2,0:T(8,128)(2,1)}, u32[]{:S(2)}) copy-start(bf16[16,8,4,512]{3,1,2,0:T(8,128)(2,1)} %copy-done.9) | copy-start | bytes 1572868
  953.8 51.1 %all-to-all-start.7 = ((bf16[2,4,64,512]{3,2,0,1:T(8,128)(2,1)}), bf16[2,4,64,512]{3,2,0,1:T(8,128)(2,1)S(1)}, u32[]{:S(2)}, u32[]{:S(2)}) async-start(bf16[2,4,64,512]{3,2,0,1:T(8,128)(2,1)} %reduce-scatter.12.cloned.1.call-done), calls=%async_computation.10 | async-start | bytes 1048576 | tf_op jit(solution)/shard_map/all_to_all | solution.py:237
  1004.9 11.6 all-to-all-start.6
  1009.1 320.5 %reduce-scatter.14.cloned.1.call-start = ((), (), s32[]{:S(2)}) async-start(), calls=%async_computation.20 | async-start | bytes 31850496 | tf_op jit(solution)/shard_map/reduce_scatter | solution.py:266
  1054.0 307.4 %reduce-scatter.16.cloned.1.call-start = ((), (), s32[]{:S(2)}) async-start(), calls=%async_computation.23 | async-start | bytes 663552
  1093.1 622.4 %all-reduce.6.cloned.1.call-start = ((), (), s32[]{:S(2)}) async-start(), calls=%async_computation.24 | async-start | bytes 38928384 | tf_op jit(solution)/shard_map/psum | solution.py:276
  (34 other events, 252.2 us)
Sparse Core Ops, SparseCore 0:
  9.7 248.3 all-gather.8
  288.8 43.8 all-gather.14
  334.3 45.8 all-gather.16
  449.5 48.9 all-gather.10
  530.0 105.2 all-reduce.3
  636.7 51.7 all-gather.12
  732.8 53.7 reduce-scatter.7
  904.9 48.9 reduce-scatter.11
  956.7 48.1 reduce-scatter.9
  1054.1 275.4 reduce-scatter.13
  1331.8 29.5 reduce-scatter.15
  1365.1 350.3 all-reduce.5
where the time goes:
time: 1760 us; the launch traced here: 1750 us
  waiting for transfers between devices  1210 us (69%)
  matrix products  208 us (12%)
  local copies, waits for them, and re-layouts  148 us (8%)
  other arithmetic  83.2 us (5%)
  blocking collectives  70.4 us (4%)
    psum x1, waiting for transfers between devices, local(): lax.psum(ffn_grad.astype(jnp.bfloat16), 'seq').astype(jnp.float32)  343 us
    all_gather x1, waiting for transfers between devices, local(): lax.all_gather(attn_weight, 'fsdp', axis=0, tiled=True)  232 us
    reduce_scatter x1, waiting for transfers between devices, local(): lax.psum_scatter(attn_grad_full.astype(jnp.bfloat16), 'fsdp', scatter_dim...  223 us
    psum x1, waiting for transfers between devices, local(): lax.psum(branch.astype(jnp.bfloat16), 'fsdp').astype(jnp.float32)  105 us
    all_gather x1, waiting for transfers between devices, local(): lax.all_gather(out_grad, 'fsdp', axis=1, tiled=True)  49.8 us
    reduce_scatter x1, waiting for transfers between devices, local(): lax.psum_scatter(grad_in.reshape(seq_count, block_rows, model_width).asty...  49.4 us
    all_gather x1, waiting for transfers between devices, local(): lax.all_gather(normed_ffn.reshape(seq_count, row_count, model_width), 'fs...  48.9 us
    unnamed x73, local copies, waits for them, and re-layouts  48.6 us
  transfers between devices with their start and end apart: 16, of which 14 were waited for; matrix products, arithmetic and copies ran while one was open for 6% of the time, Pallas kernels for 0%

commit v1 on v0

v1 whole, which is shorter than its diff:
```python
import functools

import jax
import jax.numpy as jnp
import numpy as np
from jax import lax
from jax.experimental import pallas as pl
from jax.experimental.pallas import tpu as pltpu
from jax.sharding import PartitionSpec as P

HQ = 8
KVH = 4
HD = 256
GROUP = HQ // KVH
HALF = HD // 2

soft_cap = 50.0
norm_eps = 1e-06
bf16 = jnp.bfloat16
f32 = jnp.float32


def rms_scale(values, gain_row):
    return (
        values * lax.rsqrt(jnp.mean(values * values, axis=-1, keepdims=True) + norm_eps) * gain_row
    )


def norm_back(values, gain_row, cotangent):
    inverse = lax.rsqrt(jnp.mean(values * values, axis=-1, keepdims=True) + norm_eps)
    unit_rows = values * inverse
    scaled = cotangent * gain_row
    grad_values = inverse * (
        scaled - unit_rows * jnp.mean(scaled * unit_rows, axis=-1, keepdims=True)
    )
    return (grad_values, cotangent * unit_rows)


def gated_units(gate_proj, up_proj):
    return jax.nn.gelu(gate_proj, approximate=True) * up_proj


def dot_nt(a, b):
    return lax.dot_general(a, b, (((1,), (1,)), ((), ())), preferred_element_type=f32)


def dot_nn(a, b):
    return lax.dot_general(a, b, (((1,), (0,)), ((), ())), preferred_element_type=f32)


def dot_tn(a, b):
    return lax.dot_general(a, b, (((0,), (0,)), ((), ())), preferred_element_type=f32)


def stacked_heads(block):
    heads = block.shape[1] // HD
    return jnp.concatenate([block[:, h * HD : (h + 1) * HD] for h in range(heads)], axis=0)


def visible_of(block, own, shard, rows, keys, lines):
    shape = (lines, keys)
    row = lax.broadcasted_iota(jnp.int32, shape, 0) & (rows - 1)
    col = lax.broadcasted_iota(jnp.int32, shape, 1)
    return block * keys + col <= own * keys + shard * rows + row


def attend_kernel(shard_ref, q_ref, kv_ref, o_ref, lse_ref, score_ref):
    own = pl.program_id(1)
    shard = shard_ref[0]
    parts, _, _, rows, _ = kv_ref.shape
    keys = parts * rows
    queries = stacked_heads(q_ref[0, 0])
    lines = queries.shape[0]

    def score_step(block, top):
        key_block = kv_ref[:, block, 0, :, :HD].reshape(keys, HD)
        raw = dot_nt(queries, key_block) * HD ** (-0.5)
        capped = soft_cap * jnp.tanh(raw / soft_cap)
        capped = jnp.where(visible_of(block, own, shard, rows, keys, lines), capped, -1e30)
        score_ref[block] = capped
        return jnp.maximum(top, jnp.max(capped, axis=-1, keepdims=True))

    top = lax.fori_loop(0, own + 1, score_step, jnp.full((lines, 1), -3e38, f32))

    def sum_step(block, total):
        expanded = jnp.exp(score_ref[block] - top)
        score_ref[block] = expanded
        return total + jnp.sum(expanded, axis=-1, keepdims=True)

    total = lax.fori_loop(0, own + 1, sum_step, jnp.zeros((lines, 1), f32))
    inverse = 1.0 / total

    def mix_step(block, mixed):
        weights = (score_ref[block] * inverse).astype(bf16)
        value_block = kv_ref[:, block, 0, :, HD:].reshape(keys, HD)
        return mixed + dot_nn(weights, value_block)

    mixed = lax.fori_loop(0, own + 1, mix_step, jnp.zeros((lines, HD), f32))
    for h in range(lines // rows):
        o_ref[0, 0, :, h * HD : (h + 1) * HD] = mixed[h * rows : (h + 1) * rows].astype(bf16)
    lse_ref[0, 0] = jnp.broadcast_to(top + jnp.log(total), (lines, 128))


def attend_back_kernel(
    shard_ref, q_ref, do_ref, lse_ref, kv_ref, dq_ref, dkv_ref, weight_ref, dp_ref, acc_ref
):
    own = pl.program_id(1)
    shard = shard_ref[0]
    parts, blocks, _, rows, _ = kv_ref.shape
    keys = parts * rows
    queries = stacked_heads(q_ref[0, 0])
    grads = stacked_heads(do_ref[0, 0])
    lse = lse_ref[0, 0][:, :1]
    lines = queries.shape[0]

    @pl.when(own == 0)
    def _():
        acc_ref[...] = jnp.zeros_like(acc_ref)

    def first_step(block, delta):
        key_block = kv_ref[:, block, 0, :, :HD].reshape(keys, HD)
        value_block = kv_ref[:, block, 0, :, HD:].reshape(keys, HD)
        bounded = jnp.tanh(dot_nt(queries, key_block) * (HD ** (-0.5) / soft_cap))
        capped = jnp.where(
            visible_of(block, own, shard, rows, keys, lines), soft_cap * bounded, -1e30
        )
        weights = jnp.exp(capped - lse)
        grad_weights = dot_nt(grads, value_block)
        acc_ref[block, :, HD:] += dot_tn(weights.astype(bf16), grads)
        weight_ref[block] = weights * (1.0 - bounded * bounded)
        dp_ref[block] = grad_weights
        return delta + jnp.sum(weights * grad_weights, axis=-1, keepdims=True)

    delta = lax.fori_loop(0, own + 1, first_step, jnp.zeros((lines, 1), f32))

    def second_step(block, grad_query):
        key_block = kv_ref[:, block, 0, :, :HD].reshape(keys, HD)
        grad_raw = (weight_ref[block] * (dp_ref[block] - delta)).astype(bf16)
        acc_ref[block, :, :HD] += dot_tn(grad_raw, queries)
        return grad_query + dot_nn(grad_raw, key_block)

    grad_query = lax.fori_loop(
        0, own + 1, second_step, jnp.zeros((lines, HD), f32)
    ) * HD ** (-0.5)
    for h in range(lines // rows):
        dq_ref[0, 0, :, h * HD : (h + 1) * HD] = grad_query[h * rows : (h + 1) * rows].astype(bf16)

    @pl.when(own == blocks - 1)
    def _():
        for block in range(blocks):
            dkv_ref[:, block, 0, :, :HD] = (
                (acc_ref[block, :, :HD] * HD ** (-0.5)).astype(bf16).reshape(parts, rows, HD)
            )
            dkv_ref[:, block, 0, :, HD:] = (
                acc_ref[block, :, HD:].astype(bf16).reshape(parts, rows, HD)
            )


def attend(shard, queries, kv_all):
    blocks, seqs, rows, width = queries.shape
    lines = rows * width // HD
    parts = kv_all.shape[0]
    keys = parts * rows
    row_spec = pl.BlockSpec((1, 1, rows, width), lambda n, s, shard: (s, n, 0, 0))
    lse_spec = pl.BlockSpec((1, 1, lines, 128), lambda n, s, shard: (s, n, 0, 0))
    kv_spec = pl.BlockSpec((parts, blocks, 1, rows, 2 * HD), lambda n, s, shard: (0, 0, n, 0, 0))
    return pl.pallas_call(
        attend_kernel,
        grid_spec=pltpu.PrefetchScalarGridSpec(
            num_scalar_prefetch=1,
            grid=(seqs, blocks),
            in_specs=[row_spec, kv_spec],
            out_specs=[row_spec, lse_spec],
            scratch_shapes=[pltpu.VMEM((blocks, lines, keys), f32)],
        ),
        out_shape=[
            jax.ShapeDtypeStruct(queries.shape, bf16),
            jax.ShapeDtypeStruct((blocks, seqs, lines, 128), f32),
        ],
        compiler_params=pltpu.CompilerParams(vmem_limit_bytes=48 * 2**20),
        name="attend",
    )(shard, queries, kv_all)


def attend_back(shard, queries, grads, lse, kv_all):
    blocks, seqs, rows, width = queries.shape
    lines = rows * width // HD
    parts = kv_all.shape[0]
    keys = parts * rows
    row_spec = pl.BlockSpec((1, 1, rows, width), lambda n, s, shard: (s, n, 0, 0))
    lse_spec = pl.BlockSpec((1, 1, lines, 128), lambda n, s, shard: (s, n, 0, 0))
    deep = 2 if keys * blocks <= 4096 else 1
    kv_spec = pl.BlockSpec(
        (parts, blocks, 1, rows, 2 * HD),
        lambda n, s, shard: (0, 0, n, 0, 0),
        pipeline_mode=pl.Buffered(deep),
    )
    return pl.pallas_call(
        attend_back_kernel,
        grid_spec=pltpu.PrefetchScalarGridSpec(
            num_scalar_prefetch=1,
            grid=(seqs, blocks),
            in_specs=[row_spec, row_spec, lse_spec, kv_spec],
            out_specs=[row_spec, kv_spec],
            scratch_shapes=[
                pltpu.VMEM((blocks, lines, keys), f32),
                pltpu.VMEM((blocks, lines, keys), f32),
                pltpu.VMEM((blocks, keys, 2 * HD), f32),
            ],
        ),
        out_shape=[
            jax.ShapeDtypeStruct(queries.shape, bf16),
            jax.ShapeDtypeStruct(kv_all.shape, bf16),
        ],
        compiler_params=pltpu.CompilerParams(vmem_limit_bytes=56 * 2**20),
        name="attend_back",
    )(shard, queries, grads, lse, kv_all)


def widen_kernel(*refs):
    refs[-1][0] = refs[0][...].astype(f32)


def widen_plane(plane, index, planes, whole):
    rows, width = plane.shape
    step = rows // 4 if rows % 64 == 0 else rows
    specs = [pl.BlockSpec((step, width), lambda i: (i, 0))]
    args = [plane]
    aliases = {}
    if whole is not None:
        specs.append(pl.BlockSpec(memory_space=pl.ANY))
        args.append(whole)
        aliases = {1: 0}
    return pl.pallas_call(
        widen_kernel,
        grid=(rows // step,),
        in_specs=specs,
        out_specs=pl.BlockSpec((1, step, width), lambda i: (index, i, 0)),
        out_shape=jax.ShapeDtypeStruct((planes, rows, width), f32),
        input_output_aliases=aliases,
        compiler_params=pltpu.CompilerParams(vmem_limit_bytes=40 * 2**20),
        name="widen",
    )(*args)


def granules_of(column, columns):
    per = HQ // columns
    first = column * per
    return (
        [first + i for i in range(per)]
        + [HQ + first // GROUP, HQ + KVH + first // GROUP]
        + [HQ + 2 * KVH + first + i for i in range(per)]
    )


def route(columns, chips, per_chip):
    items = len(granules_of(0, columns))
    urgent = items - HQ // columns
    source = [[g // per_chip for g in granules_of(c, columns)] for c in range(columns)]
    held = [[{k for k in range(items) if source[c][k] == z} for z in range(chips)] for c in range(columns)]
    steps = []
    urgent_steps = None
    while any(len(held[c][z]) < items for c in range(columns) for z in range(chips)):
        moves = {}
        for c in range(columns):
            for z in range(chips):
                for core, way in ((0, 1), (1, -1)):
                    if not 0 <= z + way < chips:
                        continue
                    ready = [
                        k
                        for k in held[c][z]
                        if k not in held[c][z + way] and (source[c][k] - z) * way <= 0
                    ]
                    if ready:
                        moves[c, z, core] = min(
                            ready, key=lambda k: (k >= urgent, abs(source[c][k] - z), k)
                        )
        for (c, z, core), k in moves.items():
            held[c][z + (1, -1)[core]].add(k)
        steps.append(moves)
        done = all(k in held[c][z] for c in range(columns) for z in range(chips) for k in range(urgent))
        if done and urgent_steps is None:
            urgent_steps = len(steps)
    return steps, urgent_steps


def pick_kernel(cands, which_ref, slot_ref, *refs):
    out_ref = refs[-1]
    wanted = which_ref[pl.program_id(0)]
    for code in cands:

        @pl.when(wanted == code)
        def _(code=code):
            out_ref[...] = refs[code][...]


def pick(places, sources, device, devices):
    names = []
    which = np.zeros((devices, len(places)), np.int32)
    slot = np.zeros((devices, len(places)), np.int32)
    for k, place in enumerate(places):
        for d in range(devices):
            name, at = place.get(d, ("mine", 0))
            if name not in names:
                names.append(name)
            which[d, k] = names.index(name)
            slot[d, k] = at
    _, rows, width = sources["mine"].shape
    table = jnp.asarray(np.concatenate([which, slot], axis=1))[device]
    block = (1, rows // 4, width)

    def spec(code):
        def index(k, r, which_ref, slot_ref):
            hit = which_ref[k] == code
            return jnp.where(hit, slot_ref[k], 0), jnp.where(hit, r, 0), 0

        return pl.BlockSpec(block, index)

    return pl.pallas_call(
        functools.partial(pick_kernel, range(len(names))),
        grid_spec=pltpu.PrefetchScalarGridSpec(
            num_scalar_prefetch=2,
            grid=(len(places), 4),
            in_specs=[spec(code) for code in range(len(names))],
            out_specs=pl.BlockSpec(block, lambda k, r, which_ref, slot_ref: (k, r, 0)),
        ),
        out_shape=jax.ShapeDtypeStruct((len(places), rows, width), bf16),
        compiler_params=pltpu.CompilerParams(vmem_limit_bytes=40 * 2**20),
        name="pick",
    )(table[: len(places)], table[len(places) :], *[sources[name] for name in names])


def routed_weights(attn_weight, column, shard, columns, shards, between):
    rows, width = attn_weight.shape
    count = rows // HD
    chips = shards // 2
    devices = columns * shards
    device = column * shards + shard
    swap = [(f, f ^ 1) for f in range(shards)]
    items = len(granules_of(0, columns))
    urgent = items - HQ // columns
    steps, urgent_steps = route(columns, chips, 2 * count)
    mine = attn_weight.reshape(count, HD, width)
    sources = {"mine": mine, "theirs": lax.ppermute(mine, "fsdp", swap)}
    at = [{} for _ in range(items)]
    for c in range(columns):
        for f in range(shards):
            for k, g in enumerate(granules_of(c, columns)):
                if g // (2 * count) == f // 2:
                    at[k][c * shards + f] = ("mine" if g // count == f else "theirs", g % count)
    first = None
    for number, moves in enumerate(steps):
        place = {}
        pairs = []
        for (c, z, core), k in moves.items():
            here = c * shards + 2 * z + core
            to = here + (2, -2)[core]
            place[here] = at[k][here]
            pairs.append((here, to))
            at[k][to] = ("got%d" % number, 0)
            at[k][to ^ 1] = ("swapped%d" % number, 0)
        got = lax.ppermute(pick([place], sources, device, devices), ("seq", "fsdp"), pairs)
        got = between(number, got)
        if 0 < number < urgent_steps:
            before = "swapped%d" % (number - 1)
            got, sources[before] = lax.optimization_barrier((got, sources[before]))
        sources["got%d" % number] = got
        sources["swapped%d" % number] = lax.ppermute(got, "fsdp", swap)
        if number + 1 == urgent_steps:
            first = pick(at[:urgent], sources, device, devices)
            first, sources = between(None, (first, sources))
    return first, pick(at[urgent:], sources, device, devices)


def column_weights(attn_weight, column, shard, columns, shards, between):
    rows, width = attn_weight.shape
    per = HQ // columns
    if rows % HD == 0 and shards == 8 and columns == 4:
        return routed_weights(attn_weight, column, shard, columns, shards, between)
    whole = lax.all_gather(attn_weight, "fsdp", axis=0, tiled=True).reshape(-1, HD, width)
    table = np.array([granules_of(c, columns) for c in range(columns)], np.int32)
    place = jnp.asarray(table)[column]
    taken = jnp.concatenate(
        [lax.dynamic_slice_in_dim(whole, place[k], 1, 0) for k in range(table.shape[1])], axis=0
    )
    return taken[: per + 2], taken[per + 2 :]


def ring_of(chips):
    return [0] + list(range(1, chips, 2)) + [z for z in range(chips - 1, 0, -1) if z % 2 == 0]


def ring_tables(shards):
    chips = shards // 2
    order = ring_of(chips)
    spot = {z: p for p, z in enumerate(order)}
    pairs = [
        (2 * z + c, 2 * order[(spot[z] + 1) % chips] + c) for z in range(chips) for c in range(2)
    ]
    behind = np.array(
        [[order[(spot[f // 2] - t) % chips] for t in range(chips + 1)] for f in range(shards)],
        np.int32,
    )
    return chips, pairs, behind


def ring_gather(block, shard, shards):
    chips, pairs, behind = ring_tables(shards)
    swap = [(f, f ^ 1) for f in range(shards)]
    source = jnp.asarray(behind)[shard]
    core = shard % 2
    out = jnp.zeros((shards,) + block.shape, block.dtype)
    held = block
    for t in range(chips):
        if t:
            held = lax.ppermute(held, "fsdp", pairs)
        other = lax.ppermute(held, "fsdp", swap)
        out = lax.dynamic_update_index_in_dim(out, held, 2 * source[t] + core, 0)
        out = lax.dynamic_update_index_in_dim(out, other, 2 * source[t] + 1 - core, 0)
    return out


def ring_scatter(parts, shard, shards):
    chips, pairs, behind = ring_tables(shards)
    swap = [(f, f ^ 1) for f in range(shards)]
    target = jnp.asarray(behind)[shard]
    core = shard % 2
    paired = parts.reshape((chips, 2) + parts.shape[1:])
    mine = lax.dynamic_index_in_dim(paired, core, 1, keepdims=False)
    other = lax.ppermute(
        lax.dynamic_index_in_dim(paired, 1 - core, 1, keepdims=False), "fsdp", swap
    )

    def local_sum(t):
        return lax.dynamic_index_in_dim(mine, target[t], 0, keepdims=False).astype(
            f32
        ) + lax.dynamic_index_in_dim(other, target[t], 0, keepdims=False).astype(f32)

    total = local_sum(1)
    for t in range(1, chips):
        total = lax.ppermute(total.astype(bf16), "fsdp", pairs).astype(f32) + local_sum(t + 1)
    return total


def partners(columns, bit):
    return [(c, c ^ bit) for c in range(columns)]


def column_scatter(parts):
    half = parts.shape[-1] // 2
    done = []
    for first, second, cut in ((1, 2, slice(0, half)), (2, 1, slice(half, None))):
        low = parts[..., cut].astype(bf16)
        got = lax.ppermute(
            jnp.concatenate([low[first : first + 1], low[3:]], axis=0), "seq", partners(4, first)
        )
        keep = parts[0, ..., cut] + got[0].astype(f32)
        away = parts[second, ..., cut] + got[1].astype(f32)
        done.append(
            keep + lax.ppermute(away.astype(bf16), "seq", partners(4, second)).astype(f32)
        )
    return jnp.concatenate(done, axis=-1)


def sum_everywhere(value, columns, shards):
    for axis, count in (("fsdp", shards), ("seq", columns)):
        bit = 1
        while bit < count:
            value = value + lax.ppermute(value, axis, [(c, c ^ bit) for c in range(count)])
            bit *= 2
    return value


def local(tokens, attn_weight, norm_gains, ffn_weight, out_grad):
    seqs, rows, width = tokens.shape
    columns = lax.axis_size("seq")
    shards = lax.axis_size("fsdp")
    column = lax.axis_index("seq")
    shard = lax.axis_index("fsdp")
    core = shard % 2
    per = HQ // columns
    own_rows = seqs * rows
    swap = [(f, f ^ 1) for f in range(shards)]
    shard_arg = shard.astype(jnp.int32).reshape(1)

    def whole_weights(granules, near, far):
        cut = granules.shape[0] // 2
        come = {
            (0, 1): near[0],
            (0, 2): far[0][0],
            (0, 3): far[0][1],
            (1, 2): near[1],
            (1, 1): far[1][0],
            (1, 3): far[1][1],
        }
        outs = []
        for begin, end in ((0, per + 2), (per + 2, 2 * per + 2)):
            out = jnp.zeros((columns, end - begin, 2, HALF, width), bf16)
            full = granules[begin:end].reshape(1, end - begin, 2, HALF, width)
            outs.append(lax.dynamic_update_slice(out, full, (column, 0, 0, 0, 0)))
        for (part, hop), lane in come.items():
            other = lax.ppermute(lane, "fsdp", swap)
            for half, piece in ((core, lane), (1 - core, other)):
                for i, (begin, end) in enumerate(((0, per + 2), (per + 2, 2 * per + 2))):
                    low, high = max(begin, part * cut), min(end, (part + 1) * cut)
                    if low < high:
                        chosen = piece[low - part * cut : high - part * cut]
                        outs[i] = lax.dynamic_update_slice(
                            outs[i],
                            chosen.reshape(1, high - low, 1, HALF, width),
                            (column ^ hop, low - begin, half, 0, 0),
                        )
        return outs[0].reshape(-1, width), outs[1].reshape(-1, width)

    token_slices = lax.all_gather(tokens, "seq", axis=0)
    gain_rows = lax.all_gather(norm_gains, "fsdp", axis=1, tiled=True).astype(f32)
    normed_slices = rms_scale(
        token_slices.reshape(-1, width).astype(f32), gain_rows[0]
    ).astype(bf16)
    heads = None

    def between(step, value):
        nonlocal gain_rows, normed_slices, heads
        if step == 0:
            value, gain_rows = lax.optimization_barrier((value, gain_rows))
        if step == 2:
            value, normed_slices = lax.optimization_barrier((value, normed_slices))
        if step is None:
            heads = dot_nt(normed_slices, value[0].reshape(-1, width)).astype(bf16)
            heads, value = lax.optimization_barrier((heads, value))
        return value

    weight_in, weight_out = column_weights(
        attn_weight, column, shard, columns, shards, between
    )
    if heads is None:
        heads = dot_nt(normed_slices, weight_in.reshape(-1, width)).astype(bf16)
    heads = heads.reshape(columns, seqs, rows, (per + 2) * HD)
    queries = heads[..., : per * HD]
    kv_all = lax.all_gather(heads[..., per * HD :], "fsdp", axis=0)

    mixed, lse = attend(shard_arg, queries, kv_all)
    mixed_rows = lax.all_to_all(mixed, "seq", split_axis=0, concat_axis=0, tiled=True)
    mixed_rows = mixed_rows.transpose(1, 2, 0, 3).reshape(own_rows, HQ * HD)
    weight_out_rows = weight_out.reshape(-1, width)
    if columns == 4:
        by_partner = jnp.concatenate(
            [lax.dynamic_slice_in_dim(mixed, column ^ k, 1, 0) for k in range(columns)], axis=0
        ).reshape(columns * own_rows, per * HD)
        attn_out = column_scatter(
            dot_nn(by_partner, weight_out_rows).reshape(columns, own_rows, width)
        )
    else:
        attn_out = lax.psum_scatter(
            dot_nn(mixed.reshape(-1, per * HD), weight_out_rows).astype(bf16),
            "seq",
            scatter_dimension=0,
            tiled=True,
        ).astype(f32)
    flat_tokens = tokens.reshape(-1, width).astype(f32)
    flat_cot = out_grad.reshape(-1, width).astype(f32)
    residual = flat_tokens + rms_scale(attn_out, gain_rows[1])
    normed_ffn = rms_scale(residual, gain_rows[2]).astype(bf16)

    granules = jnp.concatenate([weight_in, weight_out], axis=0)
    if columns == 4:
        lanes = lax.dynamic_index_in_dim(
            granules.reshape(-1, 2, HALF, width), core, 1, keepdims=False
        )
        lanes, normed_ffn = lax.optimization_barrier((lanes, normed_ffn))
        cut = lanes.shape[0] // 2
        lanes = (lanes[:cut], lanes[cut:])
        near = tuple(
            lax.ppermute(lane, "seq", partners(4, bit)) for lane, bit in zip(lanes, (1, 2))
        )
    ffn_in = lax.all_gather(normed_ffn, "fsdp", axis=0, tiled=True)
    gate_up = jnp.einsum("td,fgd->tgf", ffn_in, ffn_weight[:, :2], preferred_element_type=f32)
    hidden = gated_units(gate_up[:, 0], gate_up[:, 1]).astype(bf16)
    if columns == 4:
        hidden, near = lax.optimization_barrier((hidden, near))
        far = tuple(
            lax.ppermute(jnp.stack([lane, got]), "seq", partners(4, bit))
            for lane, got, bit in zip(lanes, near, (2, 1))
        )
    branch = dot_nn(hidden, ffn_weight[:, 2])
    ffn_out = lax.psum_scatter(
        branch.astype(bf16), "fsdp", scatter_dimension=0, tiled=True
    ).astype(f32)
    if columns == 4:
        ffn_out, far = lax.optimization_barrier((ffn_out, far))
        weight_in_all, weight_out_all = whole_weights(granules, near, far)
    else:
        whole = lax.all_gather(granules, "seq", axis=0)
        weight_in_all = whole[:, : per + 2].reshape(-1, width)
        weight_out_all = whole[:, per + 2 :].reshape(-1, width)
    result = residual + rms_scale(ffn_out, gain_rows[3])
    block_out = result.astype(bf16).reshape(tokens.shape)
    grad_ffn, gain_terms = norm_back(ffn_out, gain_rows[3], flat_cot)
    gain_last = jnp.sum(gain_terms, axis=0)
    grad_ffn_all = lax.all_gather(grad_ffn.astype(bf16), "fsdp", axis=0, tiled=True)
    grad_ffn_all, weight_in_all, weight_out_all = lax.optimization_barrier(
        (grad_ffn_all, weight_in_all, weight_out_all)
    )
    down_part = dot_tn(hidden, grad_ffn_all).astype(bf16)
    grad_ffn_all, down_part = lax.optimization_barrier((grad_ffn_all, down_part))
    normed_own = rms_scale(flat_tokens, gain_rows[0]).astype(bf16)
    normed_own, grad_ffn_all = lax.optimization_barrier((normed_own, grad_ffn_all))
    normed_all = ring_gather(normed_own, shard, shards).reshape(-1, width)
    grad_hidden = dot_nt(grad_ffn_all, ffn_weight[:, 2])
    unused, gated_pull = jax.vjp(gated_units, gate_up[:, 0], gate_up[:, 1])
    grad_gate, grad_up = gated_pull(grad_hidden)
    grad_gate_up = jnp.stack([grad_gate, grad_up], axis=1).astype(bf16)
    gate_part = dot_tn(grad_gate_up[:, 0], ffn_in).astype(bf16)
    up_part = dot_tn(grad_gate_up[:, 1], ffn_in).astype(bf16)
    grad_gate_up, gate_part, up_part, normed_all = lax.optimization_barrier(
        (grad_gate_up, gate_part, up_part, normed_all)
    )
    gate_grad, up_grad, down_grad = lax.psum((gate_part, up_part, down_part), "seq")
    grad_in = jnp.einsum(
        "tgf,fgd->td", grad_gate_up, ffn_weight[:, :2], preferred_element_type=f32
    )
    grad_normed_ffn = ring_scatter(
        grad_in.astype(bf16).reshape(shards, own_rows, width), shard, shards
    )

    grad_mid, gain_pre_ffn = norm_back(residual, gain_rows[2], grad_normed_ffn)
    grad_residual = flat_cot + grad_mid
    grad_attn, gain_post_attn = norm_back(attn_out, gain_rows[1], grad_residual)
    grad_attn_low = grad_attn.astype(bf16)
    grad_mixed = (
        dot_nt(grad_attn_low, weight_out_all).astype(bf16).reshape(seqs, rows, columns, per * HD)
    )
    grad_heads = lax.all_to_all(
        grad_mixed.transpose(2, 0, 1, 3), "seq", split_axis=0, concat_axis=0, tiled=True
    )
    grad_attn_all = ring_gather(grad_attn_low, shard, shards).reshape(-1, width)
    grad_queries, grad_kv = attend_back(shard_arg, queries, grad_heads, lse, kv_all)
    grad_kv, grad_attn_all = lax.optimization_barrier((grad_kv, grad_attn_all))
    grad_kv_own = ring_scatter(
        grad_kv.reshape(shards, columns * own_rows, 2 * HD), shard, shards
    ).astype(bf16).reshape(columns, seqs, rows, 2 * HD)
    grad_proj = lax.all_to_all(
        jnp.concatenate([grad_queries, grad_kv_own], axis=-1),
        "seq",
        split_axis=0,
        concat_axis=0,
        tiled=True,
    )
    grad_rows = grad_proj.reshape(columns, own_rows, (per + 2) * HD).transpose(1, 0, 2)
    grad_normed = dot_nn(grad_rows.reshape(own_rows, -1), weight_in_all)
    grad_tokens, gain_pre_attn = norm_back(flat_tokens, gain_rows[0], grad_normed)
    token_grad = (grad_residual + grad_tokens).reshape(tokens.shape)


    def shared(copies):
        if columns == KVH:
            return copies.reshape(own_rows, -1)
        summed = copies.reshape(own_rows, KVH, columns // KVH, HD).astype(f32).sum(axis=2)
        return summed.astype(bf16).reshape(own_rows, -1)

    weight_cols = jnp.concatenate(
        [
            grad_rows[:, :, : per * HD].reshape(own_rows, -1),
            shared(grad_rows[:, :, per * HD : (per + 1) * HD]),
            shared(grad_rows[:, :, (per + 1) * HD :]),
            mixed_rows,
        ],
        axis=1,
    )
    shard_cols = attn_weight.shape[0]
    col_all = lax.all_to_all(
        weight_cols.reshape(own_rows, shards, shard_cols).transpose(1, 0, 2),
        "fsdp",
        split_axis=0,
        concat_axis=0,
        tiled=True,
    ).reshape(-1, shard_cols)
    is_out = (shard * shard_cols + jnp.arange(shard_cols)) >= (HQ + 2 * KVH) * HD
    attn_grad = dot_tn(jnp.where(is_out, 0, col_all), normed_all) + dot_tn(
        jnp.where(is_out, col_all, 0), grad_attn_all
    )
    attn_grad_low, gate_grad, up_grad, down_grad = lax.optimization_barrier(
        (attn_grad.astype(bf16), gate_grad, up_grad, down_grad)
    )
    attn_total = lax.psum(attn_grad_low, "seq").astype(f32)
    ffn_grad = widen_plane(down_grad, 2, 3, None)
    ffn_grad = widen_plane(gate_grad, 0, 3, ffn_grad)
    ffn_grad = widen_plane(up_grad, 1, 3, ffn_grad)
    ffn_grad = ffn_grad.transpose(1, 0, 2)
    gain_grad = jnp.stack(
        [
            jnp.sum(gain_pre_attn, axis=0),
            jnp.sum(gain_post_attn, axis=0),
            jnp.sum(gain_pre_ffn, axis=0),
            gain_last,
        ]
    )
    gain_total = lax.dynamic_slice_in_dim(
        sum_everywhere(gain_grad, columns, shards),
        shard * norm_gains.shape[1],
        norm_gains.shape[1],
        1,
    )
    return (block_out, token_grad, attn_total, gain_total, ffn_grad)


def solution(mesh):
    in_specs = (
        P(None, ("seq", "fsdp"), None),
        P("fsdp", None),
        P(None, "fsdp"),
        P("fsdp", None, None),
        P(None, ("seq", "fsdp"), None),
    )
    out_specs = (
        P(None, ("seq", "fsdp"), None),
        P(None, ("seq", "fsdp"), None),
        P("fsdp", None),
        P(None, "fsdp"),
        P("fsdp", None, None),
    )
    return jax.shard_map(local, mesh=mesh, in_specs=in_specs, out_specs=out_specs, check_vma=False)
```

time: 1760 us -> 1130 us (0.64)
  waiting for transfers between devices: 1210 us -> 548 us
  starting transfers between devices: 16.5 us -> 127 us
  matrix products: 208 us -> 118 us
  Pallas kernels: 0 us -> 83.3 us
  blocking collectives: 70.4 us -> 22.1 us
  other arithmetic: 83.2 us -> 60.8 us
  local copies, waits for them, and re-layouts: 148 us -> 130 us
    reduce_scatter x4 -> x1, waiting for transfers between devices: 342 us -> 13.6 us  [local(): lax.psum_scatter(branch.astype(bf16), 'fsdp', scatter_dimension=0, tiled=...]
    all_gather x5 -> x4, waiting for transfers between devices: 380 us -> 86.6 us  [the longest x1 48.2 us: local(): ffn_in = lax.all_gather(normed_ffn, 'fsdp', axis=0, tiled=True)]
    psum x2, waiting for transfers between devices: 447 us -> 158 us  [the longest x1 106 us: local(): lax.psum((gate_part, up_part, down_part), 'seq')]
    ppermute x0 -> x54, waiting for transfers between devices: none -> 221 us  [the longest x6 77.6 us: ring_scatter(): lax.ppermute(total.astype(bf16), 'fsdp', pairs).astype(f32)]
    ppermute x0 -> x54, starting transfers between devices: none -> 109 us  [the longest x2 37.1 us: column_scatter(): lax.ppermute(jnp.concatenate([low[first:first + 1], low[3:]], axis=0), 's...]
    dot_general x24 -> x11, matrix products: 175 us -> 86.9 us  [the longest x5 38 us: dot_tn(): lax.dot_general(a, b, (((0,), (0,)), ((), ())), preferred_element_type=f32)]
    pallas_call x0 -> x13, Pallas kernels: none -> 83.3 us  [the longest x8 32.7 us: pick(): pl.pallas_call(functools.partial(pick_kernel, range(len(names))), grid_sp...]
    all_to_all x4, waiting for transfers between devices: 12.4 us -> 67.7 us  [the longest x1 37.8 us: local(): lax.all_to_all(weight_cols.reshape(own_rows, shards, shard_cols).transpos...]
  transfers between devices with their start and end apart: 16 -> 65, of which waited for: 14 -> 40; matrix products, arithmetic and copies ran while one was open for 6% -> 18% of each run, Pallas kernels for 0% -> 5%
where the time goes in v1:
time: 1130 us; the launch traced here: 1110 us
  waiting for transfers between devices  548 us (48%)
  local copies, waits for them, and re-layouts  130 us (12%)
  starting transfers between devices  127 us (11%)
  matrix products  118 us (10%)
  Pallas kernels  83.3 us (7%)
  other arithmetic  60.8 us (5%)
  between operations  25 us (2%)
  blocking collectives  22.1 us (2%)
    psum x1, waiting for transfers between devices, local(): lax.psum((gate_part, up_part, down_part), 'seq')  106 us
    ppermute x6, waiting for transfers between devices, ring_scatter(): lax.ppermute(total.astype(bf16), 'fsdp', pairs).astype(f32)  77.6 us
    ppermute x6, waiting for transfers between devices, ring_gather(): held = lax.ppermute(held, 'fsdp', pairs)  53.5 us
    psum x1, waiting for transfers between devices, local(): attn_total = lax.psum(attn_grad_low, 'seq').astype(f32)  52.2 us
    all_gather x1, waiting for transfers between devices, local(): ffn_in = lax.all_gather(normed_ffn, 'fsdp', axis=0, tiled=True)  48.2 us
    dot_general x5, matrix products, dot_tn(): lax.dot_general(a, b, (((0,), (0,)), ((), ())), preferred_element_type=f32)  38 us
    all_to_all x1, waiting for transfers between devices, local(): lax.all_to_all(weight_cols.reshape(own_rows, shards, shard_cols).transpos...  37.8 us
    ppermute x2, waiting for transfers between devices, local(): lax.ppermute(jnp.stack([lane, got]), 'seq', partners(4, bit))  37.7 us
  transfers between devices with their start and end apart: 65, of which 40 were waited for; matrix products, arithmetic and copies ran while one was open for 18% of the time, Pallas kernels for 5%

profile of v1, /device:TPU:0, one launch (start us, length us, event | category | flops | bytes accessed | tf_op | source)
XLA Modules:
  0.0 1113.8 jit_solution(8605409932991436963)
XLA Ops:
  29.1 22.1 %all-gather.2 = bf16[8,288,4]{1,2,0:T(4,128)(2,1)S(1)} all-gather(bf16[1,288,4]{1,2,0:T(4,128)(2,1)S(1)} %bitcast.431), channel_id=1, replica_groups=mesh['seq'=4,'fsdp'=8] {'fsdp'}, dimensions={0}, use_global_device_ids=true | all-gather | bytes 20736 | tf_op jit(solution)/shard_map/all_gather | solution.py:517
  91.5 13.2 %collective-permute-start.7 = (bf16[1,256,2304]{2,1,0:T(8,128)(2,1)}, bf16[1,256,2304]{2,1,0:T(8,128)(2,1)S(1)}, u32[]{:S(2)}, u32[]{:S(2)}) collective-permute-start(bf16[1,256,2304]{2,1,0:T(8,128)(2,1)} %collective-permute-done.4.refs_1_.refs_6_.refs_2_), channel_id=1, source_target_pairs={{0,1},{1,0},{2,3},{3,2},{4,5},{5,4},{6,7},{7,6},{8,9},{9,8},{10,11... | collective-permute-start | bytes 3538952 | tf_op jit(solution)/shard_map/ppermute | solution.py:369
  107.4 13.2 %collective-permute-start.8 = (bf16[1,256,2304]{2,1,0:T(8,128)(2,1)S(1)}, bf16[1,256,2304]{2,1,0:T(8,128)(2,1)S(1)}, u32[]{:S(2)}, u32[]{:S(2)}) collective-permute-start(bf16[1,256,2304]{2,1,0:T(8,128)(2,1)S(1)} %collective-permute-done.6.refs_8_.refs_11_), channel_id=1, source_target_pairs={{0,1},{1,0},{2,3},{3,2},{4,5},{5,4},{6,7},{7,6},{8,9},{9,8},{10,11... | collective-permute-start | bytes 3538952 | tf_op jit(solution)/shard_map/ppermute | solution.py:369
  167.6 19.7 %all-gather.14.cloned.1.call-done = bf16[32,2,64,512]{3,2,1,0:T(8,128)(2,1)} async-done(((bf16[4,2,64,512]{3,2,1,0:T(8,128)(2,1)}), bf16[32,2,64,512]{3,2,1,0:T(8,128)(2,1)}) %all-gather.14.cloned.1.call-update) | async-done | bytes 4194320 | tf_op jit(solution)/shard_map/all_gather | solution.py:541
  189.4 14.5 %attend.1 = (bf16[4,2,64,512]{3,2,1,0:T(8,128)(2,1)}, f32[4,2,128,128]{3,2,1,0:T(8,128)S(1)}) custom-call(s32[1]{0:T(128)} %bitcast.1.shard_ref, bf16[4,2,64,512]{3,2,1,0:T(8,128)(2,1)S(1)} %copy-done.8, bf16[8,4,2,64,512]{4,3,2,1,0:T(8,128)(2,1)S(1)} %bitcast.381), custom_call_target="tpu_custom_call" | custom-call | tf_op jit(solution)/shard_map/attend/pallas_call | solution.py:167
  213.5 34.3 %collective-permute-start.15 = (bf16[2,128,1152]{2,1,0:T(8,128)(2,1)}, bf16[2,128,1152]{2,1,0:T(8,128)(2,1)}, u32[]{:S(2)}, u32[]{:S(2)}) collective-permute-start(bf16[2,128,1152]{2,1,0:T(8,128)(2,1)} %concatenate.38), channel_id=1, source_target_pairs={{0,16},{8,24},{16,0},{24,8},{1,17},{9,25},{17,1},{25,9},{2,18},{10... | collective-permute-start | bytes 1769480 | tf_op jit(solution)/shard_map/ppermute | solution.py:455
  284.5 48.2 %all-gather.8.cloned.1.call-done = bf16[1024,2304]{1,0:T(8,128)(2,1)} async-done(((bf16[128,2304]{1,0:T(8,128)(2,1)}), bf16[1024,2304]{1,0:T(8,128)(2,1)}) %all-gather.8.cloned.1.call-update) | async-done | bytes 4718608 | tf_op jit(solution)/shard_map/all_gather | solution.py:577
  332.7 16.6 %fusion.4 = f32[1024,2,1152]{2,0,1:T(8,128)S(1)} fusion(bf16[1152,3,2304]{2,0,1:T(8,128)(2,1)} %param.20, bf16[1024,2304]{1,0:T(8,128)(2,1)} %all-gather.8.cloned.1.call-done), kind=kOutput, calls=%fused_computation.12 | convolution fusion | flops 10871635968 | bytes 24772608 | tf_op jit(solution)/shard_map/td,fgd->tgf/dot_general | solution.py:578
  405.1 13.6 %reduce-scatter.2.cloned.1.call-done = bf16[128,2304]{1,0:T(8,128)(2,1)} async-done(((bf16[1024,2304]{1,0:T(8,128)(2,1)}), bf16[128,2304]{1,0:T(8,128)(2,1)}) %reduce-scatter.2.cloned.1.call-update) | async-done | bytes 589840 | tf_op jit(solution)/shard_map/reduce_scatter | solution.py:587
  419.9 32.6 %collective-permute-done.19 = bf16[2,3,128,2304]{3,2,1,0:T(8,128)(2,1)} collective-permute-done((bf16[2,3,128,2304]{3,2,1,0:T(8,128)(2,1)}, bf16[2,3,128,2304]{3,2,1,0:T(8,128)(2,1)}, u32[]{:S(2)}, u32[]{:S(2)}) %collective-permute-start.19) | collective-permute-done | bytes 3538976 | tf_op jit(solution)/shard_map/ppermute | solution.py:583
  491.6 18.7 %all-gather.10.cloned.1.call-done = bf16[1024,2304]{1,0:T(8,128)(2,1)} async-done(((bf16[128,2304]{1,0:T(8,128)(2,1)}), bf16[1024,2304]{1,0:T(8,128)(2,1)}) %all-gather.10.cloned.1.call-update) | async-done | bytes 4718608 | tf_op jit(solution)/shard_map/all_gather | solution.py:601
  521.4 13.0 %fusion.18 = (bf16[1024,1152]{1,0:T(8,128)(2,1)S(1)}, bf16[1024,1152]{1,0:T(8,128)(2,1)S(1)}) fusion(f32[1024,2,1152]{2,0,1:T(8,128)} %copy-done.23, bf16[1024,2304]{1,0:T(8,128)(2,1)S(1)} %copy-done.45, bf16[1152,3,2304]{2,0,1:T(8,128)(2,1)} %param.20), kind=kOutput, calls=%fused_computation.23 | convolution fusion | flops 5464129536 | bytes 24182784 | tf_op jit(solution)/shard_map/dot_general | solution.py:44
  555.2 14.2 %collective-permute-done.30 = bf16[128,2304]{1,0:T(8,128)(2,1)S(1)} collective-permute-done((bf16[128,2304]{1,0:T(8,128)(2,1)S(1)}, bf16[128,2304]{1,0:T(8,128)(2,1)S(1)}, u32[]{:S(2)}, u32[]{:S(2)}) %collective-permute-start.30) | collective-permute-done | bytes 589856 | tf_op jit(solution)/shard_map/ppermute | solution.py:417
  570.1 16.3 %collective-permute-done.32 = bf16[128,2304]{1,0:T(8,128)(2,1)S(1)} collective-permute-done((bf16[128,2304]{1,0:T(8,128)(2,1)S(1)}, bf16[128,2304]{1,0:T(8,128)(2,1)S(1)}, u32[]{:S(2)}, u32[]{:S(2)}) %collective-permute-start.32) | collective-permute-done | bytes 589856 | tf_op jit(solution)/shard_map/ppermute | solution.py:417
  590.5 14.9 %bitcast_convert_fusion = bf16[1024,2304]{1,0:T(8,128)(2,1)S(1)} fusion(bf16[1024,2,1152]{2,0,1:T(8,128)(2,1)} %pad_maximum_fusion.1, bf16[1152,3,2304]{2,0,1:T(8,128)(2,1)} %param.20), kind=kOutput, calls=%fused_computation.3 | convolution fusion | flops 10873995264 | bytes 20054016 | tf_op jit(solution)/shard_map/tgf,fgd->td/dot_general | solution.py:620
  617.3 14.6 %collective-permute-done.35 = bf16[128,2304]{1,0:T(8,128)(2,1)S(1)} collective-permute-done((bf16[128,2304]{1,0:T(8,128)(2,1)S(1)}, bf16[128,2304]{1,0:T(8,128)(2,1)S(1)}, u32[]{:S(2)}, u32[]{:S(2)}) %collective-permute-start.35) | collective-permute-done | bytes 589856 | tf_op jit(solution)/shard_map/ppermute | solution.py:442
  635.1 13.9 %collective-permute-done.36 = bf16[128,2304]{1,0:T(8,128)(2,1)} collective-permute-done((bf16[128,2304]{1,0:T(8,128)(2,1)S(1)}, bf16[128,2304]{1,0:T(8,128)(2,1)}, u32[]{:S(2)}, u32[]{:S(2)}) %collective-permute-start.36) | collective-permute-done | bytes 589856 | tf_op jit(solution)/shard_map/ppermute | solution.py:442
  694.8 22.2 %attend_back.1 = (bf16[4,2,64,512]{3,2,1,0:T(8,128)(2,1)}, bf16[8,4,2,64,512]{4,3,2,1,0:T(8,128)(2,1)}) custom-call(s32[1]{0:T(128)} %bitcast.1.shard_ref, bf16[4,2,64,512]{3,2,1,0:T(8,128)(2,1)} %get-tuple-element.152.q_ref, bf16[4,2,64,512]{3,2,1,0:T(8,128)(2,1)} %copy-done.33, f32[4,2,128,128]{3,2,1,0:T(8,128)} %copy-done.18, ...), custom_call_target="tpu_custom_call" | custom-call | tf_op jit(solution)/shard_map/attend_back/pallas_call | solution.py:198
  759.3 13.5 %collective-permute-done.46 = bf16[512,512]{1,0:T(8,128)(2,1)S(1)} collective-permute-done((bf16[512,512]{1,0:T(8,128)(2,1)S(1)}, bf16[512,512]{1,0:T(8,128)(2,1)S(1)}, u32[]{:S(2)}, u32[]{:S(2)}) %collective-permute-start.46) | collective-permute-done | bytes 524320 | tf_op jit(solution)/shard_map/ppermute | solution.py:442
  773.7 13.6 %collective-permute-done.47 = bf16[512,512]{1,0:T(8,128)(2,1)S(1)} collective-permute-done((bf16[512,512]{1,0:T(8,128)(2,1)S(1)}, bf16[512,512]{1,0:T(8,128)(2,1)S(1)}, u32[]{:S(2)}, u32[]{:S(2)}) %collective-permute-start.47) | collective-permute-done | bytes 524320 | tf_op jit(solution)/shard_map/ppermute | solution.py:442
  811.0 21.2 %all-to-all-done.1 = bf16[4,2,64,1024]{3,2,1,0:T(8,128)(2,1)S(1)} async-done(((bf16[4,2,64,1024]{3,2,1,0:T(8,128)(2,1)}), bf16[4,2,64,1024]{3,2,1,0:T(8,128)(2,1)S(1)}, u32[]{:S(2)}, u32[]{:S(2)}) %all-to-all-start.1) | async-done | bytes 1048608 | tf_op jit(solution)/shard_map/all_to_all | solution.py:643
  841.1 37.8 %all-to-all-done.3 = bf16[8,128,768]{1,2,0:T(8,128)(2,1)} async-done(((bf16[8,128,768]{1,2,0:T(8,128)(2,1)}), bf16[8,128,768]{1,2,0:T(8,128)(2,1)}, u32[]{:S(2)}, u32[]{:S(2)}) %all-to-all-start.3) | async-done | bytes 1572896 | tf_op jit(solution)/shard_map/all_to_all | solution.py:672
  895.8 105.7 %all-reduce.6.cloned.1.call-done = (bf16[1152,2304]{1,0:T(8,128)(2,1)}, bf16[1152,2304]{1,0:T(8,128)(2,1)}, bf16[1152,2304]{1,0:T(8,128)(2,1)}) async-done(((bf16[1152,2304]{1,0:T(8,128)(2,1)}, bf16[1152,2304]{1,0:T(8,128)(2,1)}, bf16[1152,2304]{1,0:T(8,128)(2,1)}), (bf16[1152,2304]{1,0:T(8,128)(2,1)}, bf16[1152,2304]{1,0:T(8,128)(2,1)}, bf16[1152,2304]{1,0:T(8,128)(2,1)})) %all-reduce.6.cloned.1.call-update) | async-done | bytes 15925264 | tf_op jit(solution)/shard_map/psum | solution.py:619
  1048.9 52.2 %all-reduce.4.cloned.1.call-done = bf16[768,2304]{1,0:T(8,128)(2,1)} async-done(((bf16[768,2304]{1,0:T(8,128)(2,1)}), bf16[768,2304]{1,0:T(8,128)(2,1)}) %all-reduce.4.cloned.1.call-update) | async-done | bytes 3538960 | tf_op jit(solution)/shard_map/psum | solution.py:686
  (395 shorter events, 489.0 us)
Async XLA Ops:
  7.2 75.7 %all-gather.12.cloned.1.call-start = ((), (), s32[]{:S(2)}) async-start(), calls=%async_computation.9 | async-start | bytes 2949120 | tf_op jit(solution)/shard_map/all_gather | solution.py:516
  7.9 179.4 %all-gather.14.cloned.1.call-start = ((), (), s32[]{:S(2)}) async-start(), calls=%async_computation.10 | async-start | bytes 4718592 | tf_op jit(solution)/shard_map/all_gather | solution.py:541
  23.3 31.3 %collective-permute-start.1 = (bf16[1,256,2304]{2,1,0:T(8,128)(2,1)}, bf16[1,256,2304]{2,1,0:T(8,128)(2,1)}, u32[]{:S(2)}, u32[]{:S(2)}) collective-permute-start(bf16[1,256,2304]{2,1,0:T(8,128)(2,1)} %pick.8), channel_id=1, source_target_pairs={{0,2},{2,4},{3,1},{4,6},{5,3},{8,10},{10,12},{11,9},{12,14},{13,11... | collective-permute-start | bytes 3538952 | tf_op jit(solution)/shard_map/ppermute | solution.py:363
  59.1 18.1 %collective-permute-start.2 = (bf16[1,256,2304]{2,1,0:T(8,128)(2,1)S(1)}, bf16[1,256,2304]{2,1,0:T(8,128)(2,1)}, u32[]{:S(2)}, u32[]{:S(2)}) collective-permute-start(bf16[1,256,2304]{2,1,0:T(8,128)(2,1)S(1)} %pick.9), channel_id=1, source_target_pairs={{0,2},{2,4},{3,1},{4,6},{5,3},{8,10},{10,12},{11,9},{12,14},{13,11... | collective-permute-start | bytes 3538952 | tf_op jit(solution)/shard_map/ppermute | solution.py:363
  138.7 194.0 %all-gather.8.cloned.1.call-start = ((), (), s32[]{:S(2)}) async-start(), calls=%async_computation.5 | async-start | bytes 5308416 | tf_op jit(solution)/shard_map/all_gather | solution.py:577
  210.7 43.1 %collective-permute-start.13 = (bf16[2,128,1152]{2,1,0:T(8,128)(2,1)}, bf16[2,128,1152]{2,1,0:T(8,128)(2,1)}, u32[]{:S(2)}, u32[]{:S(2)}) collective-permute-start(bf16[2,128,1152]{2,1,0:T(8,128)(2,1)} %pad_maximum_fusion.7), channel_id=1, source_target_pairs={{0,8},{8,0},{16,24},{24,16},{1,9},{9,1},{17,25},{25,17},{2,10},{10... | collective-permute-start | bytes 1769480 | tf_op jit(solution)/shard_map/ppermute | solution.py:455
  213.5 47.8 %collective-permute-start.15 = (bf16[2,128,1152]{2,1,0:T(8,128)(2,1)}, bf16[2,128,1152]{2,1,0:T(8,128)(2,1)}, u32[]{:S(2)}, u32[]{:S(2)}) collective-permute-start(bf16[2,128,1152]{2,1,0:T(8,128)(2,1)} %concatenate.38), channel_id=1, source_target_pairs={{0,16},{8,24},{16,0},{24,8},{1,17},{9,25},{17,1},{25,9},{2,18},{10... | collective-permute-start | bytes 1769480 | tf_op jit(solution)/shard_map/ppermute | solution.py:455
  277.8 141.0 %reduce-scatter.2.cloned.1.call-start = ((), (), s32[]{:S(2)}) async-start(), calls=%async_computation.6 | async-start | bytes 5308416 | tf_op jit(solution)/shard_map/reduce_scatter | solution.py:587
  283.3 69.7 %collective-permute-start.17 = (bf16[3,128,2304]{2,1,0:T(8,128)(2,1)}, bf16[3,128,2304]{2,1,0:T(8,128)(2,1)}, u32[]{:S(2)}, u32[]{:S(2)}) collective-permute-start(bf16[3,128,2304]{2,1,0:T(8,128)(2,1)} %get-tuple-element.142), channel_id=1, source_target_pairs={{0,8},{8,0},{16,24},{24,16},{1,9},{9,1},{17,25},{25,17},{2,10},{10... | collective-permute-start | bytes 5308424 | tf_op jit(solution)/shard_map/ppermute | solution.py:575
  283.9 69.1 %collective-permute-start.18 = (bf16[3,128,2304]{2,1,0:T(8,128)(2,1)}, bf16[3,128,2304]{2,1,0:T(8,128)(2,1)}, u32[]{:S(2)}, u32[]{:S(2)}) collective-permute-start(bf16[3,128,2304]{2,1,0:T(8,128)(2,1)} %get-tuple-element.141), channel_id=1, source_target_pairs={{0,16},{8,24},{16,0},{24,8},{1,17},{9,25},{17,1},{25,9},{2,18},{10... | collective-permute-start | bytes 5308424 | tf_op jit(solution)/shard_map/ppermute | solution.py:575
  364.8 145.5 %all-gather.10.cloned.1.call-start = ((), (), s32[]{:S(2)}) async-start(), calls=%async_computation.7 | async-start | bytes 5308416 | tf_op jit(solution)/shard_map/all_gather | solution.py:601
  373.5 79.0 %collective-permute-start.19 = (bf16[2,3,128,2304]{3,2,1,0:T(8,128)(2,1)}, bf16[2,3,128,2304]{3,2,1,0:T(8,128)(2,1)}, u32[]{:S(2)}, u32[]{:S(2)}) collective-permute-start(bf16[2,3,128,2304]{3,2,1,0:T(8,128)(2,1)} %pad_maximum_fusion.2), channel_id=1, source_target_pairs={{0,16},{8,24},{16,0},{24,8},{1,17},{9,25},{17,1},{25,9},{2,18},{10... | collective-permute-start | bytes 10616840 | tf_op jit(solution)/shard_map/ppermute | solution.py:583
  378.9 78.7 %collective-permute-start.20 = (bf16[2,3,128,2304]{3,2,1,0:T(8,128)(2,1)}, bf16[2,3,128,2304]{3,2,1,0:T(8,128)(2,1)}, u32[]{:S(2)}, u32[]{:S(2)}) collective-permute-start(bf16[2,3,128,2304]{3,2,1,0:T(8,128)(2,1)} %pad_maximum_fusion.3), channel_id=1, source_target_pairs={{0,8},{8,0},{16,24},{24,16},{1,9},{9,1},{17,25},{25,17},{2,10},{10... | collective-permute-start | bytes 10616840 | tf_op jit(solution)/shard_map/ppermute | solution.py:583
  466.3 19.9 %collective-permute-start.26 = (bf16[3,128,2304]{2,1,0:T(8,128)(2,1)S(1)}, bf16[3,128,2304]{2,1,0:T(8,128)(2,1)S(1)}, u32[]{:S(2)}, u32[]{:S(2)}) collective-permute-start(bf16[3,128,2304]{2,1,0:T(8,128)(2,1)S(1)} %get-tuple-element.135), channel_id=1, source_target_pairs={{0,1},{1,0},{2,3},{3,2},{4,5},{5,4},{6,7},{7,6},{8,9},{9,8},{10,11... | collective-permute-start | bytes 5308424 | tf_op jit(solution)/shard_map/ppermute | solution.py:503
  521.0 33.1 %collective-permute-start.27 = (bf16[128,2304]{1,0:T(8,128)(2,1)S(1)}, bf16[128,2304]{1,0:T(8,128)(2,1)}, u32[]{:S(2)}, u32[]{:S(2)}) collective-permute-start(bf16[128,2304]{1,0:T(8,128)(2,1)S(1)} %get-tuple-element.90), channel_id=1, source_target_pairs={{0,1},{1,0},{2,3},{3,2},{4,5},{5,4},{6,7},{7,6},{8,9},{9,8},{10,11... | collective-permute-start | bytes 1769480 | tf_op jit(solution)/shard_map/ppermute | solution.py:418
  521.3 31.3 %collective-permute-start.28 = (bf16[128,2304]{1,0:T(8,128)(2,1)S(1)}, bf16[128,2304]{1,0:T(8,128)(2,1)S(1)}, u32[]{:S(2)}, u32[]{:S(2)}) collective-permute-start(bf16[128,2304]{1,0:T(8,128)(2,1)S(1)} %get-tuple-element.90), channel_id=1, source_target_pairs={{0,2},{1,3},{2,6},{3,7},{4,0},{5,1},{6,4},{7,5},{8,10},{9,11},{10,... | collective-permute-start | bytes 1769480 | tf_op jit(solution)/shard_map/ppermute | solution.py:417
  552.5 17.4 %collective-permute-start.29 = (bf16[128,2304]{1,0:T(8,128)(2,1)S(1)}, bf16[128,2304]{1,0:T(8,128)(2,1)S(1)}, u32[]{:S(2)}, u32[]{:S(2)}) collective-permute-start(bf16[128,2304]{1,0:T(8,128)(2,1)S(1)} %collective-permute-done.28), channel_id=1, source_target_pairs={{0,1},{1,0},{2,3},{3,2},{4,5},{5,4},{6,7},{7,6},{8,9},{9,8},{10,11... | collective-permute-start | bytes 1769480 | tf_op jit(solution)/shard_map/ppermute | solution.py:418
  673.5 46.9 %collective-permute-start.38 = (bf16[128,2304]{1,0:T(8,128)(2,1)S(1)}, bf16[128,2304]{1,0:T(8,128)(2,1)}, u32[]{:S(2)}, u32[]{:S(2)}) collective-permute-start(bf16[128,2304]{1,0:T(8,128)(2,1)S(1)} %get-tuple-element.125), channel_id=1, source_target_pairs={{0,1},{1,0},{2,3},{3,2},{4,5},{5,4},{6,7},{7,6},{8,9},{9,8},{10,11... | collective-permute-start | bytes 1769480 | tf_op jit(solution)/shard_map/ppermute | solution.py:418
  673.5 43.5 %collective-permute-start.39 = (bf16[128,2304]{1,0:T(8,128)(2,1)S(1)}, bf16[128,2304]{1,0:T(8,128)(2,1)S(1)}, u32[]{:S(2)}, u32[]{:S(2)}) collective-permute-start(bf16[128,2304]{1,0:T(8,128)(2,1)S(1)} %get-tuple-element.125), channel_id=1, source_target_pairs={{0,2},{1,3},{2,6},{3,7},{4,0},{5,1},{6,4},{7,5},{8,10},{9,11},{10,... | collective-permute-start | bytes 1769480 | tf_op jit(solution)/shard_map/ppermute | solution.py:417
  685.3 316.2 %all-reduce.6.cloned.1.call-start = ((), (), s32[]{:S(2)}) async-start(), calls=%async_computation.11 | async-start | bytes 31850496 | tf_op jit(solution)/shard_map/psum | solution.py:619
  717.0 19.1 %collective-permute-start.40 = (bf16[128,2304]{1,0:T(8,128)(2,1)S(1)}, bf16[128,2304]{1,0:T(8,128)(2,1)S(1)}, u32[]{:S(2)}, u32[]{:S(2)}) collective-permute-start(bf16[128,2304]{1,0:T(8,128)(2,1)S(1)} %collective-permute-done.39), channel_id=1, source_target_pairs={{0,1},{1,0},{2,3},{3,2},{4,5},{5,4},{6,7},{7,6},{8,9},{9,8},{10,11... | collective-permute-start | bytes 1769480 | tf_op jit(solution)/shard_map/ppermute | solution.py:418
  803.8 28.4 %all-to-all-start.1 = ((bf16[4,2,64,1024]{3,2,1,0:T(8,128)(2,1)}), bf16[4,2,64,1024]{3,2,1,0:T(8,128)(2,1)S(1)}, u32[]{:S(2)}, u32[]{:S(2)}) async-start(bf16[4,2,64,1024]{3,2,1,0:T(8,128)(2,1)} %pad_maximum_fusion.6), calls=%async_computation.2 | async-start | bytes 2097152 | tf_op jit(solution)/shard_map/all_to_all | solution.py:643
  835.4 43.5 %all-to-all-start.3 = ((bf16[8,128,768]{1,2,0:T(8,128)(2,1)}), bf16[8,128,768]{1,2,0:T(8,128)(2,1)}, u32[]{:S(2)}, u32[]{:S(2)}) async-start(bf16[8,128,768]{1,2,0:T(8,128)(2,1)} %bitcast.401), calls=%async_computation.4 | async-start | bytes 3145728 | tf_op jit(solution)/shard_map/all_to_all | solution.py:672
  841.0 260.0 %all-reduce.4.cloned.1.call-start = ((), (), s32[]{:S(2)}) async-start(), calls=%async_computation.8 | async-start | bytes 7077888 | tf_op jit(solution)/shard_map/psum | solution.py:686
  (99 other events, 1459.0 us)
Sparse Core Ops, SparseCore 0:
  9.8 40.1 all-gather.11
  138.8 48.4 all-gather.13
  277.9 54.7 all-gather.7
  364.9 53.7 reduce-scatter.1
  461.1 49.2 all-gather.9
  690.3 311.1 all-reduce.5
  1005.0 95.9 all-reduce.3

commit v2 on v1

--- a/solution.py
+++ b/solution.py
@@ -285,17 +285,7 @@
     return steps, urgent_steps
 
 
-def pick_kernel(cands, which_ref, slot_ref, *refs):
-    out_ref = refs[-1]
-    wanted = which_ref[pl.program_id(0)]
-    for code in cands:
-
-        @pl.when(wanted == code)
-        def _(code=code):
-            out_ref[...] = refs[code][...]
-
-
-def pick(places, sources, device, devices):
+def chosen(places, devices):
     names = []
     which = np.zeros((devices, len(places)), np.int32)
     slot = np.zeros((devices, len(places)), np.int32)
@@ -306,29 +296,104 @@
                 names.append(name)
             which[d, k] = names.index(name)
             slot[d, k] = at
+    return names, which, slot
+
+
+def fetch(cands, which_ref, slot_ref, sources, place, buffer, sem):
+    for code in cands[place]:
+
+        @pl.when(which_ref[place] == code)
+        def _(code=code):
+            pltpu.make_async_copy(sources[code].at[slot_ref[place]], buffer, sem).start()
+
+
+def pick_kernel(cands, which_ref, slot_ref, *refs):
+    out_ref, buffers, in_sems, out_sems = refs[-4:]
+    count, deep = len(cands), buffers.shape[0]
+
+    def begin(k):
+        at = k % deep
+        fetch(cands, which_ref, slot_ref, refs, k, buffers.at[at], in_sems.at[at])
+
+    def leaving(k):
+        at = k % deep
+        return pltpu.make_async_copy(buffers.at[at], out_ref.at[k], out_sems.at[at])
+
+    for k in range(min(deep, count)):
+        begin(k)
+    for k in range(count):
+        at = k % deep
+        pltpu.make_async_copy(buffers.at[at], buffers.at[at], in_sems.at[at]).wait()
+        leaving(k).start()
+        again = k - deep // 2
+        if again >= 0 and again + deep < count:
+            leaving(again).wait()
+            begin(again + deep)
+    for k in range(max(0, count - deep), count):
+        leaving(k).wait()
+
+
+def project_kernel(cands, which_ref, slot_ref, rows_ref, *refs):
+    out_ref, buffers, sems = refs[-3:]
+    rows = buffers.shape[1]
+    for k in range(len(cands)):
+        fetch(cands, which_ref, slot_ref, refs, k, buffers.at[k], sems.at[k])
+    for k in range(len(cands)):
+        pltpu.make_async_copy(buffers.at[k], buffers.at[k], sems.at[k]).wait()
+        out_ref[:, k * rows : (k + 1) * rows] = dot_nt(rows_ref[...], buffers[k]).astype(bf16)
+
+
+def apply_kernel(cands, which_ref, slot_ref, rows_ref, *refs):
+    out_ref, buffers, sems = refs[-3:]
+    _, rows, width = buffers.shape
+    for k in range(len(cands)):
+        fetch(cands, which_ref, slot_ref, refs, k, buffers.at[k], sems.at[k])
+    for k in range(len(cands)):
+        pltpu.make_async_copy(buffers.at[k], buffers.at[k], sems.at[k]).wait()
+    step = width // 3 if width % 384 == 0 else width
+    for low in range(0, width, step):
+        total = dot_nn(rows_ref[:, :rows], buffers[0, :, low : low + step])
+        for k in range(1, len(cands)):
+            total += dot_nn(
+                rows_ref[:, k * rows : (k + 1) * rows], buffers[k, :, low : low + step]
+            )
+        out_ref[:, low : low + step] = total.astype(bf16)
+
+
+def pick(places, sources, device, devices, kind="pick", rows_in=None):
+    names, which, slot = chosen(places, devices)
     _, rows, width = sources["mine"].shape
     table = jnp.asarray(np.concatenate([which, slot], axis=1))[device]
-    block = (1, rows // 4, width)
-
-    def spec(code):
-        def index(k, r, which_ref, slot_ref):
-            hit = which_ref[k] == code
-            return jnp.where(hit, slot_ref[k], 0), jnp.where(hit, r, 0), 0
-
-        return pl.BlockSpec(block, index)
-
+    count = len(places)
+    cands = [sorted(set(which[:, k].tolist())) for k in range(count)]
+    kernel = {"pick": pick_kernel, "project": project_kernel, "apply": apply_kernel}[kind]
+    args = [sources[name] for name in names]
+    in_specs = [pl.BlockSpec(memory_space=pl.ANY)] * len(names)
+    if kind == "pick":
+        deep = min(count, 8)
+        out_spec = pl.BlockSpec(memory_space=pl.ANY)
+        out_shape = (count, rows, width)
+        sems = [pltpu.SemaphoreType.DMA((deep,)), pltpu.SemaphoreType.DMA((deep,))]
+    else:
+        deep = count
+        args = [rows_in] + args
+        in_specs = [pl.BlockSpec(memory_space=pltpu.VMEM)] + in_specs
+        out_spec = pl.BlockSpec(memory_space=pltpu.VMEM)
+        out_shape = (rows_in.shape[0], count * rows if kind == "project" else width)
+        sems = [pltpu.SemaphoreType.DMA((deep,))]
     return pl.pallas_call(
-        functools.partial(pick_kernel, range(len(names))),
+        functools.partial(kernel, cands),
         grid_spec=pltpu.PrefetchScalarGridSpec(
             num_scalar_prefetch=2,
-            grid=(len(places), 4),
-            in_specs=[spec(code) for code in range(len(names))],
-            out_specs=pl.BlockSpec(block, lambda k, r, which_ref, slot_ref: (k, r, 0)),
+            grid=(1,),
+            in_specs=in_specs,
+            out_specs=out_spec,
+            scratch_shapes=[pltpu.VMEM((deep, rows, width), bf16)] + sems,
         ),
-        out_shape=jax.ShapeDtypeStruct((len(places), rows, width), bf16),
-        compiler_params=pltpu.CompilerParams(vmem_limit_bytes=40 * 2**20),
-        name="pick",
-    )(table[: len(places)], table[len(places) :], *[sources[name] for name in names])
+        out_shape=jax.ShapeDtypeStruct(out_shape, bf16),
+        compiler_params=pltpu.CompilerParams(vmem_limit_bytes=58 * 2**20),
+        name=kind,
+    )(table[:count], table[count:], *args)
 
 
 def routed_weights(attn_weight, column, shard, columns, shards, between):
@@ -342,35 +407,84 @@
     urgent = items - HQ // columns
     steps, urgent_steps = route(columns, chips, 2 * count)
     mine = attn_weight.reshape(count, HD, width)
-    sources = {"mine": mine, "theirs": lax.ppermute(mine, "fsdp", swap)}
+    theirs = between("start", lax.ppermute(mine, "fsdp", swap))
+    sources = {"mine": mine, "theirs": theirs}
     at = [{} for _ in range(items)]
     for c in range(columns):
         for f in range(shards):
             for k, g in enumerate(granules_of(c, columns)):
                 if g // (2 * count) == f // 2:
                     at[k][c * shards + f] = ("mine" if g // count == f else "theirs", g % count)
-    first = None
+    sends = []
     for number, moves in enumerate(steps):
-        place = {}
-        pairs = []
+        own, passed, pairs = {}, {}, []
         for (c, z, core), k in moves.items():
             here = c * shards + 2 * z + core
             to = here + (2, -2)[core]
-            place[here] = at[k][here]
+            name, slot = at[k][here]
+            if name in ("mine", "theirs"):
+                own[here] = (name, slot)
+            else:
+                passed[here] = name
             pairs.append((here, to))
             at[k][to] = ("got%d" % number, 0)
             at[k][to ^ 1] = ("swapped%d" % number, 0)
-        got = lax.ppermute(pick([place], sources, device, devices), ("seq", "fsdp"), pairs)
-        got = between(number, got)
+        sends.append((own, passed, pairs))
+    with_own = [n for n in range(1, len(sends)) if sends[n][0]]
+    own_first = pick([sends[0][0]], sources, device, devices)
+    own_later = None
+    for number, (own, passed, pairs) in enumerate(sends):
+        if number == 0:
+            piece = own_first
+        else:
+            names = sorted(set(passed.values()))
+            code = np.zeros((devices,), np.int32)
+            for d, name in passed.items():
+                code[d] = 1 + names.index(name)
+            here = jnp.asarray(code)[device]
+            piece = sources[names[-1]]
+            for i, name in enumerate(names[:-1]):
+                piece = jnp.where(here == 1 + i, sources[name], piece)
+            if number in with_own:
+                place = with_own.index(number)
+                piece = jnp.where(here == 0, own_later[place : place + 1], piece)
+        got = lax.ppermute(piece, ("seq", "fsdp"), pairs)
+        if number == 0:
+            own_later = pick([sends[n][0] for n in with_own], sources, device, devices)
+            got, own_later = lax.optimization_barrier((got, own_later))
+        if number < urgent_steps:
+            got = between(number, got)
         if 0 < number < urgent_steps:
             before = "swapped%d" % (number - 1)
             got, sources[before] = lax.optimization_barrier((got, sources[before]))
         sources["got%d" % number] = got
-        sources["swapped%d" % number] = lax.ppermute(got, "fsdp", swap)
+        if number < urgent_steps:
+            sources["swapped%d" % number] = lax.ppermute(got, "fsdp", swap)
         if number + 1 == urgent_steps:
-            first = pick(at[:urgent], sources, device, devices)
-            first, sources = between(None, (first, sources))
-    return first, pick(at[urgent:], sources, device, devices)
+            ready = dict(sources)
+            made = between(
+                None,
+                lambda times: pick(at[:urgent], ready, device, devices, "project", times),
+            )
+
+    def first(after):
+        held, after = lax.optimization_barrier((ready, after))
+        return pick(at[:urgent], held, device, devices)
+
+    held = None
+
+    def times_rest(rows_in):
+        nonlocal held
+        held, rows_in = lax.optimization_barrier((sources, rows_in))
+        for number in range(urgent_steps, len(steps)):
+            held["swapped%d" % number] = lax.ppermute(held["got%d" % number], "fsdp", swap)
+        return pick(at[urgent:], held, device, devices, "apply", rows_in)
+
+    def others(after):
+        kept, after = lax.optimization_barrier((held, after))
+        return pick(at[urgent:], kept, device, devices)
+
+    return made, first, times_rest, others
 
 
 def column_weights(attn_weight, column, shard, columns, shards, between):
@@ -384,7 +498,15 @@
     taken = jnp.concatenate(
         [lax.dynamic_slice_in_dim(whole, place[k], 1, 0) for k in range(table.shape[1])], axis=0
     )
-    return taken[: per + 2], taken[per + 2 :]
+    made = between(
+        None, lambda times: dot_nt(times, taken[: per + 2].reshape(-1, width)).astype(bf16)
+    )
+    return (
+        made,
+        lambda after: taken[: per + 2],
+        lambda rows_in: dot_nn(rows_in, taken[per + 2 :].reshape(-1, width)).astype(bf16),
+        lambda after: taken[per + 2 :],
+    )
 
 
 def ring_of(chips):
@@ -405,7 +527,7 @@
     return chips, pairs, behind
 
 
-def ring_gather(block, shard, shards):
+def ring_gather(block, shard, shards, beside=None):
     chips, pairs, behind = ring_tables(shards)
     swap = [(f, f ^ 1) for f in range(shards)]
     source = jnp.asarray(behind)[shard]
@@ -415,6 +537,7 @@
     for t in range(chips):
         if t:
             held = lax.ppermute(held, "fsdp", pairs)
+            held = beside(t, held) if beside else held
         other = lax.ppermute(held, "fsdp", swap)
         out = lax.dynamic_update_index_in_dim(out, held, 2 * source[t] + core, 0)
         out = lax.dynamic_update_index_in_dim(out, other, 2 * source[t] + 1 - core, 0)
@@ -451,12 +574,12 @@
     half = parts.shape[-1] // 2
     done = []
     for first, second, cut in ((1, 2, slice(0, half)), (2, 1, slice(half, None))):
-        low = parts[..., cut].astype(bf16)
+        low = parts[..., cut]
         got = lax.ppermute(
             jnp.concatenate([low[first : first + 1], low[3:]], axis=0), "seq", partners(4, first)
         )
-        keep = parts[0, ..., cut] + got[0].astype(f32)
-        away = parts[second, ..., cut] + got[1].astype(f32)
+        keep = low[0].astype(f32) + got[0].astype(f32)
+        away = low[second].astype(f32) + got[1].astype(f32)
         done.append(
             keep + lax.ppermute(away.astype(bf16), "seq", partners(4, second)).astype(f32)
         )
@@ -484,8 +607,29 @@
     swap = [(f, f ^ 1) for f in range(shards)]
     shard_arg = shard.astype(jnp.int32).reshape(1)
 
-    def whole_weights(granules, near, far):
-        cut = granules.shape[0] // 2
+    def core_half(granules):
+        return lax.dynamic_index_in_dim(
+            granules.reshape(-1, 2, HALF, width), core, 1, keepdims=False
+        )
+
+    def round_start(granules):
+        lanes = core_half(granules)
+        cut = lanes.shape[0] // 2
+        lanes = (lanes[:cut], lanes[cut:])
+        near = tuple(
+            lax.ppermute(lane, "seq", partners(4, bit)) for lane, bit in zip(lanes, (1, 2))
+        )
+        return lanes, near
+
+    def round_on(lanes, near):
+        return tuple(
+            tuple(lax.ppermute(piece, "seq", partners(4, bit)) for piece in pieces)
+            for pieces, bit in zip(zip(lanes, near), (2, 1))
+        )
+
+    def all_columns(granules, near, far):
+        count = granules.shape[0]
+        cut = count // 2
         come = {
             (0, 1): near[0],
             (0, 2): far[0][0],
@@ -494,66 +638,69 @@
             (1, 1): far[1][0],
             (1, 3): far[1][1],
         }
-        outs = []
-        for begin, end in ((0, per + 2), (per + 2, 2 * per + 2)):
-            out = jnp.zeros((columns, end - begin, 2, HALF, width), bf16)
-            full = granules[begin:end].reshape(1, end - begin, 2, HALF, width)
-            outs.append(lax.dynamic_update_slice(out, full, (column, 0, 0, 0, 0)))
+        sources = {"mine": granules.reshape(2 * count, HALF, width)}
         for (part, hop), lane in come.items():
-            other = lax.ppermute(lane, "fsdp", swap)
-            for half, piece in ((core, lane), (1 - core, other)):
-                for i, (begin, end) in enumerate(((0, per + 2), (per + 2, 2 * per + 2))):
-                    low, high = max(begin, part * cut), min(end, (part + 1) * cut)
-                    if low < high:
-                        chosen = piece[low - part * cut : high - part * cut]
-                        outs[i] = lax.dynamic_update_slice(
-                            outs[i],
-                            chosen.reshape(1, high - low, 1, HALF, width),
-                            (column ^ hop, low - begin, half, 0, 0),
-                        )
-        return outs[0].reshape(-1, width), outs[1].reshape(-1, width)
+            sources["own%d%d" % (part, hop)] = lane
+            sources["other%d%d" % (part, hop)] = lax.ppermute(lane, "fsdp", swap)
+        places = []
+        for home in range(columns):
+            for k in range(count):
+                for half in range(2):
+                    place = {}
+                    for c in range(columns):
+                        for f in range(shards):
+                            part, hop = int(k >= cut), home ^ c
+                            whose = "own" if f % 2 == half else "other"
+                            place[c * shards + f] = (
+                                ("%s%d%d" % (whose, part, hop), k - part * cut)
+                                if hop
+                                else ("mine", 2 * k + half)
+                            )
+                    places.append(place)
+        device = column * shards + shard
+        return pick(places, sources, device, columns * shards).reshape(-1, width)
 
     token_slices = lax.all_gather(tokens, "seq", axis=0)
     gain_rows = lax.all_gather(norm_gains, "fsdp", axis=1, tiled=True).astype(f32)
-    normed_slices = rms_scale(
-        token_slices.reshape(-1, width).astype(f32), gain_rows[0]
-    ).astype(bf16)
-    heads = None
+    normed_slices = None
 
     def between(step, value):
-        nonlocal gain_rows, normed_slices, heads
-        if step == 0:
+        nonlocal gain_rows, normed_slices
+        if step == 1:
             value, gain_rows = lax.optimization_barrier((value, gain_rows))
+            normed_slices = rms_scale(
+                token_slices.reshape(-1, width).astype(f32), gain_rows[0]
+            ).astype(bf16)
         if step == 2:
             value, normed_slices = lax.optimization_barrier((value, normed_slices))
         if step is None:
-            heads = dot_nt(normed_slices, value[0].reshape(-1, width)).astype(bf16)
-            heads, value = lax.optimization_barrier((heads, value))
+            if normed_slices is None:
+                normed_slices = rms_scale(
+                    token_slices.reshape(-1, width).astype(f32), gain_rows[0]
+                ).astype(bf16)
+            return value(normed_slices)
         return value
 
-    weight_in, weight_out = column_weights(
+    heads, first_weights, times_out, out_weights = column_weights(
         attn_weight, column, shard, columns, shards, between
     )
-    if heads is None:
-        heads = dot_nt(normed_slices, weight_in.reshape(-1, width)).astype(bf16)
     heads = heads.reshape(columns, seqs, rows, (per + 2) * HD)
     queries = heads[..., : per * HD]
     kv_all = lax.all_gather(heads[..., per * HD :], "fsdp", axis=0)
+    weight_in = first_weights(heads)
+    if columns == 4:
+        in_lanes, in_near = round_start(weight_in)
+        kv_all, in_lanes = lax.optimization_barrier((kv_all, in_lanes))
 
     mixed, lse = attend(shard_arg, queries, kv_all)
-    mixed_rows = lax.all_to_all(mixed, "seq", split_axis=0, concat_axis=0, tiled=True)
-    mixed_rows = mixed_rows.transpose(1, 2, 0, 3).reshape(own_rows, HQ * HD)
-    weight_out_rows = weight_out.reshape(-1, width)
     if columns == 4:
         by_partner = jnp.concatenate(
             [lax.dynamic_slice_in_dim(mixed, column ^ k, 1, 0) for k in range(columns)], axis=0
         ).reshape(columns * own_rows, per * HD)
-        attn_out = column_scatter(
-            dot_nn(by_partner, weight_out_rows).reshape(columns, own_rows, width)
-        )
+        attn_out = column_scatter(times_out(by_partner).reshape(columns, own_rows, width))
     else:
         attn_out = lax.psum_scatter(
-            dot_nn(mixed.reshape(-1, per * HD), weight_out_rows).astype(bf16),
+            times_out(mixed.reshape(-1, per * HD)),
             "seq",
             scatter_dimension=0,
             tiled=True,
@@ -563,139 +710,163 @@
     residual = flat_tokens + rms_scale(attn_out, gain_rows[1])
     normed_ffn = rms_scale(residual, gain_rows[2]).astype(bf16)
 
-    granules = jnp.concatenate([weight_in, weight_out], axis=0)
     if columns == 4:
-        lanes = lax.dynamic_index_in_dim(
-            granules.reshape(-1, 2, HALF, width), core, 1, keepdims=False
-        )
-        lanes, normed_ffn = lax.optimization_barrier((lanes, normed_ffn))
-        cut = lanes.shape[0] // 2
-        lanes = (lanes[:cut], lanes[cut:])
-        near = tuple(
-            lax.ppermute(lane, "seq", partners(4, bit)) for lane, bit in zip(lanes, (1, 2))
-        )
+        normed_ffn, in_near = lax.optimization_barrier((normed_ffn, in_near))
+        in_far = round_on(in_lanes, in_near)
+    mixed_later, normed_ffn = lax.optimization_barrier((mixed, normed_ffn))
+    weight_out = out_weights(normed_ffn)
     ffn_in = lax.all_gather(normed_ffn, "fsdp", axis=0, tiled=True)
+    mixed_rows = lax.all_to_all(mixed_later, "seq", split_axis=0, concat_axis=0, tiled=True)
+    mixed_rows = mixed_rows.transpose(1, 2, 0, 3).reshape(own_rows, HQ * HD)
+    if columns == 4:
+        out_lanes, out_near = round_start(weight_out)
+        ffn_in, out_lanes, mixed_rows = lax.optimization_barrier((ffn_in, out_lanes, mixed_rows))
     gate_up = jnp.einsum("td,fgd->tgf", ffn_in, ffn_weight[:, :2], preferred_element_type=f32)
     hidden = gated_units(gate_up[:, 0], gate_up[:, 1]).astype(bf16)
     if columns == 4:
-        hidden, near = lax.optimization_barrier((hidden, near))
-        far = tuple(
-            lax.ppermute(jnp.stack([lane, got]), "seq", partners(4, bit))
-            for lane, got, bit in zip(lanes, near, (2, 1))
-        )
-    branch = dot_nn(hidden, ffn_weight[:, 2])
-    ffn_out = lax.psum_scatter(
-        branch.astype(bf16), "fsdp", scatter_dimension=0, tiled=True
-    ).astype(f32)
+        hidden, out_near = lax.optimization_barrier((hidden, out_near))
+        out_far = round_on(out_lanes, out_near)
+    branch = dot_nn(hidden, ffn_weight[:, 2]).astype(bf16)
     if columns == 4:
-        ffn_out, far = lax.optimization_barrier((ffn_out, far))
-        weight_in_all, weight_out_all = whole_weights(granules, near, far)
+        branch, in_far = lax.optimization_barrier((branch, in_far))
+    ffn_out = lax.psum_scatter(branch, "fsdp", scatter_dimension=0, tiled=True).astype(f32)
+    if columns == 4:
+        weight_in_all = all_columns(weight_in, in_near, in_far)
+        ffn_out, weight_in_all = lax.optimization_barrier((ffn_out, weight_in_all))
     else:
-        whole = lax.all_gather(granules, "seq", axis=0)
-        weight_in_all = whole[:, : per + 2].reshape(-1, width)
-        weight_out_all = whole[:, per + 2 :].reshape(-1, width)
+        weight_in_all = lax.all_gather(weight_in, "seq", axis=0).reshape(-1, width)
+        weight_out_all = lax.all_gather(weight_out, "seq", axis=0).reshape(-1, width)
     result = residual + rms_scale(ffn_out, gain_rows[3])
     block_out = result.astype(bf16).reshape(tokens.shape)
     grad_ffn, gain_terms = norm_back(ffn_out, gain_rows[3], flat_cot)
     gain_last = jnp.sum(gain_terms, axis=0)
     grad_ffn_all = lax.all_gather(grad_ffn.astype(bf16), "fsdp", axis=0, tiled=True)
-    grad_ffn_all, weight_in_all, weight_out_all = lax.optimization_barrier(
-        (grad_ffn_all, weight_in_all, weight_out_all)
-    )
-    down_part = dot_tn(hidden, grad_ffn_all).astype(bf16)
-    grad_ffn_all, down_part = lax.optimization_barrier((grad_ffn_all, down_part))
+    if columns == 4:
+        weight_out_all = all_columns(weight_out, out_near, out_far)
+        grad_ffn_all, weight_out_all = lax.optimization_barrier((grad_ffn_all, weight_out_all))
+
     normed_own = rms_scale(flat_tokens, gain_rows[0]).astype(bf16)
-    normed_own, grad_ffn_all = lax.optimization_barrier((normed_own, grad_ffn_all))
-    normed_all = ring_gather(normed_own, shard, shards).reshape(-1, width)
-    grad_hidden = dot_nt(grad_ffn_all, ffn_weight[:, 2])
-    unused, gated_pull = jax.vjp(gated_units, gate_up[:, 0], gate_up[:, 1])
-    grad_gate, grad_up = gated_pull(grad_hidden)
-    grad_gate_up = jnp.stack([grad_gate, grad_up], axis=1).astype(bf16)
-    gate_part = dot_tn(grad_gate_up[:, 0], ffn_in).astype(bf16)
-    up_part = dot_tn(grad_gate_up[:, 1], ffn_in).astype(bf16)
-    grad_gate_up, gate_part, up_part, normed_all = lax.optimization_barrier(
-        (grad_gate_up, gate_part, up_part, normed_all)
-    )
-    gate_grad, up_grad, down_grad = lax.psum((gate_part, up_part, down_part), "seq")
-    grad_in = jnp.einsum(
-        "tgf,fgd->td", grad_gate_up, ffn_weight[:, :2], preferred_element_type=f32
-    )
-    grad_normed_ffn = ring_scatter(
-        grad_in.astype(bf16).reshape(shards, own_rows, width), shard, shards
-    )
-
-    grad_mid, gain_pre_ffn = norm_back(residual, gain_rows[2], grad_normed_ffn)
-    grad_residual = flat_cot + grad_mid
-    grad_attn, gain_post_attn = norm_back(attn_out, gain_rows[1], grad_residual)
-    grad_attn_low = grad_attn.astype(bf16)
-    grad_mixed = (
-        dot_nt(grad_attn_low, weight_out_all).astype(bf16).reshape(seqs, rows, columns, per * HD)
-    )
-    grad_heads = lax.all_to_all(
-        grad_mixed.transpose(2, 0, 1, 3), "seq", split_axis=0, concat_axis=0, tiled=True
-    )
-    grad_attn_all = ring_gather(grad_attn_low, shard, shards).reshape(-1, width)
-    grad_queries, grad_kv = attend_back(shard_arg, queries, grad_heads, lse, kv_all)
-    grad_kv, grad_attn_all = lax.optimization_barrier((grad_kv, grad_attn_all))
-    grad_kv_own = ring_scatter(
-        grad_kv.reshape(shards, columns * own_rows, 2 * HD), shard, shards
-    ).astype(bf16).reshape(columns, seqs, rows, 2 * HD)
-    grad_proj = lax.all_to_all(
-        jnp.concatenate([grad_queries, grad_kv_own], axis=-1),
-        "seq",
-        split_axis=0,
-        concat_axis=0,
-        tiled=True,
-    )
-    grad_rows = grad_proj.reshape(columns, own_rows, (per + 2) * HD).transpose(1, 0, 2)
-    grad_normed = dot_nn(grad_rows.reshape(own_rows, -1), weight_in_all)
-    grad_tokens, gain_pre_attn = norm_back(flat_tokens, gain_rows[0], grad_normed)
-    token_grad = (grad_residual + grad_tokens).reshape(tokens.shape)
-
-
-    def shared(copies):
-        if columns == KVH:
-            return copies.reshape(own_rows, -1)
-        summed = copies.reshape(own_rows, KVH, columns // KVH, HD).astype(f32).sum(axis=2)
-        return summed.astype(bf16).reshape(own_rows, -1)
-
-    weight_cols = jnp.concatenate(
-        [
-            grad_rows[:, :, : per * HD].reshape(own_rows, -1),
-            shared(grad_rows[:, :, per * HD : (per + 1) * HD]),
-            shared(grad_rows[:, :, (per + 1) * HD :]),
-            mixed_rows,
-        ],
-        axis=1,
-    )
-    shard_cols = attn_weight.shape[0]
-    col_all = lax.all_to_all(
-        weight_cols.reshape(own_rows, shards, shard_cols).transpose(1, 0, 2),
-        "fsdp",
-        split_axis=0,
-        concat_axis=0,
-        tiled=True,
-    ).reshape(-1, shard_cols)
-    is_out = (shard * shard_cols + jnp.arange(shard_cols)) >= (HQ + 2 * KVH) * HD
-    attn_grad = dot_tn(jnp.where(is_out, 0, col_all), normed_all) + dot_tn(
-        jnp.where(is_out, col_all, 0), grad_attn_all
-    )
-    attn_grad_low, gate_grad, up_grad, down_grad = lax.optimization_barrier(
-        (attn_grad.astype(bf16), gate_grad, up_grad, down_grad)
-    )
-    attn_total = lax.psum(attn_grad_low, "seq").astype(f32)
+    grad_ffn_all, normed_own = lax.optimization_barrier((grad_ffn_all, normed_own))
+    kept = {}
+
+    def beside(step, held):
+        if step == 1:
+            part = dot_tn(hidden, grad_ffn_all).astype(bf16)
+            held, kept["down"], kept["all"] = lax.optimization_barrier((held, part, grad_ffn_all))
+        if step == 2:
+            grad_hidden = dot_nt(kept["all"], ffn_weight[:, 2])
+            unused, gated_pull = jax.vjp(gated_units, gate_up[:, 0], gate_up[:, 1])
+            grad_gate, grad_up = gated_pull(grad_hidden)
+            part = jnp.stack([grad_gate, grad_up], axis=1).astype(bf16)
+            held, kept["units"] = lax.optimization_barrier((held, part))
+        if step == 3:
+            parts = (
+                dot_tn(kept["units"][:, 0], ffn_in).astype(bf16),
+                dot_tn(kept["units"][:, 1], ffn_in).astype(bf16),
+            )
+            held, kept["up"], kept["units"] = lax.optimization_barrier(
+                (held, parts, kept["units"])
+            )
+        return held
+
+    normed_all = ring_gather(normed_own, shard, shards, beside).reshape(-1, width)
+    grad_gate_up = kept["units"]
+    gate_grad, up_grad, down_grad = lax.psum((*kept["up"], kept["down"]), "seq")
+
+    def attention_back():
+        grad_in = jnp.einsum(
+            "tgf,fgd->td", grad_gate_up, ffn_weight[:, :2], preferred_element_type=f32
+        )
+        grad_normed_ffn = ring_scatter(
+            grad_in.astype(bf16).reshape(shards, own_rows, width), shard, shards
+        )
+        grad_mid, gain_pre_ffn = norm_back(residual, gain_rows[2], grad_normed_ffn)
+        grad_residual = flat_cot + grad_mid
+        grad_attn, gain_post_attn = norm_back(attn_out, gain_rows[1], grad_residual)
+        grad_attn_low = grad_attn.astype(bf16)
+        grad_mixed = (
+            dot_nt(grad_attn_low, weight_out_all)
+            .astype(bf16)
+            .reshape(seqs, rows, columns, per * HD)
+        )
+        grad_heads = lax.all_to_all(
+            grad_mixed.transpose(2, 0, 1, 3), "seq", split_axis=0, concat_axis=0, tiled=True
+        )
+        grad_attn_all = ring_gather(grad_attn_low, shard, shards).reshape(-1, width)
+        grad_queries, grad_kv = attend_back(shard_arg, queries, grad_heads, lse, kv_all)
+        grad_kv, grad_attn_all = lax.optimization_barrier((grad_kv, grad_attn_all))
+        grad_kv_own = (
+            ring_scatter(grad_kv.reshape(shards, columns * own_rows, 2 * HD), shard, shards)
+            .astype(bf16)
+            .reshape(columns, seqs, rows, 2 * HD)
+        )
+        grad_proj = lax.all_to_all(
+            jnp.concatenate([grad_queries, grad_kv_own], axis=-1),
+            "seq",
+            split_axis=0,
+            concat_axis=0,
+            tiled=True,
+        )
+        grad_rows = grad_proj.reshape(columns, own_rows, (per + 2) * HD).transpose(1, 0, 2)
+        grad_normed = dot_nn(grad_rows.reshape(own_rows, -1), weight_in_all)
+        grad_tokens, gain_pre_attn = norm_back(flat_tokens, gain_rows[0], grad_normed)
+        token_grad = (grad_residual + grad_tokens).reshape(tokens.shape)
+
+        def shared(copies):
+            if columns == KVH:
+                return copies.reshape(own_rows, -1)
+            summed = copies.reshape(own_rows, KVH, columns // KVH, HD).astype(f32).sum(axis=2)
+            return summed.astype(bf16).reshape(own_rows, -1)
+
+        weight_cols = jnp.concatenate(
+            [
+                grad_rows[:, :, : per * HD].reshape(own_rows, -1),
+                shared(grad_rows[:, :, per * HD : (per + 1) * HD]),
+                shared(grad_rows[:, :, (per + 1) * HD :]),
+                mixed_rows,
+            ],
+            axis=1,
+        )
+        shard_cols = attn_weight.shape[0]
+        col_all = lax.all_to_all(
+            weight_cols.reshape(own_rows, shards, shard_cols).transpose(1, 0, 2),
+            "fsdp",
+            split_axis=0,
+            concat_axis=0,
+            tiled=True,
+        ).reshape(-1, shard_cols)
+        is_out = (shard * shard_cols + jnp.arange(shard_cols)) >= (HQ + 2 * KVH) * HD
+        attn_grad = dot_tn(jnp.where(is_out, 0, col_all), normed_all) + dot_tn(
+            jnp.where(is_out, col_all, 0), grad_attn_all
+        )
+        gain_grad = jnp.stack(
+            [
+                jnp.sum(gain_pre_attn, axis=0),
+                jnp.sum(gain_post_attn, axis=0),
+                jnp.sum(gain_pre_ffn, axis=0),
+                gain_last,
+            ]
+        )
+        return attn_grad.astype(bf16), gain_grad, token_grad
+
+    def nothing():
+        return (
+            jnp.zeros(attn_weight.shape, bf16),
+            jnp.zeros((4, width), f32),
+            jnp.zeros(tokens.shape, f32),
+        )
+
+    attn_grad, gain_grad, token_grad = lax.cond(
+        shard < 2**20, attention_back, nothing
+    )
+    attn_grad, gate_grad, up_grad, down_grad = lax.optimization_barrier(
+        (attn_grad, gate_grad, up_grad, down_grad)
+    )
+    attn_total = lax.psum(attn_grad, "seq").astype(f32)
     ffn_grad = widen_plane(down_grad, 2, 3, None)
     ffn_grad = widen_plane(gate_grad, 0, 3, ffn_grad)
     ffn_grad = widen_plane(up_grad, 1, 3, ffn_grad)
     ffn_grad = ffn_grad.transpose(1, 0, 2)
-    gain_grad = jnp.stack(
-        [
-            jnp.sum(gain_pre_attn, axis=0),
-            jnp.sum(gain_post_attn, axis=0),
-            jnp.sum(gain_pre_ffn, axis=0),
-            gain_last,
-        ]
-    )
     gain_total = lax.dynamic_slice_in_dim(
         sum_everywhere(gain_grad, columns, shards),
         shard * norm_gains.shape[1],

time: 1130 us -> 962 us (0.85)
  waiting for transfers between devices: 548 us -> 443 us
  local copies, waits for them, and re-layouts: 130 us -> 80.8 us
  starting transfers between devices: 127 us -> 96.8 us
  Pallas kernels: 83.3 us -> 108 us
  loops' own time: 0 us -> 18.5 us
    psum x2, waiting for transfers between devices: 158 us -> 57 us  [the longest x1 57 us: local(): attn_total = lax.psum(attn_grad, 'seq').astype(f32)]
    dynamic_update_slice x20 -> x0, local copies, waits for them, and re-layouts: 36.7 us -> none  [the longest x18 32.4 us: whole_weights(): lax.dynamic_update_slice(outs[i], chosen.reshape(1, high - low, 1, HALF,...]
    ppermute x17 -> x33, waiting for transfers between devices: 53 us -> 80.1 us  [the longest x8 38.9 us: round_on(): lax.ppermute(piece, 'seq', partners(4, bit))]
    ppermute x2, starting transfers between devices: 37.1 us -> 11.5 us  [column_scatter(): lax.ppermute(jnp.concatenate([low[first:first + 1], low[3:]], axis=0), 's...]
    ppermute x6, waiting for transfers between devices: 53.5 us -> 29.9 us  [ring_gather(): held = lax.ppermute(held, 'fsdp', pairs)]
    pallas_call x8, Pallas kernels: 32.7 us -> 56.1 us  [pick(): pl.pallas_call(functools.partial(kernel, cands), grid_spec=pltpu.Prefetch...]
    all_gather x1, waiting for transfers between devices: 19.7 us -> 39.9 us  [local(): kv_all = lax.all_gather(heads[..., per * HD:], 'fsdp', axis=0)]
    unnamed x116 -> x113, local copies, waits for them, and re-layouts: 31.9 us -> 12 us
  transfers between devices with their start and end apart: 65 -> 79, of which waited for: 40 -> 51; matrix products, arithmetic and copies ran while one was open for 18% -> 22% of each run, Pallas kernels for 5% -> 9%
where the time goes in v2:
time: 962 us; the launch traced here: 951 us
  waiting for transfers between devices  443 us (46%)
  Pallas kernels  108 us (11%)
  matrix products  107 us (11%)
  starting transfers between devices  96.8 us (10%)
  local copies, waits for them, and re-layouts  80.8 us (8%)
  other arithmetic  55.6 us (6%)
  blocking collectives  21.1 us (2%)
  between operations  19.6 us (2%)
  loops' own time  18.5 us (2%)
    ppermute x6, waiting for transfers between devices, ring_scatter(): lax.ppermute(total.astype(bf16), 'fsdp', pairs).astype(f32)  59.7 us
    psum x1, waiting for transfers between devices, local(): attn_total = lax.psum(attn_grad, 'seq').astype(f32)  57 us
    pallas_call x8, Pallas kernels, pick(): pl.pallas_call(functools.partial(kernel, cands), grid_spec=pltpu.Prefetch...  56.1 us
    dot_general x5, matrix products, dot_tn(): lax.dot_general(a, b, (((0,), (0,)), ((), ())), preferred_element_type=f32)  40 us
    all_gather x1, waiting for transfers between devices, local(): kv_all = lax.all_gather(heads[..., per * HD:], 'fsdp', axis=0)  39.9 us
    ppermute x8, waiting for transfers between devices, round_on(): lax.ppermute(piece, 'seq', partners(4, bit))  38.9 us
    all_gather x1, waiting for transfers between devices, local(): ffn_in = lax.all_gather(normed_ffn, 'fsdp', axis=0, tiled=True)  33 us
    ppermute x6, waiting for transfers between devices, ring_gather(): held = lax.ppermute(held, 'fsdp', pairs)  29.9 us
  transfers between devices with their start and end apart: 79, of which 51 were waited for; matrix products, arithmetic and copies ran while one was open for 22% of the time, Pallas kernels for 9%

profile of v2, /device:TPU:0, one launch (start us, length us, event | category | flops | bytes accessed | tf_op | source)
XLA Modules:
  0.0 951.1 jit_solution(1116048428990539938)
XLA Ops:
  47.2 21.1 %all-gather.2 = bf16[8,288,4]{1,2,0:T(4,128)(2,1)S(1)} all-gather(bf16[1,288,4]{1,2,0:T(4,128)(2,1)S(1)} %bitcast.351), channel_id=1, replica_groups=mesh['seq'=4,'fsdp'=8] {'fsdp'}, dimensions={0}, use_global_device_ids=true | all-gather | bytes 20736 | tf_op jit(solution)/shard_map/all_gather | solution.py:664
  99.3 13.2 %collective-permute-start.25 = (bf16[1,256,2304]{2,1,0:T(8,128)(2,1)S(1)}, bf16[1,256,2304]{2,1,0:T(8,128)(2,1)S(1)}, u32[]{:S(2)}, u32[]{:S(2)}) collective-permute-start(bf16[1,256,2304]{2,1,0:T(8,128)(2,1)S(1)} %collective-permute-done.21.refs_8_.refs_11_), channel_id=1, source_target_pairs={{0,1},{1,0},{2,3},{3,2},{4,5},{5,4},{6,7},{7,6},{8,9},{9,8},{10,11... | collective-permute-start | bytes 3538952 | tf_op jit(solution)/shard_map/ppermute | solution.py:462
  137.6 39.9 %all-gather.14.cloned.1.call-done = bf16[32,2,64,512]{3,2,1,0:T(8,128)(2,1)} async-done(((bf16[4,2,64,512]{3,2,1,0:T(8,128)(2,1)}), bf16[32,2,64,512]{3,2,1,0:T(8,128)(2,1)}) %all-gather.14.cloned.1.call-update) | async-done | bytes 4194320 | tf_op jit(solution)/shard_map/all_gather | solution.py:689
  177.5 15.8 %attend.1 = (bf16[4,2,64,512]{3,2,1,0:T(8,128)(2,1)}, f32[4,2,128,128]{3,2,1,0:T(8,128)}) custom-call(s32[1]{0:T(128)} %bitcast.78.shard_ref, bf16[4,2,64,512]{3,2,1,0:T(8,128)(2,1)S(1)} %get-tuple-element.838.q_ref, bf16[8,4,2,64,512]{4,3,2,1,0:T(8,128)(2,1)} %bitcast.308), custom_call_target="tpu_custom_call" | custom-call | tf_op jit(solution)/shard_map/attend/pallas_call | solution.py:167
  251.9 16.6 %collective-permute-done.33.refs_9_ = bf16[2,128,2304]{2,1,0:T(8,128)(2,1)} collective-permute-done((bf16[2,128,2304]{2,1,0:T(8,128)(2,1)}, bf16[2,128,2304]{2,1,0:T(8,128)(2,1)}, u32[]{:S(2)}, u32[]{:S(2)}) %collective-permute-start.33) | collective-permute-done | bytes 1179680 | tf_op jit(solution)/shard_map/ppermute | solution.py:620
  286.7 33.0 %all-gather.8.cloned.1.call-done = bf16[1024,2304]{1,0:T(8,128)(2,1)} async-done(((bf16[128,2304]{1,0:T(8,128)(2,1)}), bf16[1024,2304]{1,0:T(8,128)(2,1)}) %all-gather.8.cloned.1.call-update) | async-done | bytes 4718608 | tf_op jit(solution)/shard_map/all_gather | solution.py:718
  319.7 16.6 %fusion.19 = f32[1024,2,1152]{2,0,1:T(8,128)S(1)} fusion(bf16[1152,3,2304]{2,0,1:T(8,128)(2,1)} %param.27, bf16[1024,2304]{1,0:T(8,128)(2,1)} %all-gather.8.cloned.1.call-done), kind=kOutput, calls=%fused_computation.83 | convolution fusion | flops 10871635968 | bytes 24772608 | tf_op jit(solution)/shard_map/td,fgd->tgf/dot_general | solution.py:724
  351.6 16.5 %collective-permute-done.39.refs_11_ = bf16[2,128,2304]{2,1,0:T(8,128)(2,1)S(1)} collective-permute-done((bf16[2,128,2304]{2,1,0:T(8,128)(2,1)}, bf16[2,128,2304]{2,1,0:T(8,128)(2,1)S(1)}, u32[]{:S(2)}, u32[]{:S(2)}) %collective-permute-start.39) | collective-permute-done | bytes 1179680 | tf_op jit(solution)/shard_map/ppermute | solution.py:626
  381.8 14.4 %pick.10 = bf16[32,128,2304]{2,1,0:T(8,128)(2,1)} custom-call(s32[32]{0:T(128)} %get-tuple-element.851.which_ref, s32[32]{0:T(128)} %get-tuple-element.850.slot_ref, bf16[8,128,2304]{2,1,0:T(8,128)(2,1)} %bitcast.307, bf16[2,128,2304]{2,1,0:T(8,128)(2,1)} %collective-permute-done.32.refs_1_, bf16[2,128,2304]{2,1,0:T(8,128)(2,1)} %copy-done.33, ...), custom_call_target="tpu_custom_call" | custom-call | tf_op jit(solution)/shard_map/pick/pallas_call | solution.py:384
  396.2 25.8 %reduce-scatter.2.cloned.1.call-done = bf16[128,2304]{1,0:T(8,128)(2,1)} async-done(((bf16[1024,2304]{1,0:T(8,128)(2,1)}), bf16[128,2304]{1,0:T(8,128)(2,1)}) %reduce-scatter.2.cloned.1.call-update) | async-done | bytes 589840 | tf_op jit(solution)/shard_map/reduce_scatter | solution.py:732
  429.4 12.4 %collective-permute-done.47.refs_3_ = bf16[1,128,2304]{2,1,0:T(8,128)(2,1)S(1)} collective-permute-done((bf16[1,128,2304]{2,1,0:T(8,128)(2,1)}, bf16[1,128,2304]{2,1,0:T(8,128)(2,1)S(1)}, u32[]{:S(2)}, u32[]{:S(2)}) %collective-permute-start.47) | collective-permute-done | bytes 589856 | tf_op jit(solution)/shard_map/ppermute | solution.py:626
  464.3 11.2 %all-gather.10.cloned.1.call-done = bf16[1024,2304]{1,0:T(8,128)(2,1)} async-done(((bf16[128,2304]{1,0:T(8,128)(2,1)}), bf16[1024,2304]{1,0:T(8,128)(2,1)}) %all-gather.10.cloned.1.call-update) | async-done | bytes 4718608 | tf_op jit(solution)/shard_map/all_gather | solution.py:743
  492.6 12.4 %fusion.42 = (bf16[1024,1,1152]{2,0,1:T(8,128)(2,1)S(1)}, bf16[1024,1,1152]{2,0,1:T(8,128)(2,1)S(1)}) fusion(f32[1024,2,1152]{2,0,1:T(8,128)S(1)} %bitcast.320, bf16[1024,2304]{1,0:T(8,128)(2,1)} %all-gather.10.cloned.1.call-done, bf16[1152,3,2304]{2,0,1:T(8,128)(2,1)} %param.27), kind=kOutput, calls=%fused_computation.113 | convolution fusion | flops 5464129536 | bytes 24182784 | tf_op jit(solution)/shard_map/dot_general | solution.py:44
  535.5 307.4 %conditional.1 = (bf16[768,2304]{1,0:T(8,128)(2,1)}, f32[4,2304]{1,0:T(4,128)}, f32[2,64,2304]{2,1,0:T(8,128)}) conditional(s32[]{:T(128)} %convert_element_type.296, () %tuple.55, (s32[]{:T(128)}, f32[128,2304]{1,0:T(8,128)S(1)}, f32[128,2304]{1,0:T(8,128)S(1)}, bf16[1152,3,2304]{2,0,1:T(8,128)(2,1)}, bf16[1024,2,1152]{2,0,1:T(8,128)(2,1)}, ...), branch_computations={%region_8.9_spmd, %region_9.19_spmd} | conditional | flops 21785825280 | bytes 354714720 | solution.py:859
  535.5 14.9 %bitcast_convert_fusion = bf16[1024,2304]{1,0:T(8,128)(2,1)S(1)} fusion(bf16[1024,2,1152]{2,0,1:T(8,128)(2,1)} %get-tuple-element.46, bf16[1152,3,2304]{2,0,1:T(8,128)(2,1)} %get-tuple-element.47), kind=kOutput, calls=%fused_computation.2 | convolution fusion | flops 10873995264 | bytes 20054016 | tf_op jit(solution)/shard_map/cond/branch_1_fun/tgf,fgd->td/dot_general | solution.py:777
  601.6 13.7 %collective-permute-done.3 = bf16[128,2304]{1,0:T(8,128)(2,1)S(1)} collective-permute-done((bf16[128,2304]{1,0:T(8,128)(2,1)S(1)}, bf16[128,2304]{1,0:T(8,128)(2,1)S(1)}, u32[]{:S(2)}, u32[]{:S(2)}) %collective-permute-start.3) | collective-permute-done | bytes 589856 | tf_op jit(solution)/shard_map/cond/branch_1_fun/ppermute | solution.py:565
  648.5 22.1 %attend_back.1 = (bf16[4,2,64,512]{3,2,1,0:T(8,128)(2,1)}, bf16[8,4,2,64,512]{4,3,2,1,0:T(8,128)(2,1)}) custom-call(s32[1]{0:T(128)} %get-tuple-element.41.shard_ref, bf16[4,2,64,512]{3,2,1,0:T(8,128)(2,1)S(1)} %copy-done.25, bf16[4,2,64,512]{3,2,1,0:T(8,128)(2,1)} %copy-done.30, f32[4,2,128,128]{3,2,1,0:T(8,128)} %get-tuple-element.51.lse_ref, ...), custom_call_target="tpu_custom_call" | custom-call | tf_op jit(solution)/shard_map/cond/branch_1_fun/attend_back/pallas_call | solution.py:198
  689.9 11.2 %collective-permute-done.9 = bf16[128,2304]{1,0:T(8,128)(2,1)S(1)} collective-permute-done((bf16[128,2304]{1,0:T(8,128)(2,1)S(1)}, bf16[128,2304]{1,0:T(8,128)(2,1)S(1)}, u32[]{:S(2)}, u32[]{:S(2)}) %collective-permute-start.9) | collective-permute-done | bytes 589856 | tf_op jit(solution)/shard_map/cond/branch_1_fun/ppermute | solution.py:539
  713.0 12.4 %collective-permute-done.12 = bf16[512,512]{1,0:T(8,128)(2,1)S(1)} collective-permute-done((bf16[512,512]{1,0:T(8,128)(2,1)S(1)}, bf16[512,512]{1,0:T(8,128)(2,1)S(1)}, u32[]{:S(2)}, u32[]{:S(2)}) %collective-permute-start.12) | collective-permute-done | bytes 524320 | tf_op jit(solution)/shard_map/cond/branch_1_fun/ppermute | solution.py:565
  727.7 12.3 %collective-permute-done.13 = bf16[512,512]{1,0:T(8,128)(2,1)S(1)} collective-permute-done((bf16[512,512]{1,0:T(8,128)(2,1)S(1)}, bf16[512,512]{1,0:T(8,128)(2,1)S(1)}, u32[]{:S(2)}, u32[]{:S(2)}) %collective-permute-start.13) | collective-permute-done | bytes 524320 | tf_op jit(solution)/shard_map/cond/branch_1_fun/ppermute | solution.py:565
  742.3 11.2 %collective-permute-done.14 = bf16[512,512]{1,0:T(8,128)(2,1)S(1)} collective-permute-done((bf16[512,512]{1,0:T(8,128)(2,1)S(1)}, bf16[512,512]{1,0:T(8,128)(2,1)S(1)}, u32[]{:S(2)}, u32[]{:S(2)}) %collective-permute-start.14) | collective-permute-done | bytes 524320 | tf_op jit(solution)/shard_map/cond/branch_1_fun/ppermute | solution.py:565
  760.3 23.1 %all-to-all-done.1 = bf16[4,2,64,1024]{3,2,1,0:T(8,128)(2,1)S(1)} async-done(((bf16[4,2,64,1024]{3,2,1,0:T(8,128)(2,1)}), bf16[4,2,64,1024]{3,2,1,0:T(8,128)(2,1)S(1)}, u32[]{:S(2)}, u32[]{:S(2)}) %all-to-all-start.1) | async-done | bytes 1048608 | tf_op jit(solution)/shard_map/cond/branch_1_fun/all_to_all | solution.py:803
  803.0 25.8 %all-to-all-done.2 = bf16[8,128,768]{1,2,0:T(8,128)(2,1)} async-done(((bf16[8,128,768]{1,2,0:T(8,128)(2,1)}), bf16[8,128,768]{1,2,0:T(8,128)(2,1)}, u32[]{:S(2)}, u32[]{:S(2)}) %all-to-all-start.2) | async-done | bytes 1572896 | tf_op jit(solution)/shard_map/cond/branch_1_fun/all_to_all | solution.py:831
  881.4 57.0 %all-reduce.4.cloned.1.call-done = bf16[768,2304]{1,0:T(8,128)(2,1)} async-done(((bf16[768,2304]{1,0:T(8,128)(2,1)}), bf16[768,2304]{1,0:T(8,128)(2,1)}) %all-reduce.4.cloned.1.call-update) | async-done | bytes 3538960 | tf_op jit(solution)/shard_map/psum | solution.py:865
  (445 shorter events, 460.4 us)
Async XLA Ops:
  7.2 68.7 %all-gather.12.cloned.1.call-start = ((), (), s32[]{:S(2)}) async-start(), calls=%async_computation.9 | async-start | bytes 2949120 | tf_op jit(solution)/shard_map/all_gather | solution.py:663
  24.2 153.4 %all-gather.14.cloned.1.call-start = ((), (), s32[]{:S(2)}) async-start(), calls=%async_computation.10 | async-start | bytes 4718592 | tf_op jit(solution)/shard_map/all_gather | solution.py:689
  41.0 30.1 %collective-permute-start.17 = (bf16[1,256,2304]{2,1,0:T(8,128)(2,1)}, bf16[1,256,2304]{2,1,0:T(8,128)(2,1)S(1)}, u32[]{:S(2)}, u32[]{:S(2)}) collective-permute-start(bf16[1,256,2304]{2,1,0:T(8,128)(2,1)} %slice_select_fusion.3), channel_id=1, source_target_pairs={{0,2},{2,4},{3,1},{4,6},{5,3},{8,10},{10,12},{11,9},{12,14},{13,11... | collective-permute-start | bytes 3538952 | tf_op jit(solution)/shard_map/ppermute | solution.py:451
  45.3 25.7 %collective-permute-start.18 = (bf16[1,256,2304]{2,1,0:T(8,128)(2,1)S(1)}, bf16[1,256,2304]{2,1,0:T(8,128)(2,1)S(1)}, u32[]{:S(2)}, u32[]{:S(2)}) collective-permute-start(bf16[1,256,2304]{2,1,0:T(8,128)(2,1)S(1)} %collective-permute-done.16.refs_2_.refs_9_), channel_id=1, source_target_pairs={{0,1},{1,0},{2,3},{3,2},{4,5},{5,4},{6,7},{7,6},{8,9},{9,8},{10,11... | collective-permute-start | bytes 3538952 | tf_op jit(solution)/shard_map/ppermute | solution.py:462
  128.3 191.4 %all-gather.8.cloned.1.call-start = ((), (), s32[]{:S(2)}) async-start(), calls=%async_computation.5 | async-start | bytes 5308416 | tf_op jit(solution)/shard_map/all_gather | solution.py:718
  128.4 67.0 %collective-permute-start.23 = (bf16[1,256,2304]{2,1,0:T(8,128)(2,1)}, bf16[1,256,2304]{2,1,0:T(8,128)(2,1)S(1)}, u32[]{:S(2)}, u32[]{:S(2)}) collective-permute-start(bf16[1,256,2304]{2,1,0:T(8,128)(2,1)} %get-tuple-element.819), channel_id=1, source_target_pairs={{4,6},{27,25}} | collective-permute-start | bytes 3538952 | tf_op jit(solution)/shard_map/ppermute | solution.py:451
  129.1 66.2 %collective-permute-start.24 = (bf16[1,256,2304]{2,1,0:T(8,128)(2,1)}, bf16[1,256,2304]{2,1,0:T(8,128)(2,1)S(1)}, u32[]{:S(2)}, u32[]{:S(2)}) collective-permute-start(bf16[1,256,2304]{2,1,0:T(8,128)(2,1)} %get-tuple-element.835), channel_id=1, source_target_pairs={{4,6},{27,25}} | collective-permute-start | bytes 3538952 | tf_op jit(solution)/shard_map/ppermute | solution.py:451
  236.9 31.6 %collective-permute-start.33 = (bf16[2,128,2304]{2,1,0:T(8,128)(2,1)}, bf16[2,128,2304]{2,1,0:T(8,128)(2,1)}, u32[]{:S(2)}, u32[]{:S(2)}) collective-permute-start(bf16[2,128,2304]{2,1,0:T(8,128)(2,1)} %get-tuple-element.220), channel_id=1, source_target_pairs={{0,16},{8,24},{16,0},{24,8},{1,17},{9,25},{17,1},{25,9},{2,18},{10... | collective-permute-start | bytes 3538952 | tf_op jit(solution)/shard_map/ppermute | solution.py:620
  237.2 32.5 %collective-permute-start.32 = (bf16[2,128,2304]{2,1,0:T(8,128)(2,1)}, bf16[2,128,2304]{2,1,0:T(8,128)(2,1)}, u32[]{:S(2)}, u32[]{:S(2)}) collective-permute-start(bf16[2,128,2304]{2,1,0:T(8,128)(2,1)} %get-tuple-element.218), channel_id=1, source_target_pairs={{0,8},{8,0},{16,24},{24,16},{1,9},{9,1},{17,25},{25,17},{2,10},{10... | collective-permute-start | bytes 3538952 | tf_op jit(solution)/shard_map/ppermute | solution.py:620
  273.2 148.9 %reduce-scatter.2.cloned.1.call-start = ((), (), s32[]{:S(2)}) async-start(), calls=%async_computation.6 | async-start | bytes 5308416 | tf_op jit(solution)/shard_map/reduce_scatter | solution.py:732
  273.4 78.2 %collective-permute-start.36 = (bf16[2,128,2304]{2,1,0:T(8,128)(2,1)}, bf16[2,128,2304]{2,1,0:T(8,128)(2,1)}, u32[]{:S(2)}, u32[]{:S(2)}) collective-permute-start(bf16[2,128,2304]{2,1,0:T(8,128)(2,1)} %get-tuple-element.218), channel_id=1, source_target_pairs={{0,16},{8,24},{16,0},{24,8},{1,17},{9,25},{17,1},{25,9},{2,18},{10... | collective-permute-start | bytes 3538952 | tf_op jit(solution)/shard_map/ppermute | solution.py:626
  275.4 76.2 %collective-permute-start.38 = (bf16[2,128,2304]{2,1,0:T(8,128)(2,1)}, bf16[2,128,2304]{2,1,0:T(8,128)(2,1)}, u32[]{:S(2)}, u32[]{:S(2)}) collective-permute-start(bf16[2,128,2304]{2,1,0:T(8,128)(2,1)} %get-tuple-element.220), channel_id=1, source_target_pairs={{0,8},{8,0},{16,24},{24,16},{1,9},{9,1},{17,25},{25,17},{2,10},{10... | collective-permute-start | bytes 3538952 | tf_op jit(solution)/shard_map/ppermute | solution.py:626
  282.7 57.1 %collective-permute-start.35 = (bf16[1,128,2304]{2,1,0:T(8,128)(2,1)}, bf16[1,128,2304]{2,1,0:T(8,128)(2,1)}, u32[]{:S(2)}, u32[]{:S(2)}) collective-permute-start(bf16[1,128,2304]{2,1,0:T(8,128)(2,1)} %get-tuple-element.230), channel_id=1, source_target_pairs={{0,16},{8,24},{16,0},{24,8},{1,17},{9,25},{17,1},{25,9},{2,18},{10... | collective-permute-start | bytes 1769480 | tf_op jit(solution)/shard_map/ppermute | solution.py:620
  283.3 57.9 %collective-permute-start.34 = (bf16[1,128,2304]{2,1,0:T(8,128)(2,1)}, bf16[1,128,2304]{2,1,0:T(8,128)(2,1)}, u32[]{:S(2)}, u32[]{:S(2)}) collective-permute-start(bf16[1,128,2304]{2,1,0:T(8,128)(2,1)} %get-tuple-element.229), channel_id=1, source_target_pairs={{0,8},{8,0},{16,24},{24,16},{1,9},{9,1},{17,25},{25,17},{2,10},{10... | collective-permute-start | bytes 1769480 | tf_op jit(solution)/shard_map/ppermute | solution.py:620
  283.4 68.2 %collective-permute-start.37 = (bf16[2,128,2304]{2,1,0:T(8,128)(2,1)}, bf16[2,128,2304]{2,1,0:T(8,128)(2,1)}, u32[]{:S(2)}, u32[]{:S(2)}) collective-permute-start(bf16[2,128,2304]{2,1,0:T(8,128)(2,1)} %collective-permute-done.32.refs_1_), channel_id=1, source_target_pairs={{0,16},{8,24},{16,0},{24,8},{1,17},{9,25},{17,1},{25,9},{2,18},{10... | collective-permute-start | bytes 3538952 | tf_op jit(solution)/shard_map/ppermute | solution.py:626
  339.8 28.3 %collective-permute-start.39 = (bf16[2,128,2304]{2,1,0:T(8,128)(2,1)}, bf16[2,128,2304]{2,1,0:T(8,128)(2,1)S(1)}, u32[]{:S(2)}, u32[]{:S(2)}) collective-permute-start(bf16[2,128,2304]{2,1,0:T(8,128)(2,1)} %collective-permute-done.33.refs_9_), channel_id=1, source_target_pairs={{0,8},{8,0},{16,24},{24,16},{1,9},{9,1},{17,25},{25,17},{2,10},{10... | collective-permute-start | bytes 3538952 | tf_op jit(solution)/shard_map/ppermute | solution.py:626
  368.1 107.4 %all-gather.10.cloned.1.call-start = ((), (), s32[]{:S(2)}) async-start(), calls=%async_computation.7 | async-start | bytes 5308416 | tf_op jit(solution)/shard_map/all_gather | solution.py:743
  425.2 417.7 %all-reduce.6.cloned.1.call-start = ((), (), s32[]{:S(2)}) async-start(), calls=%async_computation.11 | async-start | bytes 31850496 | tf_op jit(solution)/shard_map/psum | solution.py:774
  428.9 23.5 %collective-permute-start.54 = (bf16[1,128,2304]{2,1,0:T(8,128)(2,1)}, bf16[1,128,2304]{2,1,0:T(8,128)(2,1)S(1)}, u32[]{:S(2)}, u32[]{:S(2)}) collective-permute-start(bf16[1,128,2304]{2,1,0:T(8,128)(2,1)} %collective-permute-done.35.refs_9_), channel_id=1, source_target_pairs={{0,8},{8,0},{16,24},{24,16},{1,9},{9,1},{17,25},{25,17},{2,10},{10... | collective-permute-start | bytes 1769480 | tf_op jit(solution)/shard_map/ppermute | solution.py:626
  525.7 412.7 %all-reduce.4.cloned.1.call-start = ((), (), s32[]{:S(2)}) async-start(), calls=%async_computation.8 | async-start | bytes 7077888 | tf_op jit(solution)/shard_map/psum | solution.py:865
  623.8 49.7 %collective-permute-start.4 = (bf16[128,2304]{1,0:T(8,128)(2,1)S(1)}, bf16[128,2304]{1,0:T(8,128)(2,1)}, u32[]{:S(2)}, u32[]{:S(2)}) collective-permute-start(bf16[128,2304]{1,0:T(8,128)(2,1)S(1)} %get-tuple-element.790), channel_id=1, source_target_pairs={{0,1},{1,0},{2,3},{3,2},{4,5},{5,4},{6,7},{7,6},{8,9},{9,8},{10,11... | collective-permute-start | bytes 1769480 | tf_op jit(solution)/shard_map/cond/branch_1_fun/ppermute | solution.py:541
  623.8 46.8 %collective-permute-start.5 = (bf16[128,2304]{1,0:T(8,128)(2,1)S(1)}, bf16[128,2304]{1,0:T(8,128)(2,1)S(1)}, u32[]{:S(2)}, u32[]{:S(2)}) collective-permute-start(bf16[128,2304]{1,0:T(8,128)(2,1)S(1)} %get-tuple-element.790), channel_id=1, source_target_pairs={{0,2},{1,3},{2,6},{3,7},{4,0},{5,1},{6,4},{7,5},{8,10},{9,11},{10,... | collective-permute-start | bytes 1769480 | tf_op jit(solution)/shard_map/cond/branch_1_fun/ppermute | solution.py:539
  754.8 28.6 %all-to-all-start.1 = ((bf16[4,2,64,1024]{3,2,1,0:T(8,128)(2,1)}), bf16[4,2,64,1024]{3,2,1,0:T(8,128)(2,1)S(1)}, u32[]{:S(2)}, u32[]{:S(2)}) async-start(bf16[4,2,64,1024]{3,2,1,0:T(8,128)(2,1)} %pad_maximum_fusion.1), calls=%async_computation.1 | async-start | bytes 2097152 | tf_op jit(solution)/shard_map/cond/branch_1_fun/all_to_all | solution.py:803
  786.5 42.3 %all-to-all-start.2 = ((bf16[8,128,768]{1,2,0:T(8,128)(2,1)}), bf16[8,128,768]{1,2,0:T(8,128)(2,1)}, u32[]{:S(2)}, u32[]{:S(2)}) async-start(bf16[8,128,768]{1,2,0:T(8,128)(2,1)} %bitcast.323), calls=%async_computation.2 | async-start | bytes 3145728 | tf_op jit(solution)/shard_map/cond/branch_1_fun/all_to_all | solution.py:831
  (129 other events, 1259.4 us)
Sparse Core Ops, SparseCore 0:
  24.3 37.6 all-gather.11
  128.4 49.0 all-gather.13
  269.8 49.8 all-gather.7
  368.2 53.7 reduce-scatter.1
  425.3 50.0 all-gather.9
  525.8 313.0 all-reduce.5
  843.1 95.2 all-reduce.3

commit v3 on v2

--- a/solution.py
+++ b/solution.py
@@ -256,10 +256,11 @@
 def route(columns, chips, per_chip):
     items = len(granules_of(0, columns))
     urgent = items - HQ // columns
+    rank = [1] * (urgent - 2) + [0] * 2 + [2] * (items - urgent)
     source = [[g // per_chip for g in granules_of(c, columns)] for c in range(columns)]
     held = [[{k for k in range(items) if source[c][k] == z} for z in range(chips)] for c in range(columns)]
     steps = []
-    urgent_steps = None
+    urgent_steps = kv_steps = None
     while any(len(held[c][z]) < items for c in range(columns) for z in range(chips)):
         moves = {}
         for c in range(columns):
@@ -274,7 +275,7 @@
                     ]
                     if ready:
                         moves[c, z, core] = min(
-                            ready, key=lambda k: (k >= urgent, abs(source[c][k] - z), k)
+                            ready, key=lambda k: (rank[k], abs(source[c][k] - z), k)
                         )
         for (c, z, core), k in moves.items():
             held[c][z + (1, -1)[core]].add(k)
@@ -282,7 +283,15 @@
         done = all(k in held[c][z] for c in range(columns) for z in range(chips) for k in range(urgent))
         if done and urgent_steps is None:
             urgent_steps = len(steps)
-    return steps, urgent_steps
+        done = all(
+            k in held[c][z]
+            for c in range(columns)
+            for z in range(chips)
+            for k in (urgent - 2, urgent - 1)
+        )
+        if done and kv_steps is None:
+            kv_steps = len(steps)
+    return steps, urgent_steps, kv_steps
 
 
 def chosen(places, devices):
@@ -405,7 +414,7 @@
     swap = [(f, f ^ 1) for f in range(shards)]
     items = len(granules_of(0, columns))
     urgent = items - HQ // columns
-    steps, urgent_steps = route(columns, chips, 2 * count)
+    steps, urgent_steps, kv_steps = route(columns, chips, 2 * count)
     mine = attn_weight.reshape(count, HD, width)
     theirs = between("start", lax.ppermute(mine, "fsdp", swap))
     sources = {"mine": mine, "theirs": theirs}
@@ -460,12 +469,19 @@
         sources["got%d" % number] = got
         if number < urgent_steps:
             sources["swapped%d" % number] = lax.ppermute(got, "fsdp", swap)
-        if number + 1 == urgent_steps:
-            ready = dict(sources)
-            made = between(
-                None,
-                lambda times: pick(at[:urgent], ready, device, devices, "project", times),
-            )
+        for name, wanted, count_of in (
+            ("kv", (urgent - 2, urgent), kv_steps),
+            ("q", (0, urgent - 2), urgent_steps),
+        ):
+            if number + 1 == count_of:
+                ready = dict(sources)
+                places = [dict(place) for place in at[slice(*wanted)]]
+                between(
+                    name,
+                    lambda times, ready=ready, places=places: pick(
+                        places, ready, device, devices, "project", times
+                    ),
+                )
 
     def first(after):
         held, after = lax.optimization_barrier((ready, after))
@@ -484,7 +500,7 @@
         kept, after = lax.optimization_barrier((held, after))
         return pick(at[urgent:], kept, device, devices)
 
-    return made, first, times_rest, others
+    return first, times_rest, others
 
 
 def column_weights(attn_weight, column, shard, columns, shards, between):
@@ -498,11 +514,14 @@
     taken = jnp.concatenate(
         [lax.dynamic_slice_in_dim(whole, place[k], 1, 0) for k in range(table.shape[1])], axis=0
     )
-    made = between(
-        None, lambda times: dot_nt(times, taken[: per + 2].reshape(-1, width)).astype(bf16)
-    )
+    for name, low, high in (("kv", per, per + 2), ("q", 0, per)):
+        between(
+            name,
+            lambda times, low=low, high=high: dot_nt(
+                times, taken[low:high].reshape(-1, width)
+            ).astype(bf16),
+        )
     return (
-        made,
         lambda after: taken[: per + 2],
         lambda rows_in: dot_nn(rows_in, taken[per + 2 :].reshape(-1, width)).astype(bf16),
         lambda after: taken[per + 2 :],
@@ -527,21 +546,96 @@
     return chips, pairs, behind
 
 
-def ring_gather(block, shard, shards, beside=None):
+def ring_pieces(block, shard, shards, beside):
     chips, pairs, behind = ring_tables(shards)
     swap = [(f, f ^ 1) for f in range(shards)]
     source = jnp.asarray(behind)[shard]
     core = shard % 2
-    out = jnp.zeros((shards,) + block.shape, block.dtype)
+    pieces = []
     held = block
     for t in range(chips):
         if t:
             held = lax.ppermute(held, "fsdp", pairs)
-            held = beside(t, held) if beside else held
-        other = lax.ppermute(held, "fsdp", swap)
-        out = lax.dynamic_update_index_in_dim(out, held, 2 * source[t] + core, 0)
-        out = lax.dynamic_update_index_in_dim(out, other, 2 * source[t] + 1 - core, 0)
-    return out
+            held = beside(t, held)
+        pieces.append((held, 2 * source[t] + core))
+        pieces.append((lax.ppermute(held, "fsdp", swap), 2 * source[t] + 1 - core))
+    return pieces
+
+
+def direct_pieces(block, shard, shards):
+    chips = shards // 2
+    swap = [(f, f ^ 1) for f in range(shards)]
+    core = shard % 2
+    come = [block] + [
+        lax.ppermute(block, "fsdp", [(f, (f + 2 * hop) % shards) for f in range(shards)])
+        for hop in range(1, chips)
+    ]
+
+    def finish(after):
+        held, after = lax.optimization_barrier((come, after))
+        pieces = []
+        for hop, piece in enumerate(held):
+            chip = (shard // 2 - hop) % chips
+            pieces.append((piece, 2 * chip + core))
+            pieces.append((lax.ppermute(piece, "fsdp", swap), 2 * chip + 1 - core))
+        return pieces, after
+
+    return finish
+
+
+def weight_grad_kernel(half, place_ref, cols_ref, *refs):
+    pieces = refs[: 2 * half]
+    out_ref, rows_ref, turned_ref, sems = refs[2 * half :]
+    lines = pieces[0].shape[0]
+    for i, piece in enumerate(pieces):
+        start = pl.multiple_of(place_ref[i] * lines, lines)
+        pltpu.make_async_copy(
+            piece, rows_ref.at[i // half, pl.ds(start, lines)], sems.at[i]
+        ).start()
+    limit = place_ref[2 * half]
+    turned = cols_ref[...].T
+    col = lax.broadcasted_iota(jnp.int32, turned.shape, 0)
+    turned_ref[0] = jnp.where(col < limit, turned, 0)
+    turned_ref[1] = jnp.where(col < limit, 0, turned)
+    for i, piece in enumerate(pieces):
+        pltpu.make_async_copy(piece, rows_ref.at[0, pl.ds(0, lines)], sems.at[i]).wait()
+    width = out_ref.shape[1]
+    step = width // 3 if width % 384 == 0 else width
+
+    def chunk(n, carry):
+        cut = pl.ds(pl.multiple_of(n * step, step), step)
+        total = dot_nn(turned_ref[0], rows_ref[0, :, cut])
+        total += dot_nn(turned_ref[1], rows_ref[1, :, cut])
+        out_ref[:, cut] = total.astype(bf16)
+        return carry
+
+    lax.fori_loop(0, width // step, chunk, 0)
+
+
+def weight_grad(cols, limit, first, second):
+    lines, width = first[0][0].shape
+    half = len(first)
+    place = jnp.stack(
+        [where.astype(jnp.int32) for _, where in first + second] + [limit.astype(jnp.int32)]
+    )
+    return pl.pallas_call(
+        functools.partial(weight_grad_kernel, half),
+        grid_spec=pltpu.PrefetchScalarGridSpec(
+            num_scalar_prefetch=1,
+            grid=(1,),
+            in_specs=[pl.BlockSpec(memory_space=pltpu.VMEM)]
+            + [pl.BlockSpec(memory_space=pl.ANY)] * (2 * half),
+            out_specs=pl.BlockSpec(memory_space=pltpu.VMEM),
+            scratch_shapes=[
+                pltpu.VMEM((2, half * lines, width), bf16),
+                pltpu.VMEM((2, cols.shape[1], cols.shape[0]), bf16),
+                pltpu.SemaphoreType.DMA((2 * half,)),
+            ],
+        ),
+        out_shape=jax.ShapeDtypeStruct((cols.shape[1], width), bf16),
+        compiler_params=pltpu.CompilerParams(vmem_limit_bytes=58 * 2**20),
+        name="weight_grad",
+    )(place, cols, *[piece for piece, _ in first + second])
 
 
 def ring_scatter(parts, shard, shards):
@@ -662,32 +756,32 @@
 
     token_slices = lax.all_gather(tokens, "seq", axis=0)
     gain_rows = lax.all_gather(norm_gains, "fsdp", axis=1, tiled=True).astype(f32)
-    normed_slices = None
+    normed_slices = rms_scale(
+        token_slices.reshape(-1, width).astype(f32), gain_rows[0]
+    ).astype(bf16)
+    made = {}
 
     def between(step, value):
-        nonlocal gain_rows, normed_slices
-        if step == 1:
+        nonlocal normed_slices, gain_rows
+        if step == "start":
             value, gain_rows = lax.optimization_barrier((value, gain_rows))
             normed_slices = rms_scale(
                 token_slices.reshape(-1, width).astype(f32), gain_rows[0]
             ).astype(bf16)
+        if step == 1:
+            value, normed_slices = lax.optimization_barrier((value, normed_slices))
         if step == 2:
-            value, normed_slices = lax.optimization_barrier((value, normed_slices))
-        if step is None:
-            if normed_slices is None:
-                normed_slices = rms_scale(
-                    token_slices.reshape(-1, width).astype(f32), gain_rows[0]
-                ).astype(bf16)
-            return value(normed_slices)
+            value, made["kv"] = lax.optimization_barrier((value, made["kv"]))
+        if step in ("kv", "q"):
+            made[step] = value(normed_slices)
         return value
 
-    heads, first_weights, times_out, out_weights = column_weights(
+    first_weights, times_out, out_weights = column_weights(
         attn_weight, column, shard, columns, shards, between
     )
-    heads = heads.reshape(columns, seqs, rows, (per + 2) * HD)
-    queries = heads[..., : per * HD]
-    kv_all = lax.all_gather(heads[..., per * HD :], "fsdp", axis=0)
-    weight_in = first_weights(heads)
+    kv_all = lax.all_gather(made["kv"].reshape(columns, seqs, rows, 2 * HD), "fsdp", axis=0)
+    queries = made["q"].reshape(columns, seqs, rows, per * HD)
+    weight_in = first_weights(queries)
     if columns == 4:
         in_lanes, in_near = round_start(weight_in)
         kv_all, in_lanes = lax.optimization_barrier((kv_all, in_lanes))
@@ -710,9 +804,6 @@
     residual = flat_tokens + rms_scale(attn_out, gain_rows[1])
     normed_ffn = rms_scale(residual, gain_rows[2]).astype(bf16)
 
-    if columns == 4:
-        normed_ffn, in_near = lax.optimization_barrier((normed_ffn, in_near))
-        in_far = round_on(in_lanes, in_near)
     mixed_later, normed_ffn = lax.optimization_barrier((mixed, normed_ffn))
     weight_out = out_weights(normed_ffn)
     ffn_in = lax.all_gather(normed_ffn, "fsdp", axis=0, tiled=True)
@@ -720,19 +811,18 @@
     mixed_rows = mixed_rows.transpose(1, 2, 0, 3).reshape(own_rows, HQ * HD)
     if columns == 4:
         out_lanes, out_near = round_start(weight_out)
-        ffn_in, out_lanes, mixed_rows = lax.optimization_barrier((ffn_in, out_lanes, mixed_rows))
+        ffn_in, out_near, in_near, mixed_rows = lax.optimization_barrier(
+            (ffn_in, out_near, in_near, mixed_rows)
+        )
+        in_far = round_on(in_lanes, in_near)
     gate_up = jnp.einsum("td,fgd->tgf", ffn_in, ffn_weight[:, :2], preferred_element_type=f32)
     hidden = gated_units(gate_up[:, 0], gate_up[:, 1]).astype(bf16)
-    if columns == 4:
-        hidden, out_near = lax.optimization_barrier((hidden, out_near))
-        out_far = round_on(out_lanes, out_near)
     branch = dot_nn(hidden, ffn_weight[:, 2]).astype(bf16)
-    if columns == 4:
-        branch, in_far = lax.optimization_barrier((branch, in_far))
     ffn_out = lax.psum_scatter(branch, "fsdp", scatter_dimension=0, tiled=True).astype(f32)
     if columns == 4:
+        ffn_out, in_far = lax.optimization_barrier((ffn_out, in_far))
+        out_far = round_on(out_lanes, out_near)
         weight_in_all = all_columns(weight_in, in_near, in_far)
-        ffn_out, weight_in_all = lax.optimization_barrier((ffn_out, weight_in_all))
     else:
         weight_in_all = lax.all_gather(weight_in, "seq", axis=0).reshape(-1, width)
         weight_out_all = lax.all_gather(weight_out, "seq", axis=0).reshape(-1, width)
@@ -743,7 +833,9 @@
     grad_ffn_all = lax.all_gather(grad_ffn.astype(bf16), "fsdp", axis=0, tiled=True)
     if columns == 4:
         weight_out_all = all_columns(weight_out, out_near, out_far)
-        grad_ffn_all, weight_out_all = lax.optimization_barrier((grad_ffn_all, weight_out_all))
+        grad_ffn_all, weight_out_all, weight_in_all = lax.optimization_barrier(
+            (grad_ffn_all, weight_out_all, weight_in_all)
+        )
 
     normed_own = rms_scale(flat_tokens, gain_rows[0]).astype(bf16)
     grad_ffn_all, normed_own = lax.optimization_barrier((grad_ffn_all, normed_own))
@@ -769,7 +861,7 @@
             )
         return held
 
-    normed_all = ring_gather(normed_own, shard, shards, beside).reshape(-1, width)
+    normed_pieces = ring_pieces(normed_own, shard, shards, beside)
     grad_gate_up = kept["units"]
     gate_grad, up_grad, down_grad = lax.psum((*kept["up"], kept["down"]), "seq")
 
@@ -792,9 +884,8 @@
         grad_heads = lax.all_to_all(
             grad_mixed.transpose(2, 0, 1, 3), "seq", split_axis=0, concat_axis=0, tiled=True
         )
-        grad_attn_all = ring_gather(grad_attn_low, shard, shards).reshape(-1, width)
+        later_pieces = direct_pieces(grad_attn_low, shard, shards)
         grad_queries, grad_kv = attend_back(shard_arg, queries, grad_heads, lse, kv_all)
-        grad_kv, grad_attn_all = lax.optimization_barrier((grad_kv, grad_attn_all))
         grad_kv_own = (
             ring_scatter(grad_kv.reshape(shards, columns * own_rows, 2 * HD), shard, shards)
             .astype(bf16)
@@ -807,6 +898,7 @@
             concat_axis=0,
             tiled=True,
         )
+        attn_pieces, grad_proj = later_pieces(grad_proj)
         grad_rows = grad_proj.reshape(columns, own_rows, (per + 2) * HD).transpose(1, 0, 2)
         grad_normed = dot_nn(grad_rows.reshape(own_rows, -1), weight_in_all)
         grad_tokens, gain_pre_attn = norm_back(flat_tokens, gain_rows[0], grad_normed)
@@ -835,10 +927,8 @@
             concat_axis=0,
             tiled=True,
         ).reshape(-1, shard_cols)
-        is_out = (shard * shard_cols + jnp.arange(shard_cols)) >= (HQ + 2 * KVH) * HD
-        attn_grad = dot_tn(jnp.where(is_out, 0, col_all), normed_all) + dot_tn(
-            jnp.where(is_out, col_all, 0), grad_attn_all
-        )
+        limit = jnp.clip((HQ + 2 * KVH) * HD - shard * shard_cols, 0, shard_cols)
+        attn_grad = weight_grad(col_all, limit, normed_pieces, attn_pieces)
         gain_grad = jnp.stack(
             [
                 jnp.sum(gain_pre_attn, axis=0),
@@ -847,7 +937,7 @@
                 gain_last,
             ]
         )
-        return attn_grad.astype(bf16), gain_grad, token_grad
+        return attn_grad, gain_grad, token_grad
 
     def nothing():
         return (

time: 962 us -> 927 us (0.964)
  waiting for transfers between devices: 443 us -> 351 us
  blocking collectives: 21.1 us -> 68.5 us
  starting transfers between devices: 96.8 us -> 121 us
  local copies, waits for them, and re-layouts: 80.8 us -> 57.4 us
  Pallas kernels: 108 us -> 128 us
    all_to_all x0 -> x2, blocking collectives: none -> 52.8 us  [the longest x1 36.3 us: local(): lax.all_to_all(mixed_later, 'seq', split_axis=0, concat_axis=0, tiled=True)]
    all_gather x1, waiting for transfers between devices: 39.9 us -> 0.01 us  [local(): lax.all_gather(made['kv'].reshape(columns, seqs, rows, 2 * HD), 'fsdp', a...]
    ppermute x4, starting transfers between devices: 23.3 us -> 54.6 us  [routed_weights(): sources['swapped%d' % number] = lax.ppermute(got, 'fsdp', swap)]
    reduce_scatter x1, waiting for transfers between devices: 25.8 us -> 49.7 us  [local(): lax.psum_scatter(branch, 'fsdp', scatter_dimension=0, tiled=True)]
    all_gather x1, waiting for transfers between devices: 33 us -> 9.76 us  [local(): ffn_in = lax.all_gather(normed_ffn, 'fsdp', axis=0, tiled=True)]
    all_to_all x1, waiting for transfers between devices: 23.1 us -> 0.01 us  [attention_back(): lax.all_to_all(jnp.concatenate([grad_queries, grad_kv_own], axis=-1), 'se...]
    dynamic_update_slice x15 -> x0, local copies, waits for them, and re-layouts: 22.8 us -> none  [the longest x8 12.3 us: ring_gather(): lax.dynamic_update_index_in_dim(out, other, 2 * source[t] + 1 - core, 0)]
    ppermute x6, waiting for transfers between devices: 59.7 us -> 77.9 us  [ring_scatter(): lax.ppermute(total.astype(bf16), 'fsdp', pairs).astype(f32)]
  transfers between devices with their start and end apart: 79 -> 77, of which waited for: 51 -> 44; matrix products, arithmetic and copies ran while one was open for 22% -> 16% of each run, Pallas kernels for 9% -> 13%
where the time goes in v3:
time: 927 us; the launch traced here: 916 us
  waiting for transfers between devices  351 us (38%)
  Pallas kernels  128 us (14%)
  starting transfers between devices  121 us (13%)
  matrix products  99 us (11%)
  blocking collectives  68.5 us (7%)
  local copies, waits for them, and re-layouts  57.4 us (6%)
  other arithmetic  55.7 us (6%)
  between operations  20.4 us (2%)
  loops' own time  15.4 us (2%)
    ppermute x6, waiting for transfers between devices, ring_scatter(): lax.ppermute(total.astype(bf16), 'fsdp', pairs).astype(f32)  77.9 us
    pallas_call x9, Pallas kernels, pick(): pl.pallas_call(functools.partial(kernel, cands), grid_spec=pltpu.Prefetch...  60.2 us
    psum x1, waiting for transfers between devices, local(): attn_total = lax.psum(attn_grad, 'seq').astype(f32)  59.6 us
    ppermute x4, starting transfers between devices, routed_weights(): sources['swapped%d' % number] = lax.ppermute(got, 'fsdp', swap)  54.6 us
    reduce_scatter x1, waiting for transfers between devices, local(): lax.psum_scatter(branch, 'fsdp', scatter_dimension=0, tiled=True)  49.7 us
    all_to_all x1, blocking collectives, local(): lax.all_to_all(mixed_later, 'seq', split_axis=0, concat_axis=0, tiled=True)  36.3 us
    ppermute x3, waiting for transfers between devices, direct_pieces(): lax.ppermute(block, 'fsdp', [(f, (f + 2 * hop) % shards) for f in range(s...  32.5 us
    dot_general x3, matrix products, dot_tn(): lax.dot_general(a, b, (((0,), (0,)), ((), ())), preferred_element_type=f32)  29 us
  transfers between devices with their start and end apart: 77, of which 44 were waited for; matrix products, arithmetic and copies ran while one was open for 16% of the time, Pallas kernels for 13%

profile of v3, /device:TPU:0, one launch (start us, length us, event | category | flops | bytes accessed | tf_op | source)
XLA Modules:
  0.0 915.7 jit_solution(7655960485593025492)
XLA Ops:
  8.0 15.7 %all-gather.1 = bf16[8,288,4]{1,2,0:T(4,128)(2,1)S(1)} all-gather(bf16[1,288,4]{1,2,0:T(4,128)(2,1)} %bitcast.336), channel_id=1, replica_groups=mesh['seq'=4,'fsdp'=8] {'fsdp'}, dimensions={0}, use_global_device_ids=true | all-gather | bytes 20736 | tf_op jit(solution)/shard_map/all_gather | solution.py:758
  101.7 47.2 %collective-permute-start.25 = (bf16[1,256,2304]{2,1,0:T(8,128)(2,1)S(1)}, bf16[1,256,2304]{2,1,0:T(8,128)(2,1)S(1)}, u32[]{:S(2)}, u32[]{:S(2)}) collective-permute-start(bf16[1,256,2304]{2,1,0:T(8,128)(2,1)S(1)} %collective-permute-done.21.refs_8_.refs_11_), channel_id=1, source_target_pairs={{0,1},{1,0},{2,3},{3,2},{4,5},{5,4},{6,7},{7,6},{8,9},{9,8},{10,11... | collective-permute-start | bytes 3538952 | tf_op jit(solution)/shard_map/ppermute | solution.py:471
  169.3 15.8 %attend.1 = (bf16[4,2,64,512]{3,2,1,0:T(8,128)(2,1)S(1)}, f32[4,2,128,128]{3,2,1,0:T(8,128)}) custom-call(s32[1]{0:T(128)} %bitcast.76.shard_ref, bf16[4,2,64,512]{3,2,1,0:T(8,128)(2,1)S(1)} %bitcast.316, bf16[8,4,2,64,512]{4,3,2,1,0:T(8,128)(2,1)} %all-gather.7.cloned.1.call-done.kv_ref), custom_call_target="tpu_custom_call" | custom-call | tf_op jit(solution)/shard_map/attend/pallas_call | solution.py:167
  202.0 13.8 %collective-permute-done.28 = bf16[2,128,1152]{2,1,0:T(8,128)(2,1)S(1)} collective-permute-done((bf16[2,128,1152]{2,1,0:T(8,128)(2,1)S(1)}, bf16[2,128,1152]{2,1,0:T(8,128)(2,1)S(1)}, u32[]{:S(2)}, u32[]{:S(2)}) %collective-permute-start.28) | collective-permute-done | bytes 589856 | tf_op jit(solution)/shard_map/ppermute | solution.py:672
  239.3 36.3 %all_to_all.18 = bf16[4,2,64,512]{3,2,1,0:T(8,128)(2,1)S(1)} all-to-all(bf16[4,2,64,512]{3,2,1,0:T(8,128)(2,1)S(1)} %get-tuple-element.258), channel_id=1, replica_groups=mesh['seq'=4,'fsdp'=8] {'seq'}, dimensions={0} | all-to-all | bytes 1048576 | tf_op jit(solution)/shard_map/all_to_all | solution.py:810
  286.8 16.6 %fusion.19 = f32[1024,2,1152]{2,0,1:T(8,128)S(1)} fusion(bf16[1152,3,2304]{2,0,1:T(8,128)(2,1)} %param.27, bf16[1024,2304]{1,0:T(8,128)(2,1)} %all-gather.9.cloned.1.call-done), kind=kOutput, calls=%fused_computation.63 | convolution fusion | flops 10871635968 | bytes 24772608 | tf_op jit(solution)/shard_map/td,fgd->tgf/dot_general | solution.py:818
  322.4 49.7 %reduce-scatter.2.cloned.1.call-done = bf16[128,2304]{1,0:T(8,128)(2,1)} async-done(((bf16[1024,2304]{1,0:T(8,128)(2,1)}), bf16[128,2304]{1,0:T(8,128)(2,1)}) %reduce-scatter.2.cloned.1.call-update) | async-done | bytes 589840 | tf_op jit(solution)/shard_map/reduce_scatter | solution.py:821
  395.0 12.5 %collective-permute-done.43.refs_5_ = bf16[1,128,2304]{2,1,0:T(8,128)(2,1)S(1)} collective-permute-done((bf16[1,128,2304]{2,1,0:T(8,128)(2,1)}, bf16[1,128,2304]{2,1,0:T(8,128)(2,1)S(1)}, u32[]{:S(2)}, u32[]{:S(2)}) %collective-permute-start.43) | collective-permute-done | bytes 589856 | tf_op jit(solution)/shard_map/ppermute | solution.py:720
  424.2 14.3 %pick.11 = bf16[32,128,2304]{2,1,0:T(8,128)(2,1)} custom-call(s32[32]{0:T(128)} %get-tuple-element.576.which_ref, s32[32]{0:T(128)} %get-tuple-element.575.slot_ref, bf16[8,128,2304]{2,1,0:T(8,128)(2,1)} %bitcast.296, bf16[2,128,2304]{2,1,0:T(8,128)(2,1)} %copy-done.30, bf16[2,128,2304]{2,1,0:T(8,128)(2,1)} %copy-done.31, ...), custom_call_target="tpu_custom_call" | custom-call | tf_op jit(solution)/shard_map/pick/pallas_call | solution.py:393
  441.1 13.9 %convolution_convert_fusion.3 = bf16[1152,2304]{1,0:T(8,128)(2,1)} fusion(bf16[1024,2304]{1,0:T(8,128)(2,1)} %all-gather.11.cloned.1.call-done, f32[1024,2,1152]{2,0,1:T(8,128)} %copy-done.58), kind=kOutput, calls=%fused_computation.57 | convolution fusion | flops 5450268672 | bytes 19464192 | tf_op jit(solution)/shard_map/dot_general | solution.py:52
  456.9 13.0 %fusion.60 = (bf16[1024,1,1152]{2,0,1:T(8,128)(2,1)S(1)}, bf16[1024,1,1152]{2,0,1:T(8,128)(2,1)S(1)}) fusion(f32[1024,2,1152]{2,0,1:T(8,128)} %copy-done.58, bf16[1024,2304]{1,0:T(8,128)(2,1)S(1)} %bitcast.340, bf16[1152,3,2304]{2,0,1:T(8,128)(2,1)} %param.27), kind=kOutput, calls=%fused_computation.109 | convolution fusion | flops 5464129536 | bytes 24182784 | tf_op jit(solution)/shard_map/dot_general | solution.py:44
  505.8 300.1 %conditional.1 = (bf16[768,2304]{1,0:T(8,128)(2,1)}, f32[4,2304]{1,0:T(4,128)S(1)}, f32[2,64,2304]{2,1,0:T(8,128)}) conditional(s32[]{:T(128)} %convert_element_type.295, () %tuple.51, (s32[]{:T(128)}, s32[]{:T(128)}, s32[]{:T(128)}, s32[]{:T(128)}, s32[]{:T(128)}, /*index=5*/s32[]{:T(128)}, s32[]{:T(128)}, s32[]{:T(128)}, s32[]{:T(128)}, ...), branch_computations={%region_8.9_spmd, %region_9.19_spmd} | conditional | flops 14532955136 | bytes 256229952 | solution.py:949
  505.8 15.3 %bitcast_convert_fusion = bf16[1024,2304]{1,0:T(8,128)(2,1)S(1)} fusion(bf16[1024,2,1152]{2,0,1:T(8,128)(2,1)} %get-tuple-element.80, bf16[1152,3,2304]{2,0,1:T(8,128)(2,1)} %get-tuple-element.81), kind=kOutput, calls=%fused_computation.2 | convolution fusion | flops 10873995264 | bytes 20054016 | tf_op jit(solution)/shard_map/cond/branch_1_fun/tgf,fgd->td/dot_general | solution.py:869
  533.0 15.1 %collective-permute-done.1 = bf16[128,2304]{1,0:T(8,128)(2,1)} collective-permute-done((bf16[128,2304]{1,0:T(8,128)(2,1)}, bf16[128,2304]{1,0:T(8,128)(2,1)}, u32[]{:S(2)}, u32[]{:S(2)}) %collective-permute-start.1) | collective-permute-done | bytes 589856 | tf_op jit(solution)/shard_map/cond/branch_1_fun/ppermute | solution.py:659
  568.4 14.6 %collective-permute-done.3 = bf16[128,2304]{1,0:T(8,128)(2,1)S(1)} collective-permute-done((bf16[128,2304]{1,0:T(8,128)(2,1)S(1)}, bf16[128,2304]{1,0:T(8,128)(2,1)S(1)}, u32[]{:S(2)}, u32[]{:S(2)}) %collective-permute-start.3) | collective-permute-done | bytes 589856 | tf_op jit(solution)/shard_map/cond/branch_1_fun/ppermute | solution.py:659
  593.6 16.5 %all_to_all.17.do_ref = bf16[4,2,64,512]{3,2,1,0:T(8,128)(2,1)} all-to-all(bf16[4,2,64,512]{3,2,1,0:T(8,128)(2,1)S(1)} %bitcast.327), channel_id=1, replica_groups=mesh['seq'=4,'fsdp'=8] {'seq'}, dimensions={0} | all-to-all | bytes 1048576 | tf_op jit(solution)/shard_map/cond/branch_1_fun/all_to_all | solution.py:884
  610.1 22.1 %attend_back.1 = (bf16[4,2,64,512]{3,2,1,0:T(8,128)(2,1)}, bf16[8,4,2,64,512]{4,3,2,1,0:T(8,128)(2,1)}) custom-call(s32[1]{0:T(128)} %get-tuple-element.84.shard_ref, bf16[4,2,64,512]{3,2,1,0:T(8,128)(2,1)S(1)} %copy-done.28, bf16[4,2,64,512]{3,2,1,0:T(8,128)(2,1)} %all_to_all.17.do_ref, f32[4,2,128,128]{3,2,1,0:T(8,128)S(1)} %copy-done.48, ...), custom_call_target="tpu_custom_call" | custom-call | tf_op jit(solution)/shard_map/cond/branch_1_fun/attend_back/pallas_call | solution.py:198
  641.7 13.1 %collective-permute-done.8 = bf16[512,512]{1,0:T(8,128)(2,1)S(1)} collective-permute-done((bf16[512,512]{1,0:T(8,128)(2,1)S(1)}, bf16[512,512]{1,0:T(8,128)(2,1)S(1)}, u32[]{:S(2)}, u32[]{:S(2)}) %collective-permute-start.8) | collective-permute-done | bytes 524320 | tf_op jit(solution)/shard_map/cond/branch_1_fun/ppermute | solution.py:659
  658.3 12.1 %collective-permute-done.9 = bf16[512,512]{1,0:T(8,128)(2,1)S(1)} collective-permute-done((bf16[512,512]{1,0:T(8,128)(2,1)S(1)}, bf16[512,512]{1,0:T(8,128)(2,1)S(1)}, u32[]{:S(2)}, u32[]{:S(2)}) %collective-permute-start.9) | collective-permute-done | bytes 524320 | tf_op jit(solution)/shard_map/cond/branch_1_fun/ppermute | solution.py:659
  711.4 21.9 %collective-permute-done.5.refs_12_ = bf16[128,2304]{1,0:T(8,128)(2,1)} collective-permute-done((bf16[128,2304]{1,0:T(8,128)(2,1)S(1)}, bf16[128,2304]{1,0:T(8,128)(2,1)}, u32[]{:S(2)}, u32[]{:S(2)}) %collective-permute-start.5) | collective-permute-done | bytes 589856 | tf_op jit(solution)/shard_map/cond/branch_1_fun/ppermute | solution.py:570
  738.9 13.5 %all-to-all-start.2 = ((bf16[8,128,768]{2,1,0:T(8,128)(2,1)}), bf16[8,128,768]{2,1,0:T(8,128)(2,1)}, u32[]{:S(2)}, u32[]{:S(2)}) async-start(bf16[8,128,768]{2,1,0:T(8,128)(2,1)} %bitcast.308), calls=%async_computation.2 | async-start | bytes 3145728 | tf_op jit(solution)/shard_map/cond/branch_1_fun/all_to_all | solution.py:923
  767.5 22.8 %all-to-all-done.2 = bf16[8,128,768]{2,1,0:T(8,128)(2,1)} async-done(((bf16[8,128,768]{2,1,0:T(8,128)(2,1)}), bf16[8,128,768]{2,1,0:T(8,128)(2,1)}, u32[]{:S(2)}, u32[]{:S(2)}) %all-to-all-start.2) | async-done | bytes 1572896 | tf_op jit(solution)/shard_map/cond/branch_1_fun/all_to_all | solution.py:923
  790.3 15.6 %weight_grad.1 = bf16[768,2304]{1,0:T(8,128)(2,1)} custom-call(s32[17]{0:T(128)} %stack.72.place_ref, bf16[1024,768]{1,0:T(8,128)(2,1)} %bitcast.55.cols_ref, bf16[128,2304]{1,0:T(8,128)(2,1)} %get-tuple-element.94.refs_0_, bf16[128,2304]{1,0:T(8,128)(2,1)} %get-tuple-element.95.refs_1_, bf16[128,2304]{1,0:T(8,128)(2,1)} %get-tuple-element.96.refs_2_, ...), custom_call_target="tpu_custom_call" | custom-call | tf_op jit(solution)/shard_map/cond/branch_1_fun/weight_grad/pallas_call | solution.py:621
  843.4 59.6 %all-reduce.4.cloned.1.call-done = bf16[768,2304]{1,0:T(8,128)(2,1)} async-done(((bf16[768,2304]{1,0:T(8,128)(2,1)}), bf16[768,2304]{1,0:T(8,128)(2,1)}) %all-reduce.4.cloned.1.call-update) | async-done | bytes 3538960 | tf_op jit(solution)/shard_map/psum | solution.py:955
  (418 shorter events, 389.0 us)
Async XLA Ops:
  7.2 50.2 %all-gather.13.cloned.1.call-start = ((), (), s32[]{:S(2)}) async-start(), calls=%async_computation.10 | async-start | bytes 2949120 | tf_op jit(solution)/shard_map/all_gather | solution.py:757
  7.2 19.8 %collective-permute-start.15 = (bf16[3,256,2304]{2,1,0:T(8,128)(2,1)}, bf16[3,256,2304]{2,1,0:T(8,128)(2,1)S(1)}, u32[]{:S(2)}, u32[]{:S(2)}) collective-permute-start(bf16[3,256,2304]{2,1,0:T(8,128)(2,1)} %bitcast.283), channel_id=1, source_target_pairs={{0,1},{1,0},{2,3},{3,2},{4,5},{5,4},{6,7},{7,6},{8,9},{9,8},{10,11... | collective-permute-start | bytes 10616840 | tf_op jit(solution)/shard_map/ppermute | solution.py:419
  7.9 161.4 %all-gather.7.cloned.1.call-start = ((), (), s32[]{:S(2)}) async-start(), calls=%async_computation.5 | async-start | bytes 4718592 | tf_op jit(solution)/shard_map/all_gather | solution.py:782
  50.1 21.2 %collective-permute-start.18 = (bf16[1,256,2304]{2,1,0:T(8,128)(2,1)S(1)}, bf16[1,256,2304]{2,1,0:T(8,128)(2,1)S(1)}, u32[]{:S(2)}, u32[]{:S(2)}) collective-permute-start(bf16[1,256,2304]{2,1,0:T(8,128)(2,1)S(1)} %collective-permute-done.16.refs_1_.refs_2_.refs_9_), channel_id=1, source_target_pairs={{0,1},{1,0},{2,3},{3,2},{4,5},{5,4},{6,7},{7,6},{8,9},{9,8},{10,11... | collective-permute-start | bytes 3538952 | tf_op jit(solution)/shard_map/ppermute | solution.py:471
  85.5 201.2 %all-gather.9.cloned.1.call-start = ((), (), s32[]{:S(2)}) async-start(), calls=%async_computation.6 | async-start | bytes 5308416 | tf_op jit(solution)/shard_map/all_gather | solution.py:809
  101.7 52.4 %collective-permute-start.25 = (bf16[1,256,2304]{2,1,0:T(8,128)(2,1)S(1)}, bf16[1,256,2304]{2,1,0:T(8,128)(2,1)S(1)}, u32[]{:S(2)}, u32[]{:S(2)}) collective-permute-start(bf16[1,256,2304]{2,1,0:T(8,128)(2,1)S(1)} %collective-permute-done.21.refs_8_.refs_11_), channel_id=1, source_target_pairs={{0,1},{1,0},{2,3},{3,2},{4,5},{5,4},{6,7},{7,6},{8,9},{9,8},{10,11... | collective-permute-start | bytes 3538952 | tf_op jit(solution)/shard_map/ppermute | solution.py:471
  148.9 37.1 %collective-permute-start.23 = (bf16[1,256,2304]{2,1,0:T(8,128)(2,1)}, bf16[1,256,2304]{2,1,0:T(8,128)(2,1)}, u32[]{:S(2)}, u32[]{:S(2)}) collective-permute-start(bf16[1,256,2304]{2,1,0:T(8,128)(2,1)} %get-tuple-element.554), channel_id=1, source_target_pairs={{4,6},{27,25}} | collective-permute-start | bytes 3538952 | tf_op jit(solution)/shard_map/ppermute | solution.py:460
  150.6 35.5 %collective-permute-start.24 = (bf16[1,256,2304]{2,1,0:T(8,128)(2,1)}, bf16[1,256,2304]{2,1,0:T(8,128)(2,1)}, u32[]{:S(2)}, u32[]{:S(2)}) collective-permute-start(bf16[1,256,2304]{2,1,0:T(8,128)(2,1)} %get-tuple-element.552), channel_id=1, source_target_pairs={{4,6},{27,25}} | collective-permute-start | bytes 3538952 | tf_op jit(solution)/shard_map/ppermute | solution.py:460
  230.3 141.8 %reduce-scatter.2.cloned.1.call-start = ((), (), s32[]{:S(2)}) async-start(), calls=%async_computation.7 | async-start | bytes 5308416 | tf_op jit(solution)/shard_map/reduce_scatter | solution.py:821
  230.4 46.6 %collective-permute-start.34 = (bf16[2,128,2304]{2,1,0:T(8,128)(2,1)}, bf16[2,128,2304]{2,1,0:T(8,128)(2,1)S(1)}, u32[]{:S(2)}, u32[]{:S(2)}) collective-permute-start(bf16[2,128,2304]{2,1,0:T(8,128)(2,1)} %get-tuple-element.260), channel_id=1, source_target_pairs={{0,8},{8,0},{16,24},{24,16},{1,9},{9,1},{17,25},{25,17},{2,10},{10... | collective-permute-start | bytes 3538952 | tf_op jit(solution)/shard_map/ppermute | solution.py:714
  231.8 45.2 %collective-permute-start.35 = (bf16[2,128,2304]{2,1,0:T(8,128)(2,1)}, bf16[2,128,2304]{2,1,0:T(8,128)(2,1)}, u32[]{:S(2)}, u32[]{:S(2)}) collective-permute-start(bf16[2,128,2304]{2,1,0:T(8,128)(2,1)} %get-tuple-element.262), channel_id=1, source_target_pairs={{0,16},{8,24},{16,0},{24,8},{1,17},{9,25},{17,1},{25,9},{2,18},{10... | collective-permute-start | bytes 3538952 | tf_op jit(solution)/shard_map/ppermute | solution.py:714
  237.2 39.8 %collective-permute-start.32 = (bf16[1,128,2304]{2,1,0:T(8,128)(2,1)S(1)}, bf16[1,128,2304]{2,1,0:T(8,128)(2,1)}, u32[]{:S(2)}, u32[]{:S(2)}) collective-permute-start(bf16[1,128,2304]{2,1,0:T(8,128)(2,1)S(1)} %get-tuple-element.559), channel_id=1, source_target_pairs={{0,8},{8,0},{16,24},{24,16},{1,9},{9,1},{17,25},{25,17},{2,10},{10... | collective-permute-start | bytes 1769480 | tf_op jit(solution)/shard_map/ppermute | solution.py:714
  238.7 38.4 %collective-permute-start.33 = (bf16[1,128,2304]{2,1,0:T(8,128)(2,1)S(1)}, bf16[1,128,2304]{2,1,0:T(8,128)(2,1)}, u32[]{:S(2)}, u32[]{:S(2)}) collective-permute-start(bf16[1,128,2304]{2,1,0:T(8,128)(2,1)S(1)} %get-tuple-element.558), channel_id=1, source_target_pairs={{0,16},{8,24},{16,0},{24,8},{1,17},{9,25},{17,1},{25,9},{2,18},{10... | collective-permute-start | bytes 1769480 | tf_op jit(solution)/shard_map/ppermute | solution.py:714
  318.2 120.4 %all-gather.11.cloned.1.call-start = ((), (), s32[]{:S(2)}) async-start(), calls=%async_computation.8 | async-start | bytes 5308416 | tf_op jit(solution)/shard_map/all_gather | solution.py:833
  318.3 55.0 %collective-permute-start.36 = (bf16[2,128,2304]{2,1,0:T(8,128)(2,1)}, bf16[2,128,2304]{2,1,0:T(8,128)(2,1)}, u32[]{:S(2)}, u32[]{:S(2)}) collective-permute-start(bf16[2,128,2304]{2,1,0:T(8,128)(2,1)} %get-tuple-element.260), channel_id=1, source_target_pairs={{0,16},{8,24},{16,0},{24,8},{1,17},{9,25},{17,1},{25,9},{2,18},{10... | collective-permute-start | bytes 3538952 | tf_op jit(solution)/shard_map/ppermute | solution.py:720
  319.8 53.5 %collective-permute-start.38 = (bf16[2,128,2304]{2,1,0:T(8,128)(2,1)}, bf16[2,128,2304]{2,1,0:T(8,128)(2,1)}, u32[]{:S(2)}, u32[]{:S(2)}) collective-permute-start(bf16[2,128,2304]{2,1,0:T(8,128)(2,1)} %get-tuple-element.262), channel_id=1, source_target_pairs={{0,8},{8,0},{16,24},{24,16},{1,9},{9,1},{17,25},{25,17},{2,10},{10... | collective-permute-start | bytes 3538952 | tf_op jit(solution)/shard_map/ppermute | solution.py:720
  321.3 52.0 %collective-permute-start.37 = (bf16[2,128,2304]{2,1,0:T(8,128)(2,1)}, bf16[2,128,2304]{2,1,0:T(8,128)(2,1)}, u32[]{:S(2)}, u32[]{:S(2)}) collective-permute-start(bf16[2,128,2304]{2,1,0:T(8,128)(2,1)} %copy-done.30), channel_id=1, source_target_pairs={{0,16},{8,24},{16,0},{24,8},{1,17},{9,25},{17,1},{25,9},{2,18},{10... | collective-permute-start | bytes 3538952 | tf_op jit(solution)/shard_map/ppermute | solution.py:720
  321.8 51.5 %collective-permute-start.39 = (bf16[2,128,2304]{2,1,0:T(8,128)(2,1)}, bf16[2,128,2304]{2,1,0:T(8,128)(2,1)}, u32[]{:S(2)}, u32[]{:S(2)}) collective-permute-start(bf16[2,128,2304]{2,1,0:T(8,128)(2,1)} %collective-permute-done.35.refs_9_), channel_id=1, source_target_pairs={{0,8},{8,0},{16,24},{24,16},{1,9},{9,1},{17,25},{25,17},{2,10},{10... | collective-permute-start | bytes 3538952 | tf_op jit(solution)/shard_map/ppermute | solution.py:720
  376.4 429.5 %all-reduce.6.cloned.1.call-start = ((), (), s32[]{:S(2)}) async-start(), calls=%async_computation.11 | async-start | bytes 31850496 | tf_op jit(solution)/shard_map/psum | solution.py:866
  495.7 407.3 %all-reduce.4.cloned.1.call-start = ((), (), s32[]{:S(2)}) async-start(), calls=%async_computation.9 | async-start | bytes 7077888 | tf_op jit(solution)/shard_map/psum | solution.py:955
  688.8 44.5 %all-to-all-start.1 = ((bf16[4,2,64,1024]{3,2,1,0:T(8,128)(2,1)}), bf16[4,2,64,1024]{3,2,1,0:T(8,128)(2,1)}, u32[]{:S(2)}, u32[]{:S(2)}) async-start(bf16[4,2,64,1024]{3,2,1,0:T(8,128)(2,1)} %pad_maximum_fusion.1), calls=%async_computation.1 | async-start | bytes 2097152 | tf_op jit(solution)/shard_map/cond/branch_1_fun/all_to_all | solution.py:894
  693.2 40.1 %collective-permute-start.5 = (bf16[128,2304]{1,0:T(8,128)(2,1)S(1)}, bf16[128,2304]{1,0:T(8,128)(2,1)}, u32[]{:S(2)}, u32[]{:S(2)}) collective-permute-start(bf16[128,2304]{1,0:T(8,128)(2,1)S(1)} %copy-done.22), channel_id=1, source_target_pairs={{0,4},{1,5},{2,6},{3,7},{4,0},{5,1},{6,2},{7,3},{8,12},{9,13},{10,... | collective-permute-start | bytes 1769480 | tf_op jit(solution)/shard_map/cond/branch_1_fun/ppermute | solution.py:570
  693.7 39.6 %collective-permute-start.6 = (bf16[128,2304]{1,0:T(8,128)(2,1)S(1)}, bf16[128,2304]{1,0:T(8,128)(2,1)}, u32[]{:S(2)}, u32[]{:S(2)}) collective-permute-start(bf16[128,2304]{1,0:T(8,128)(2,1)S(1)} %copy-done.22), channel_id=1, source_target_pairs={{0,6},{1,7},{2,0},{3,1},{4,2},{5,3},{6,4},{7,5},{8,14},{9,15},{10,... | collective-permute-start | bytes 1769480 | tf_op jit(solution)/shard_map/cond/branch_1_fun/ppermute | solution.py:570
  738.9 51.4 %all-to-all-start.2 = ((bf16[8,128,768]{2,1,0:T(8,128)(2,1)}), bf16[8,128,768]{2,1,0:T(8,128)(2,1)}, u32[]{:S(2)}, u32[]{:S(2)}) async-start(bf16[8,128,768]{2,1,0:T(8,128)(2,1)} %bitcast.308), calls=%async_computation.2 | async-start | bytes 3145728 | tf_op jit(solution)/shard_map/cond/branch_1_fun/all_to_all | solution.py:923
  (123 other events, 1359.1 us)
Sparse Core Ops, SparseCore 0:
  9.8 40.2 all-gather.12
  85.7 63.5 all-gather.6
  230.5 56.2 all-gather.8
  318.3 53.7 reduce-scatter.1
  376.5 50.0 all-gather.10
  495.8 307.6 all-reduce.5
  807.0 95.9 all-reduce.3

commit v4 on v3

--- a/solution.py
+++ b/solution.py
@@ -562,12 +562,20 @@
     return pieces
 
 
-def direct_pieces(block, shard, shards):
+def direct_pieces(block, shard, shards, wanted):
     chips = shards // 2
     swap = [(f, f ^ 1) for f in range(shards)]
     core = shard % 2
     come = [block] + [
-        lax.ppermute(block, "fsdp", [(f, (f + 2 * hop) % shards) for f in range(shards)])
+        lax.ppermute(
+            block,
+            "fsdp",
+            [
+                (f, (f + 2 * hop) % shards)
+                for f in range(shards)
+                if (f + 2 * hop) % shards // 2 in wanted
+            ],
+        )
         for hop in range(1, chips)
     ]
 
@@ -680,12 +688,35 @@
     return jnp.concatenate(done, axis=-1)
 
 
-def sum_everywhere(value, columns, shards):
-    for axis, count in (("fsdp", shards), ("seq", columns)):
-        bit = 1
-        while bit < count:
-            value = value + lax.ppermute(value, axis, [(c, c ^ bit) for c in range(count)])
-            bit *= 2
+def column_total(value, column, later):
+    rows, width = value.shape
+    step, half = rows // 4, width // 2
+    parts = jnp.stack(
+        [lax.dynamic_slice_in_dim(value, (column ^ k) * step, step, 0) for k in range(4)]
+    )
+    own = column_scatter(parts).astype(bf16)
+    own, *later = lax.optimization_barrier((own, *later))
+    pieces = (own[:, :half], own[:, half:])
+    near = tuple(lax.ppermute(p, "seq", partners(4, bit)) for p, bit in zip(pieces, (1, 2)))
+    near, *later = lax.optimization_barrier((near, *later))
+    out = jnp.zeros((rows, width), f32)
+    for first, second, low, piece, got in (
+        (1, 2, 0, pieces[0], near[0]),
+        (2, 1, half, pieces[1], near[1]),
+    ):
+        far = lax.ppermute(jnp.stack([piece, got]), "seq", partners(4, second))
+        for k, block in ((0, piece), (first, got), (second, far[0]), (3, far[1])):
+            out = lax.dynamic_update_slice(
+                out, block.astype(f32), ((column ^ k) * step, low)
+            )
+    return (out, *later)
+
+
+def sum_over(value, axis, count):
+    bit = 1
+    while bit < count:
+        value = value + lax.ppermute(value, axis, [(c, c ^ bit) for c in range(count)])
+        bit *= 2
     return value
 
 
@@ -706,51 +737,22 @@
             granules.reshape(-1, 2, HALF, width), core, 1, keepdims=False
         )
 
-    def round_start(granules):
-        lanes = core_half(granules)
-        cut = lanes.shape[0] // 2
-        lanes = (lanes[:cut], lanes[cut:])
-        near = tuple(
-            lax.ppermute(lane, "seq", partners(4, bit)) for lane, bit in zip(lanes, (1, 2))
-        )
-        return lanes, near
-
-    def round_on(lanes, near):
-        return tuple(
-            tuple(lax.ppermute(piece, "seq", partners(4, bit)) for piece in pieces)
-            for pieces, bit in zip(zip(lanes, near), (2, 1))
-        )
-
-    def all_columns(granules, near, far):
-        count = granules.shape[0]
-        cut = count // 2
-        come = {
-            (0, 1): near[0],
-            (0, 2): far[0][0],
-            (0, 3): far[0][1],
-            (1, 2): near[1],
-            (1, 1): far[1][0],
-            (1, 3): far[1][1],
+    def all_columns(own, other, begin, end):
+        count = own.shape[1]
+        sources = {
+            "mine": own.reshape(columns * count, HALF, width),
+            "other": other.reshape(columns * count, HALF, width),
         }
-        sources = {"mine": granules.reshape(2 * count, HALF, width)}
-        for (part, hop), lane in come.items():
-            sources["own%d%d" % (part, hop)] = lane
-            sources["other%d%d" % (part, hop)] = lax.ppermute(lane, "fsdp", swap)
-        places = []
-        for home in range(columns):
-            for k in range(count):
-                for half in range(2):
-                    place = {}
-                    for c in range(columns):
-                        for f in range(shards):
-                            part, hop = int(k >= cut), home ^ c
-                            whose = "own" if f % 2 == half else "other"
-                            place[c * shards + f] = (
-                                ("%s%d%d" % (whose, part, hop), k - part * cut)
-                                if hop
-                                else ("mine", 2 * k + half)
-                            )
-                    places.append(place)
+        places = [
+            {
+                c * shards + f: ("mine" if f % 2 == half else "other", home * count + k)
+                for c in range(columns)
+                for f in range(shards)
+            }
+            for home in range(columns)
+            for k in range(begin, end)
+            for half in range(2)
+        ]
         device = column * shards + shard
         return pick(places, sources, device, columns * shards).reshape(-1, width)
 
@@ -781,97 +783,133 @@
     )
     kv_all = lax.all_gather(made["kv"].reshape(columns, seqs, rows, 2 * HD), "fsdp", axis=0)
     queries = made["q"].reshape(columns, seqs, rows, per * HD)
-    weight_in = first_weights(queries)
-    if columns == 4:
-        in_lanes, in_near = round_start(weight_in)
-        kv_all, in_lanes = lax.optimization_barrier((kv_all, in_lanes))
-
-    mixed, lse = attend(shard_arg, queries, kv_all)
-    if columns == 4:
-        by_partner = jnp.concatenate(
-            [lax.dynamic_slice_in_dim(mixed, column ^ k, 1, 0) for k in range(columns)], axis=0
-        ).reshape(columns * own_rows, per * HD)
-        attn_out = column_scatter(times_out(by_partner).reshape(columns, own_rows, width))
-    else:
-        attn_out = lax.psum_scatter(
-            times_out(mixed.reshape(-1, per * HD)),
-            "seq",
-            scatter_dimension=0,
-            tiled=True,
-        ).astype(f32)
     flat_tokens = tokens.reshape(-1, width).astype(f32)
     flat_cot = out_grad.reshape(-1, width).astype(f32)
+    normed_own = rms_scale(flat_tokens, gain_rows[0]).astype(bf16)
+    normed_own, kv_all = lax.optimization_barrier((normed_own, kv_all))
+    mixed, lse = attend(shard_arg, queries, kv_all)
+    kept = {"mixed": mixed}
+
+    def beside(step, held):
+        if step == 1:
+            held, kept["mixed"] = lax.optimization_barrier((held, kept["mixed"]))
+            if columns == 4:
+                by_partner = jnp.concatenate(
+                    [
+                        lax.dynamic_slice_in_dim(kept["mixed"], column ^ k, 1, 0)
+                        for k in range(columns)
+                    ],
+                    axis=0,
+                )
+                kept["part"] = times_out(by_partner.reshape(columns * own_rows, per * HD))
+            else:
+                kept["part"] = times_out(kept["mixed"].reshape(-1, per * HD))
+        if step == 2:
+            held, kept["part"] = lax.optimization_barrier((held, kept["part"]))
+            if columns == 4:
+                kept["out"] = column_scatter(kept["part"].reshape(columns, own_rows, width))
+            else:
+                kept["out"] = lax.psum_scatter(
+                    kept["part"], "seq", scatter_dimension=0, tiled=True
+                ).astype(f32)
+        if step == 3:
+            held, kept["out"] = lax.optimization_barrier((held, kept["out"]))
+        return held
+
+    normed_pieces = ring_pieces(normed_own, shard, shards, beside)
+    mixed, attn_out = kept["mixed"], kept["out"]
+    lanes = jnp.concatenate(
+        [core_half(first_weights(mixed)), core_half(out_weights(mixed))], axis=0
+    )
+    attn_out, lanes = lax.optimization_barrier((attn_out, lanes))
+    kept["lanes"] = lax.all_gather(lanes, "seq", axis=0)
     residual = flat_tokens + rms_scale(attn_out, gain_rows[1])
     normed_ffn = rms_scale(residual, gain_rows[2]).astype(bf16)
 
-    mixed_later, normed_ffn = lax.optimization_barrier((mixed, normed_ffn))
-    weight_out = out_weights(normed_ffn)
-    ffn_in = lax.all_gather(normed_ffn, "fsdp", axis=0, tiled=True)
-    mixed_rows = lax.all_to_all(mixed_later, "seq", split_axis=0, concat_axis=0, tiled=True)
-    mixed_rows = mixed_rows.transpose(1, 2, 0, 3).reshape(own_rows, HQ * HD)
-    if columns == 4:
-        out_lanes, out_near = round_start(weight_out)
-        ffn_in, out_near, in_near, mixed_rows = lax.optimization_barrier(
-            (ffn_in, out_near, in_near, mixed_rows)
-        )
-        in_far = round_on(in_lanes, in_near)
-    gate_up = jnp.einsum("td,fgd->tgf", ffn_in, ffn_weight[:, :2], preferred_element_type=f32)
-    hidden = gated_units(gate_up[:, 0], gate_up[:, 1]).astype(bf16)
-    branch = dot_nn(hidden, ffn_weight[:, 2]).astype(bf16)
-    ffn_out = lax.psum_scatter(branch, "fsdp", scatter_dimension=0, tiled=True).astype(f32)
-    if columns == 4:
-        ffn_out, in_far = lax.optimization_barrier((ffn_out, in_far))
-        out_far = round_on(out_lanes, out_near)
-        weight_in_all = all_columns(weight_in, in_near, in_far)
-    else:
-        weight_in_all = lax.all_gather(weight_in, "seq", axis=0).reshape(-1, width)
-        weight_out_all = lax.all_gather(weight_out, "seq", axis=0).reshape(-1, width)
+    chips, ring, _ = ring_tables(shards)
+    weight_gate_up, weight_down = ffn_weight[:, :2], ffn_weight[:, 2]
+
+    def pipeline(block, work, aside, before_last):
+        held = block
+        for t in range(chips):
+            rows_here = jnp.concatenate([held, lax.ppermute(held, "fsdp", swap)], axis=0)
+            if t + 1 < chips:
+                held = lax.ppermute(held, "fsdp", ring)
+            made = work(t, rows_here).astype(bf16)
+            got = lax.ppermute(made[own_rows:], "fsdp", swap)
+            pair = made[:own_rows].astype(f32) + got.astype(f32)
+            if t == 0:
+                first = pair
+            else:
+                total = pair if t == 1 else total + pair
+            if t + 1 < chips:
+                held, made = aside(t, *lax.optimization_barrier((held, made)))
+            if t:
+                total = total.astype(bf16)
+                if t + 1 < chips:
+                    held, total = lax.optimization_barrier((held, total))
+                else:
+                    total = before_last(total)
+                total = lax.ppermute(total, "fsdp", ring).astype(f32)
+        return total + first
+
+    saved = []
+
+    def forward(t, rows_here):
+        gate_up = jnp.einsum(
+            "td,fgd->tgf", rows_here, weight_gate_up, preferred_element_type=f32
+        )
+        hidden = gated_units(gate_up[:, 0], gate_up[:, 1]).astype(bf16)
+        saved.append((rows_here, gate_up, hidden))
+        return dot_nn(hidden, weight_down)
+
+    ffn_out = pipeline(
+        normed_ffn, forward, lambda t, held, made: (held, made), lambda total: total
+    )
     result = residual + rms_scale(ffn_out, gain_rows[3])
     block_out = result.astype(bf16).reshape(tokens.shape)
     grad_ffn, gain_terms = norm_back(ffn_out, gain_rows[3], flat_cot)
     gain_last = jnp.sum(gain_terms, axis=0)
-    grad_ffn_all = lax.all_gather(grad_ffn.astype(bf16), "fsdp", axis=0, tiled=True)
-    if columns == 4:
-        weight_out_all = all_columns(weight_out, out_near, out_far)
-        grad_ffn_all, weight_out_all, weight_in_all = lax.optimization_barrier(
-            (grad_ffn_all, weight_out_all, weight_in_all)
-        )
-
-    normed_own = rms_scale(flat_tokens, gain_rows[0]).astype(bf16)
-    grad_ffn_all, normed_own = lax.optimization_barrier((grad_ffn_all, normed_own))
-    kept = {}
-
-    def beside(step, held):
-        if step == 1:
-            part = dot_tn(hidden, grad_ffn_all).astype(bf16)
-            held, kept["down"], kept["all"] = lax.optimization_barrier((held, part, grad_ffn_all))
-        if step == 2:
-            grad_hidden = dot_nt(kept["all"], ffn_weight[:, 2])
-            unused, gated_pull = jax.vjp(gated_units, gate_up[:, 0], gate_up[:, 1])
-            grad_gate, grad_up = gated_pull(grad_hidden)
-            part = jnp.stack([grad_gate, grad_up], axis=1).astype(bf16)
-            held, kept["units"] = lax.optimization_barrier((held, part))
-        if step == 3:
-            parts = (
-                dot_tn(kept["units"][:, 0], ffn_in).astype(bf16),
-                dot_tn(kept["units"][:, 1], ffn_in).astype(bf16),
-            )
-            held, kept["up"], kept["units"] = lax.optimization_barrier(
-                (held, parts, kept["units"])
-            )
-        return held
-
-    normed_pieces = ring_pieces(normed_own, shard, shards, beside)
-    grad_gate_up = kept["units"]
-    gate_grad, up_grad, down_grad = lax.psum((*kept["up"], kept["down"]), "seq")
+
+    back = []
+
+    def backward(t, grads_here):
+        grad_hidden = dot_nt(grads_here, weight_down)
+        _, gate_up, _ = saved[t]
+        unused, gated_pull = jax.vjp(gated_units, gate_up[:, 0], gate_up[:, 1])
+        grad_gate, grad_up = gated_pull(grad_hidden)
+        units = jnp.stack([grad_gate, grad_up], axis=1).astype(bf16)
+        back.append((grads_here, units))
+        return jnp.einsum("tgf,fgd->td", units, weight_gate_up, preferred_element_type=f32)
+
+    def backward_aside(t, held, made):
+        if t == chips - 2:
+            held, made, kept["lanes"] = lax.optimization_barrier((held, made, kept["lanes"]))
+        return held, made
+
+    def units_after(total):
+        total, units = lax.optimization_barrier((total, [part for _, part in back]))
+        kept["units"] = units
+        return total
+
+    grad_normed_ffn = pipeline(grad_ffn.astype(bf16), backward, backward_aside, units_after)
+    ffn_in = jnp.concatenate([rows_here for rows_here, _, _ in saved], axis=0)
+    hidden = jnp.concatenate([units for _, _, units in saved], axis=0)
+    grad_ffn_all = jnp.concatenate([grads_here for grads_here, _ in back], axis=0)
+    units = jnp.concatenate(kept["units"], axis=0)
+    gate_grad, up_grad, down_grad = lax.psum(
+        (
+            dot_tn(units[:, 0], ffn_in).astype(bf16),
+            dot_tn(units[:, 1], ffn_in).astype(bf16),
+            dot_tn(hidden, grad_ffn_all).astype(bf16),
+        ),
+        "seq",
+    )
 
     def attention_back():
-        grad_in = jnp.einsum(
-            "tgf,fgd->td", grad_gate_up, ffn_weight[:, :2], preferred_element_type=f32
-        )
-        grad_normed_ffn = ring_scatter(
-            grad_in.astype(bf16).reshape(shards, own_rows, width), shard, shards
-        )
+        other_lanes = lax.ppermute(kept["lanes"], "fsdp", swap)
+        weight_in_all = all_columns(kept["lanes"], other_lanes, 0, per + 2)
+        weight_out_all = all_columns(kept["lanes"], other_lanes, per + 2, 2 * per + 2)
         grad_mid, gain_pre_ffn = norm_back(residual, gain_rows[2], grad_normed_ffn)
         grad_residual = flat_cot + grad_mid
         grad_attn, gain_post_attn = norm_back(attn_out, gain_rows[1], grad_residual)
@@ -881,10 +919,20 @@
             .astype(bf16)
             .reshape(seqs, rows, columns, per * HD)
         )
-        grad_heads = lax.all_to_all(
-            grad_mixed.transpose(2, 0, 1, 3), "seq", split_axis=0, concat_axis=0, tiled=True
-        )
-        later_pieces = direct_pieces(grad_attn_low, shard, shards)
+        both = lax.all_to_all(
+            jnp.concatenate([grad_mixed.transpose(2, 0, 1, 3), mixed], axis=-1),
+            "seq",
+            split_axis=0,
+            concat_axis=0,
+            tiled=True,
+        )
+        grad_heads = both[..., : per * HD]
+        mixed_rows = both[..., per * HD :].transpose(1, 2, 0, 3).reshape(own_rows, HQ * HD)
+        shard_cols = attn_weight.shape[0]
+        first_owner = (HQ + 2 * KVH) * HD // shard_cols // 2
+        later_pieces = direct_pieces(
+            grad_attn_low, shard, shards, range(first_owner, shards // 2)
+        )
         grad_queries, grad_kv = attend_back(shard_arg, queries, grad_heads, lse, kv_all)
         grad_kv_own = (
             ring_scatter(grad_kv.reshape(shards, columns * own_rows, 2 * HD), shard, shards)
@@ -919,7 +967,6 @@
             ],
             axis=1,
         )
-        shard_cols = attn_weight.shape[0]
         col_all = lax.all_to_all(
             weight_cols.reshape(own_rows, shards, shard_cols).transpose(1, 0, 2),
             "fsdp",
@@ -937,32 +984,38 @@
                 gain_last,
             ]
         )
+        gain_grad = lax.dynamic_slice_in_dim(
+            sum_over(gain_grad, "fsdp", shards),
+            shard * norm_gains.shape[1],
+            norm_gains.shape[1],
+            1,
+        )
         return attn_grad, gain_grad, token_grad
 
     def nothing():
         return (
             jnp.zeros(attn_weight.shape, bf16),
-            jnp.zeros((4, width), f32),
+            jnp.zeros(norm_gains.shape, f32),
             jnp.zeros(tokens.shape, f32),
         )
 
     attn_grad, gain_grad, token_grad = lax.cond(
         shard < 2**20, attention_back, nothing
     )
-    attn_grad, gate_grad, up_grad, down_grad = lax.optimization_barrier(
-        (attn_grad, gate_grad, up_grad, down_grad)
-    )
-    attn_total = lax.psum(attn_grad, "seq").astype(f32)
+    gain_total = sum_over(gain_grad, "seq", columns)
+    if columns == 4:
+        attn_total, gate_grad, up_grad, down_grad = column_total(
+            attn_grad, column, (gate_grad, up_grad, down_grad)
+        )
+    else:
+        attn_grad, gate_grad, up_grad, down_grad = lax.optimization_barrier(
+            (attn_grad, gate_grad, up_grad, down_grad)
+        )
+        attn_total = lax.psum(attn_grad, "seq").astype(f32)
     ffn_grad = widen_plane(down_grad, 2, 3, None)
     ffn_grad = widen_plane(gate_grad, 0, 3, ffn_grad)
     ffn_grad = widen_plane(up_grad, 1, 3, ffn_grad)
     ffn_grad = ffn_grad.transpose(1, 0, 2)
-    gain_total = lax.dynamic_slice_in_dim(
-        sum_everywhere(gain_grad, columns, shards),
-        shard * norm_gains.shape[1],
-        norm_gains.shape[1],
-        1,
-    )
     return (block_out, token_grad, attn_total, gain_total, ffn_grad)
 
 

time: 927 us -> 858 us (0.926)
  waiting for transfers between devices: 351 us -> 234 us
  starting transfers between devices: 121 us -> 180 us
  blocking collectives: 68.5 us -> 15.7 us
  matrix products: 99 us -> 137 us
    ppermute x29 -> x38, waiting for transfers between devices: 42.2 us -> 113 us  [the longest x6 50.5 us: pipeline(): total = lax.ppermute(total, 'fsdp', ring).astype(f32)]
    psum x2 -> x1, waiting for transfers between devices: 59.6 us -> 0.02 us  [local(): lax.psum((dot_tn(units[:, 0], ffn_in).astype(bf16), dot_tn(units[:, 1], f...]
    all_to_all x2 -> x0, blocking collectives: 52.8 us -> none  [the longest x1 36.3 us: local(): lax.all_to_all(mixed_later, 'seq', split_axis=0, concat_axis=0, tiled=True)]
    reduce_scatter x1 -> x0, waiting for transfers between devices: 49.7 us -> none  [local(): lax.psum_scatter(branch, 'fsdp', scatter_dimension=0, tiled=True)]
    ppermute x6 -> x3, waiting for transfers between devices: 77.9 us -> 32.8 us  [ring_scatter(): lax.ppermute(total.astype(bf16), 'fsdp', pairs).astype(f32)]
    ppermute x3, waiting for transfers between devices: 32.5 us -> 1.96 us  [direct_pieces(): lax.ppermute(block, 'fsdp', [(f, (f + 2 * hop) % shards) for f in range(s...]
    all_to_all x0 -> x1, waiting for transfers between devices: none -> 25.9 us  [attention_back(): lax.all_to_all(jnp.concatenate([grad_mixed.transpose(2, 0, 1, 3), mixed],...]
    all_to_all x1, waiting for transfers between devices: 22.8 us -> 0.01 us  [attention_back(): lax.all_to_all(weight_cols.reshape(own_rows, shards, shard_cols).transpos...]
  transfers between devices with their start and end apart: 77 -> 84, of which waited for: 44 -> 34; matrix products, arithmetic and copies ran while one was open for 16% -> 26% of each run, Pallas kernels for 13% -> 15%
where the time goes in v4:
time: 858 us; the launch traced here: 846 us
  waiting for transfers between devices  234 us (27%)
  starting transfers between devices  180 us (21%)
  matrix products  137 us (16%)
  Pallas kernels  129 us (15%)
  other arithmetic  62.2 us (7%)
  local copies, waits for them, and re-layouts  59.1 us (7%)
  between operations  18.1 us (2%)
  blocking collectives  15.7 us (2%)
  loops' own time  10.7 us (1%)
    pallas_call x9, Pallas kernels, pick(): pl.pallas_call(functools.partial(kernel, cands), grid_spec=pltpu.Prefetch...  61.5 us
    ppermute x4, starting transfers between devices, routed_weights(): sources['swapped%d' % number] = lax.ppermute(got, 'fsdp', swap)  52.8 us
    ppermute x6, waiting for transfers between devices, pipeline(): total = lax.ppermute(total, 'fsdp', ring).astype(f32)  50.5 us
    ppermute x5, waiting for transfers between devices, sum_over(): lax.ppermute(value, axis, [(c, c ^ bit) for c in range(count)])  34 us
    ppermute x3, waiting for transfers between devices, ring_scatter(): lax.ppermute(total.astype(bf16), 'fsdp', pairs).astype(f32)  32.8 us
    dot_general x5, matrix products, dot_nn(): lax.dot_general(a, b, (((1,), (0,)), ((), ())), preferred_element_type=f32)  32.5 us
    ppermute x4, waiting for transfers between devices, column_scatter(): lax.ppermute(jnp.concatenate([low[first:first + 1], low[3:]], axis=0), 's...  30.1 us
    dot_general x4, matrix products, backward(): jnp.einsum('tgf,fgd->td', units, weight_gate_up, preferred_element_type=f32)  29.1 us
  transfers between devices with their start and end apart: 84, of which 34 were waited for; matrix products, arithmetic and copies ran while one was open for 26% of the time, Pallas kernels for 15%

profile of v4, /device:TPU:0, one launch (start us, length us, event | category | flops | bytes accessed | tf_op | source)
XLA Modules:
  0.0 846.4 jit_solution(17773694334834037398)
XLA Ops:
  8.0 15.7 %all-gather.2 = bf16[8,288,4]{1,2,0:T(4,128)(2,1)S(1)} all-gather(bf16[1,288,4]{1,2,0:T(4,128)(2,1)} %bitcast.490), channel_id=1, replica_groups=mesh['seq'=4,'fsdp'=8] {'fsdp'}, dimensions={0}, use_global_device_ids=true | all-gather | bytes 20736 | tf_op jit(solution)/shard_map/all_gather | solution.py:760
  102.6 45.3 %collective-permute-start.24 = (bf16[1,256,2304]{2,1,0:T(8,128)(2,1)S(1)}, bf16[1,256,2304]{2,1,0:T(8,128)(2,1)S(1)}, u32[]{:S(2)}, u32[]{:S(2)}) collective-permute-start(bf16[1,256,2304]{2,1,0:T(8,128)(2,1)S(1)} %collective-permute-done.22.refs_8_.refs_11_), channel_id=1, source_target_pairs={{0,1},{1,0},{2,3},{3,2},{4,5},{5,4},{6,7},{7,6},{8,9},{9,8},{10,11... | collective-permute-start | bytes 3538952 | tf_op jit(solution)/shard_map/ppermute | solution.py:471
  158.8 16.0 %attend.1 = (bf16[4,2,64,512]{3,2,1,0:T(8,128)(2,1)S(1)}, f32[4,2,128,128]{3,2,1,0:T(8,128)}) custom-call(s32[1]{0:T(128)} %bitcast.71.shard_ref, bf16[4,2,64,512]{3,2,1,0:T(8,128)(2,1)S(1)} %bitcast.465, bf16[8,4,2,64,512]{4,3,2,1,0:T(8,128)(2,1)} %all-gather.7.cloned.1.call-done.kv_ref), custom_call_target="tpu_custom_call" | custom-call | tf_op jit(solution)/shard_map/attend/pallas_call | solution.py:167
  288.2 12.0 %collective-permute-done.42 = bf16[128,2304]{1,0:T(8,128)(2,1)S(1)} collective-permute-done((bf16[128,2304]{1,0:T(8,128)(2,1)S(1)}, bf16[128,2304]{1,0:T(8,128)(2,1)S(1)}, u32[]{:S(2)}, u32[]{:S(2)}) %collective-permute-start.42) | collective-permute-done | bytes 589856 | tf_op jit(solution)/shard_map/ppermute | solution.py:853
  320.8 13.3 %collective-permute-done.47 = bf16[128,2304]{1,0:T(8,128)(2,1)S(1)} collective-permute-done((bf16[128,2304]{1,0:T(8,128)(2,1)S(1)}, bf16[128,2304]{1,0:T(8,128)(2,1)S(1)}, u32[]{:S(2)}, u32[]{:S(2)}) %collective-permute-start.47) | collective-permute-done | bytes 589856 | tf_op jit(solution)/shard_map/ppermute | solution.py:853
  345.0 8.1 fusion.26
  389.4 11.9 %collective-permute-done.57 = bf16[128,2304]{1,0:T(8,128)(2,1)S(1)} collective-permute-done((bf16[128,2304]{1,0:T(8,128)(2,1)S(1)}, bf16[128,2304]{1,0:T(8,128)(2,1)S(1)}, u32[]{:S(2)}, u32[]{:S(2)}) %collective-permute-start.57) | collective-permute-done | bytes 589856 | tf_op jit(solution)/shard_map/ppermute | solution.py:853
  429.0 7.5 convolution_convert_fusion.2
  452.8 12.8 %collective-permute-done.62 = bf16[128,2304]{1,0:T(8,128)(2,1)S(1)} collective-permute-done((bf16[128,2304]{1,0:T(8,128)(2,1)}, bf16[128,2304]{1,0:T(8,128)(2,1)S(1)}, u32[]{:S(2)}, u32[]{:S(2)}) %collective-permute-start.62) | collective-permute-done | bytes 589856 | tf_op jit(solution)/shard_map/ppermute | solution.py:853
  466.7 283.8 %conditional.1 = (bf16[768,2304]{1,0:T(8,128)(2,1)}, f32[4,288]{1,0:T(4,128)}, f32[2,64,2304]{2,1,0:T(8,128)}) conditional(s32[]{:T(128)} %convert_element_type.461, () %tuple.68, (s32[]{:T(128)}, pred[]{:T(512)}, (), s32[]{:T(128)}, f32[128,2304]{1,0:T(8,128)S(1)}, /*index=5*/f32[128,2304]{1,0:T(8,128)S(1)}, f32[128,2304]{1,0:T(8,128)}, ...), branch_computations={%region_6.7_spmd, %region_7.18_spmd} | conditional | flops 3654062592 | bytes 229105280 | solution.py:1002
  474.8 13.7 %collective-permute-done.3 = bf16[4,6,128,2304]{3,2,1,0:T(8,128)(2,1)} collective-permute-done((bf16[4,6,128,2304]{3,2,1,0:T(8,128)(2,1)}, bf16[4,6,128,2304]{3,2,1,0:T(8,128)(2,1)}, u32[]{:S(2)}, u32[]{:S(2)}) %collective-permute-start.3) | collective-permute-done | bytes 14155808 | tf_op jit(solution)/shard_map/cond/branch_1_fun/ppermute | solution.py:910
  488.5 8.4 pick.6
  509.7 25.9 %all-to-all-done = bf16[4,2,64,1024]{3,2,1,0:T(8,128)(2,1)S(1)} async-done(((bf16[4,2,64,1024]{3,2,1,0:T(8,128)(2,1)}), bf16[4,2,64,1024]{3,2,1,0:T(8,128)(2,1)S(1)}, u32[]{:S(2)}, u32[]{:S(2)}) %all-to-all-start) | async-done | bytes 1048608 | tf_op jit(solution)/shard_map/cond/branch_1_fun/all_to_all | solution.py:922
  536.7 22.0 %attend_back.1 = (bf16[4,2,64,512]{3,2,1,0:T(8,128)(2,1)}, bf16[8,4,2,64,512]{4,3,2,1,0:T(8,128)(2,1)}) custom-call(s32[1]{0:T(128)} %get-tuple-element.132.shard_ref, bf16[4,2,64,512]{3,2,1,0:T(8,128)(2,1)S(1)} %copy-done.24, bf16[4,2,64,512]{3,2,1,0:T(8,128)(2,1)} %get-tuple-element.389.do_ref, f32[4,2,128,128]{3,2,1,0:T(8,128)S(1)} %copy-done.40, ...), custom_call_target="tpu_custom_call" | custom-call | tf_op jit(solution)/shard_map/cond/branch_1_fun/attend_back/pallas_call | solution.py:198
  571.4 11.1 %collective-permute-done.5 = bf16[512,512]{1,0:T(8,128)(2,1)S(1)} collective-permute-done((bf16[512,512]{1,0:T(8,128)(2,1)S(1)}, bf16[512,512]{1,0:T(8,128)(2,1)S(1)}, u32[]{:S(2)}, u32[]{:S(2)}) %collective-permute-start.5) | collective-permute-done | bytes 524320 | tf_op jit(solution)/shard_map/cond/branch_1_fun/ppermute | solution.py:667
  587.1 10.9 %collective-permute-done.6 = bf16[512,512]{1,0:T(8,128)(2,1)S(1)} collective-permute-done((bf16[512,512]{1,0:T(8,128)(2,1)S(1)}, bf16[512,512]{1,0:T(8,128)(2,1)S(1)}, u32[]{:S(2)}, u32[]{:S(2)}) %collective-permute-start.6) | collective-permute-done | bytes 524320 | tf_op jit(solution)/shard_map/cond/branch_1_fun/ppermute | solution.py:667
  602.0 10.7 %collective-permute-done.7 = bf16[512,512]{1,0:T(8,128)(2,1)S(1)} collective-permute-done((bf16[512,512]{1,0:T(8,128)(2,1)S(1)}, bf16[512,512]{1,0:T(8,128)(2,1)S(1)}, u32[]{:S(2)}, u32[]{:S(2)}) %collective-permute-start.7) | collective-permute-done | bytes 524320 | tf_op jit(solution)/shard_map/cond/branch_1_fun/ppermute | solution.py:667
  631.2 14.9 %pick.7 = bf16[32,128,2304]{2,1,0:T(8,128)(2,1)} custom-call(s32[32]{0:T(128)} %get-tuple-element.394.which_ref, s32[32]{0:T(128)} %get-tuple-element.393.slot_ref, bf16[24,128,2304]{2,1,0:T(8,128)(2,1)} %bitcast.450, bf16[24,128,2304]{2,1,0:T(8,128)(2,1)} %bitcast.24.refs_1_), custom_call_target="tpu_custom_call" | custom-call | tf_op jit(solution)/shard_map/cond/branch_1_fun/pick/pallas_call | solution.py:393
  651.7 10.4 %multiply_reduce_fusion = (f32[128]{0:T(128)S(1)}, f32[2304]{0:T(1024)S(1)}, f32[128,2304]{1,0:T(8,128)}) fusion(f32[128,2304]{1,0:T(8,128)S(1)} %get-tuple-element.157, f32[2304]{0:T(1024)S(1)} %copy-done.46, f32[128]{0:T(128)S(1)} %add_rsqrt_fusion, bf16[128,4096]{0,1:T(8,128)(2,1)S(1)} %bitcast.454, bf16[4096,2304]{1,0:T(8,128)(2,1)} %bitcast.447), kind=kOutput, calls=%fused_computation.4 | convolution fusion | flops 2417686272 | bytes 22301696 | tf_op jit(solution)/shard_map/cond/branch_1_fun/dot_general | solution.py:48
  663.4 27.6 %all-to-all-start.2 = ((bf16[8,128,768]{1,2,0:T(8,128)(2,1)}), bf16[8,128,768]{1,2,0:T(8,128)(2,1)}, u32[]{:S(2)}, u32[]{:S(2)}) async-start(bf16[8,128,768]{1,2,0:T(8,128)(2,1)} %bitcast.462), calls=%async_computation.2 | async-start | bytes 3145728 | tf_op jit(solution)/shard_map/cond/branch_1_fun/all_to_all | solution.py:970
  697.6 20.5 %collective-permute-done.13 = f32[4,2304]{1,0:T(4,128)S(1)} collective-permute-done((f32[4,2304]{1,0:T(4,128)S(1)}, f32[4,2304]{1,0:T(4,128)S(1)}, u32[]{:S(2)}, u32[]{:S(2)}) %collective-permute-start.13) | collective-permute-done | bytes 36896 | tf_op jit(solution)/shard_map/cond/branch_1_fun/ppermute | solution.py:718
  734.5 16.0 %weight_grad.1 = bf16[768,2304]{1,0:T(8,128)(2,1)} custom-call(s32[17]{0:T(128)} %stack.121.place_ref, bf16[1024,768]{1,0:T(8,128)(2,1)} %bitcast.463, bf16[128,2304]{1,0:T(8,128)(2,1)} %get-tuple-element.144.refs_0_, bf16[128,2304]{1,0:T(8,128)(2,1)} %get-tuple-element.145.refs_1_, bf16[128,2304]{1,0:T(8,128)(2,1)} %get-tuple-element.146.refs_2_, ...), custom_call_target="tpu_custom_call" | custom-call | tf_op jit(solution)/shard_map/cond/branch_1_fun/weight_grad/pallas_call | solution.py:629
  756.2 24.9 %collective-permute-done.69 = bf16[2,192,1152]{2,1,0:T(8,128)(2,1)S(1)} collective-permute-done((bf16[2,192,1152]{2,1,0:T(8,128)(2,1)S(1)}, bf16[2,192,1152]{2,1,0:T(8,128)(2,1)S(1)}, u32[]{:S(2)}, u32[]{:S(2)}) %collective-permute-start.69) | collective-permute-done | bytes 884768 | tf_op jit(solution)/shard_map/ppermute | solution.py:680
  784.9 8.2 collective-permute-done.70
  (520 shorter events, 449.6 us)
Async XLA Ops:
  7.2 50.2 %all-gather.9.cloned.1.call-start = ((), (), s32[]{:S(2)}) async-start(), calls=%async_computation.4 | async-start | bytes 2949120 | tf_op jit(solution)/shard_map/all_gather | solution.py:759
  7.9 142.2 %all-gather.7.cloned.1.call-start = ((), (), s32[]{:S(2)}) async-start(), calls=%async_computation.3 | async-start | bytes 4718592 | tf_op jit(solution)/shard_map/all_gather | solution.py:784
  85.4 317.0 %all-gather.11.cloned.1.call-start = ((), (), s32[]{:S(2)}) async-start(), calls=%async_computation.5 | async-start | bytes 17694720 | tf_op jit(solution)/shard_map/all_gather | solution.py:825
  99.2 76.6 %collective-permute-start.26 = (bf16[1,256,2304]{2,1,0:T(8,128)(2,1)}, bf16[1,256,2304]{2,1,0:T(8,128)(2,1)}, u32[]{:S(2)}, u32[]{:S(2)}) collective-permute-start(bf16[1,256,2304]{2,1,0:T(8,128)(2,1)} %get-tuple-element.413), channel_id=1, source_target_pairs={{4,6},{27,25}} | collective-permute-start | bytes 3538952 | tf_op jit(solution)/shard_map/ppermute | solution.py:460
  100.9 74.9 %collective-permute-start.27 = (bf16[1,256,2304]{2,1,0:T(8,128)(2,1)}, bf16[1,256,2304]{2,1,0:T(8,128)(2,1)}, u32[]{:S(2)}, u32[]{:S(2)}) collective-permute-start(bf16[1,256,2304]{2,1,0:T(8,128)(2,1)} %get-tuple-element.411), channel_id=1, source_target_pairs={{4,6},{27,25}} | collective-permute-start | bytes 3538952 | tf_op jit(solution)/shard_map/ppermute | solution.py:460
  102.6 48.8 %collective-permute-start.24 = (bf16[1,256,2304]{2,1,0:T(8,128)(2,1)S(1)}, bf16[1,256,2304]{2,1,0:T(8,128)(2,1)S(1)}, u32[]{:S(2)}, u32[]{:S(2)}) collective-permute-start(bf16[1,256,2304]{2,1,0:T(8,128)(2,1)S(1)} %collective-permute-done.22.refs_8_.refs_11_), channel_id=1, source_target_pairs={{0,1},{1,0},{2,3},{3,2},{4,5},{5,4},{6,7},{7,6},{8,9},{9,8},{10,11... | collective-permute-start | bytes 3538952 | tf_op jit(solution)/shard_map/ppermute | solution.py:471
  150.1 24.8 %collective-permute-start.21 = (bf16[128,2304]{1,0:T(8,128)(2,1)}, bf16[128,2304]{1,0:T(8,128)(2,1)}, u32[]{:S(2)}, u32[]{:S(2)}) collective-permute-start(bf16[128,2304]{1,0:T(8,128)(2,1)} %multiply_convert_fusion.7), channel_id=1, source_target_pairs={{0,2},{1,3},{2,6},{3,7},{4,0},{5,1},{6,4},{7,5},{8,10},{9,11},{10,... | collective-permute-start | bytes 1769480 | tf_op jit(solution)/shard_map/ppermute | solution.py:558
  176.4 27.8 %collective-permute-start.25 = (bf16[128,2304]{1,0:T(8,128)(2,1)}, bf16[128,2304]{1,0:T(8,128)(2,1)}, u32[]{:S(2)}, u32[]{:S(2)}) collective-permute-start(bf16[128,2304]{1,0:T(8,128)(2,1)} %collective-permute-done.21), channel_id=1, source_target_pairs={{0,2},{1,3},{2,6},{3,7},{4,0},{5,1},{6,4},{7,5},{8,10},{9,11},{10,... | collective-permute-start | bytes 1769480 | tf_op jit(solution)/shard_map/ppermute | solution.py:558
  209.7 23.8 %collective-permute-start.30 = (bf16[128,2304]{1,0:T(8,128)(2,1)}, bf16[128,2304]{1,0:T(8,128)(2,1)}, u32[]{:S(2)}, u32[]{:S(2)}) collective-permute-start(bf16[128,2304]{1,0:T(8,128)(2,1)} %collective-permute-done.25), channel_id=1, source_target_pairs={{0,2},{1,3},{2,6},{3,7},{4,0},{5,1},{6,4},{7,5},{8,10},{9,11},{10,... | collective-permute-start | bytes 1769480 | tf_op jit(solution)/shard_map/ppermute | solution.py:558
  253.3 541.7 %all-reduce.3.cloned.1.call-start = ((), (), s32[]{:S(2)}) async-start(), calls=%async_computation.6 | async-start | bytes 31850496 | tf_op jit(solution)/shard_map/psum | solution.py:900
  273.2 27.0 %collective-permute-start.42 = (bf16[128,2304]{1,0:T(8,128)(2,1)S(1)}, bf16[128,2304]{1,0:T(8,128)(2,1)S(1)}, u32[]{:S(2)}, u32[]{:S(2)}) collective-permute-start(bf16[128,2304]{1,0:T(8,128)(2,1)S(1)} %add_convert_fusion.6), channel_id=1, source_target_pairs={{0,2},{1,3},{2,6},{3,7},{4,0},{5,1},{6,4},{7,5},{8,10},{9,11},{10,... | collective-permute-start | bytes 1769480 | tf_op jit(solution)/shard_map/ppermute | solution.py:853
  373.7 27.7 %collective-permute-start.57 = (bf16[128,2304]{1,0:T(8,128)(2,1)S(1)}, bf16[128,2304]{1,0:T(8,128)(2,1)S(1)}, u32[]{:S(2)}, u32[]{:S(2)}) collective-permute-start(bf16[128,2304]{1,0:T(8,128)(2,1)S(1)} %add_convert_fusion.2), channel_id=1, source_target_pairs={{0,2},{1,3},{2,6},{3,7},{4,0},{5,1},{6,4},{7,5},{8,10},{9,11},{10,... | collective-permute-start | bytes 1769480 | tf_op jit(solution)/shard_map/ppermute | solution.py:853
  506.0 29.5 %all-to-all-start = ((bf16[4,2,64,1024]{3,2,1,0:T(8,128)(2,1)}), bf16[4,2,64,1024]{3,2,1,0:T(8,128)(2,1)S(1)}, u32[]{:S(2)}, u32[]{:S(2)}) async-start(bf16[4,2,64,1024]{3,2,1,0:T(8,128)(2,1)} %pad_maximum_fusion.1), calls=%async_computation | async-start | bytes 2097152 | tf_op jit(solution)/shard_map/cond/branch_1_fun/all_to_all | solution.py:922
  615.3 34.1 %all-to-all-start.1 = ((bf16[4,2,64,1024]{3,2,1,0:T(8,128)(2,1)}), bf16[4,2,64,1024]{3,2,1,0:T(8,128)(2,1)}, u32[]{:S(2)}, u32[]{:S(2)}) async-start(bf16[4,2,64,1024]{3,2,1,0:T(8,128)(2,1)} %pad_maximum_fusion.2), calls=%async_computation.1 | async-start | bytes 2097152 | tf_op jit(solution)/shard_map/cond/branch_1_fun/all_to_all | solution.py:942
  619.7 27.7 %collective-permute-start = (bf16[128,2304]{1,0:T(8,128)(2,1)S(1)}, bf16[128,2304]{1,0:T(8,128)(2,1)}, u32[]{:S(2)}, u32[]{:S(2)}) collective-permute-start(bf16[128,2304]{1,0:T(8,128)(2,1)S(1)} %multiply_convert_fusion.refs_8_), channel_id=1, source_target_pairs={{2,4},{3,5},{4,6},{5,7},{10,12},{11,13},{12,14},{13,15},{18,20},{1... | collective-permute-start | bytes 1769480 | tf_op jit(solution)/shard_map/cond/branch_1_fun/ppermute | solution.py:570
  621.2 26.3 %collective-permute-start.1 = (bf16[128,2304]{1,0:T(8,128)(2,1)S(1)}, bf16[128,2304]{1,0:T(8,128)(2,1)}, u32[]{:S(2)}, u32[]{:S(2)}) collective-permute-start(bf16[128,2304]{1,0:T(8,128)(2,1)S(1)} %multiply_convert_fusion.refs_8_), channel_id=1, source_target_pairs={{0,4},{1,5},{2,6},{3,7},{8,12},{9,13},{10,14},{11,15},{16,20},{17,... | collective-permute-start | bytes 1769480 | tf_op jit(solution)/shard_map/cond/branch_1_fun/ppermute | solution.py:570
  663.4 67.7 %all-to-all-start.2 = ((bf16[8,128,768]{1,2,0:T(8,128)(2,1)}), bf16[8,128,768]{1,2,0:T(8,128)(2,1)}, u32[]{:S(2)}, u32[]{:S(2)}) async-start(bf16[8,128,768]{1,2,0:T(8,128)(2,1)} %bitcast.462), calls=%async_computation.2 | async-start | bytes 3145728 | tf_op jit(solution)/shard_map/cond/branch_1_fun/all_to_all | solution.py:970
  694.9 23.3 %collective-permute-start.13 = (f32[4,2304]{1,0:T(4,128)S(1)}, f32[4,2304]{1,0:T(4,128)S(1)}, u32[]{:S(2)}, u32[]{:S(2)}) collective-permute-start(f32[4,2304]{1,0:T(4,128)S(1)} %fusion.7), channel_id=1, source_target_pairs={{0,2},{1,3},{2,0},{3,1},{4,6},{5,7},{6,4},{7,5},{8,10},{9,11},{10,... | collective-permute-start | bytes 110600 | tf_op jit(solution)/shard_map/cond/branch_1_fun/ppermute | solution.py:718
  696.6 37.0 %collective-permute-start.10 = (bf16[128,2304]{1,0:T(8,128)(2,1)}, bf16[128,2304]{1,0:T(8,128)(2,1)S(1)}, u32[]{:S(2)}, u32[]{:S(2)}) collective-permute-start(bf16[128,2304]{1,0:T(8,128)(2,1)} %collective-permute-done.1.refs_12_), channel_id=1, source_target_pairs={{0,1},{1,0},{2,3},{3,2},{4,5},{5,4},{6,7},{7,6},{8,9},{9,8},{10,11... | collective-permute-start | bytes 1769480 | tf_op jit(solution)/shard_map/cond/branch_1_fun/ppermute | solution.py:588
  696.7 37.0 %collective-permute-start.11 = (bf16[128,2304]{1,0:T(8,128)(2,1)}, bf16[128,2304]{1,0:T(8,128)(2,1)}, u32[]{:S(2)}, u32[]{:S(2)}) collective-permute-start(bf16[128,2304]{1,0:T(8,128)(2,1)} %collective-permute-done.2.refs_14_), channel_id=1, source_target_pairs={{0,1},{1,0},{2,3},{3,2},{4,5},{5,4},{6,7},{7,6},{8,9},{9,8},{10,11... | collective-permute-start | bytes 1769480 | tf_op jit(solution)/shard_map/cond/branch_1_fun/ppermute | solution.py:588
  697.1 36.5 %collective-permute-start.8 = (bf16[128,2304]{1,0:T(8,128)(2,1)S(1)}, bf16[128,2304]{1,0:T(8,128)(2,1)}, u32[]{:S(2)}, u32[]{:S(2)}) collective-permute-start(bf16[128,2304]{1,0:T(8,128)(2,1)S(1)} %multiply_convert_fusion.refs_8_), channel_id=1, source_target_pairs={{0,1},{1,0},{2,3},{3,2},{4,5},{5,4},{6,7},{7,6},{8,9},{9,8},{10,11... | collective-permute-start | bytes 1769480 | tf_op jit(solution)/shard_map/cond/branch_1_fun/ppermute | solution.py:588
  697.2 36.5 %collective-permute-start.9 = (bf16[128,2304]{1,0:T(8,128)(2,1)}, bf16[128,2304]{1,0:T(8,128)(2,1)}, u32[]{:S(2)}, u32[]{:S(2)}) collective-permute-start(bf16[128,2304]{1,0:T(8,128)(2,1)} %collective-permute-done.refs_10_), channel_id=1, source_target_pairs={{0,1},{1,0},{2,3},{3,2},{4,5},{5,4},{6,7},{7,6},{8,9},{9,8},{10,11... | collective-permute-start | bytes 1769480 | tf_op jit(solution)/shard_map/cond/branch_1_fun/ppermute | solution.py:588
  752.8 28.3 %collective-permute-start.69 = (bf16[2,192,1152]{2,1,0:T(8,128)(2,1)S(1)}, bf16[2,192,1152]{2,1,0:T(8,128)(2,1)S(1)}, u32[]{:S(2)}, u32[]{:S(2)}) collective-permute-start(bf16[2,192,1152]{2,1,0:T(8,128)(2,1)S(1)} %pad_maximum_fusion.10), channel_id=1, source_target_pairs={{0,16},{8,24},{16,0},{24,8},{1,17},{9,25},{17,1},{25,9},{2,18},{10... | collective-permute-start | bytes 2654216 | tf_op jit(solution)/shard_map/ppermute | solution.py:680
  754.6 28.1 %collective-permute-start.67 = (bf16[2,192,1152]{2,1,0:T(8,128)(2,1)S(1)}, bf16[2,192,1152]{2,1,0:T(8,128)(2,1)S(1)}, u32[]{:S(2)}, u32[]{:S(2)}) collective-permute-start(bf16[2,192,1152]{2,1,0:T(8,128)(2,1)S(1)} %pad_maximum_fusion.11), channel_id=1, source_target_pairs={{0,8},{8,0},{16,24},{24,16},{1,9},{9,1},{17,25},{25,17},{2,10},{10... | collective-permute-start | bytes 2654216 | tf_op jit(solution)/shard_map/ppermute | solution.py:680
  (144 other events, 1872.3 us)
Sparse Core Ops, SparseCore 0:
  9.8 40.1 all-gather.8
  85.6 64.3 all-gather.6
  253.5 137.1 all-gather.10
  444.1 325.0 all-reduce.2

commit v5 on v4

--- a/solution.py
+++ b/solution.py
@@ -57,14 +57,18 @@
     return jnp.concatenate([block[:, h * HD : (h + 1) * HD] for h in range(heads)], axis=0)
 
 
-def visible_of(block, own, shard, rows, keys, lines):
+def visible_of(shard, rows, keys, lines):
     shape = (lines, keys)
     row = lax.broadcasted_iota(jnp.int32, shape, 0) & (rows - 1)
     col = lax.broadcasted_iota(jnp.int32, shape, 1)
-    return block * keys + col <= own * keys + shard * rows + row
-
-
-def attend_kernel(shard_ref, q_ref, kv_ref, o_ref, lse_ref, score_ref):
+    return col <= shard * rows + row
+
+
+def lane_sums(values):
+    return sum(values[:, low : low + 128] for low in range(0, values.shape[1], 128))
+
+
+def attend_kernel(shard_ref, q_ref, kv_ref, o_ref, lse_ref, weight_ref):
     own = pl.program_id(1)
     shard = shard_ref[0]
     parts, _, _, rows, _ = kv_ref.shape
@@ -72,33 +76,31 @@
     queries = stacked_heads(q_ref[0, 0])
     lines = queries.shape[0]
 
-    def score_step(block, top):
+    def exponentials(block):
         key_block = kv_ref[:, block, 0, :, :HD].reshape(keys, HD)
-        raw = dot_nt(queries, key_block) * HD ** (-0.5)
-        capped = soft_cap * jnp.tanh(raw / soft_cap)
-        capped = jnp.where(visible_of(block, own, shard, rows, keys, lines), capped, -1e30)
-        score_ref[block] = capped
-        return jnp.maximum(top, jnp.max(capped, axis=-1, keepdims=True))
-
-    top = lax.fori_loop(0, own + 1, score_step, jnp.full((lines, 1), -3e38, f32))
-
-    def sum_step(block, total):
-        expanded = jnp.exp(score_ref[block] - top)
-        score_ref[block] = expanded
-        return total + jnp.sum(expanded, axis=-1, keepdims=True)
-
-    total = lax.fori_loop(0, own + 1, sum_step, jnp.zeros((lines, 1), f32))
+        bounded = jnp.tanh(dot_nt(queries, key_block) * (HD ** (-0.5) / soft_cap))
+        return jnp.exp(soft_cap * bounded)
+
+    def score_step(block, total):
+        expanded = exponentials(block)
+        weight_ref[block] = expanded
+        return total + lane_sums(expanded)
+
+    total = lax.fori_loop(0, own, score_step, jnp.zeros((lines, 128), f32))
+    expanded = jnp.where(visible_of(shard, rows, keys, lines), exponentials(own), 0.0)
+    weight_ref[own] = expanded
+    total = jnp.sum(total + lane_sums(expanded), axis=-1, keepdims=True)
     inverse = 1.0 / total
 
     def mix_step(block, mixed):
-        weights = (score_ref[block] * inverse).astype(bf16)
+        weights = (weight_ref[block] * inverse).astype(bf16)
         value_block = kv_ref[:, block, 0, :, HD:].reshape(keys, HD)
         return mixed + dot_nn(weights, value_block)
 
     mixed = lax.fori_loop(0, own + 1, mix_step, jnp.zeros((lines, HD), f32))
     for h in range(lines // rows):
         o_ref[0, 0, :, h * HD : (h + 1) * HD] = mixed[h * rows : (h + 1) * rows].astype(bf16)
-    lse_ref[0, 0] = jnp.broadcast_to(top + jnp.log(total), (lines, 128))
+    lse_ref[0, 0] = jnp.broadcast_to(jnp.log(total), (lines, 128))
 
 
 def attend_back_kernel(
@@ -117,21 +119,26 @@
     def _():
         acc_ref[...] = jnp.zeros_like(acc_ref)
 
-    def first_step(block, delta):
+    def first_part(block, masked):
         key_block = kv_ref[:, block, 0, :, :HD].reshape(keys, HD)
         value_block = kv_ref[:, block, 0, :, HD:].reshape(keys, HD)
         bounded = jnp.tanh(dot_nt(queries, key_block) * (HD ** (-0.5) / soft_cap))
-        capped = jnp.where(
-            visible_of(block, own, shard, rows, keys, lines), soft_cap * bounded, -1e30
-        )
-        weights = jnp.exp(capped - lse)
+        weights = jnp.exp(soft_cap * bounded - lse)
+        if masked:
+            weights = jnp.where(visible_of(shard, rows, keys, lines), weights, 0.0)
         grad_weights = dot_nt(grads, value_block)
         acc_ref[block, :, HD:] += dot_tn(weights.astype(bf16), grads)
         weight_ref[block] = weights * (1.0 - bounded * bounded)
         dp_ref[block] = grad_weights
-        return delta + jnp.sum(weights * grad_weights, axis=-1, keepdims=True)
-
-    delta = lax.fori_loop(0, own + 1, first_step, jnp.zeros((lines, 1), f32))
+        return lane_sums(weights * grad_weights)
+
+    delta = lax.fori_loop(
+        0,
+        own,
+        lambda block, delta: delta + first_part(block, False),
+        jnp.zeros((lines, 128), f32),
+    )
+    delta = jnp.sum(delta + first_part(own, True), axis=-1, keepdims=True)
 
     def second_step(block, grad_query):
         key_block = kv_ref[:, block, 0, :, :HD].reshape(keys, HD)
@@ -139,9 +146,7 @@
         acc_ref[block, :, :HD] += dot_tn(grad_raw, queries)
         return grad_query + dot_nn(grad_raw, key_block)
 
-    grad_query = lax.fori_loop(
-        0, own + 1, second_step, jnp.zeros((lines, HD), f32)
-    ) * HD ** (-0.5)
+    grad_query = lax.fori_loop(0, own + 1, second_step, jnp.zeros((lines, HD), f32)) * HD ** (-0.5)
     for h in range(lines // rows):
         dq_ref[0, 0, :, h * HD : (h + 1) * HD] = grad_query[h * rows : (h + 1) * rows].astype(bf16)
 
@@ -601,20 +606,20 @@
             piece, rows_ref.at[i // half, pl.ds(start, lines)], sems.at[i]
         ).start()
     limit = place_ref[2 * half]
-    turned = cols_ref[...].T
-    col = lax.broadcasted_iota(jnp.int32, turned.shape, 0)
-    turned_ref[0] = jnp.where(col < limit, turned, 0)
-    turned_ref[1] = jnp.where(col < limit, 0, turned)
+    turned_ref[...] = cols_ref[...].T
     for i, piece in enumerate(pieces):
         pltpu.make_async_copy(piece, rows_ref.at[0, pl.ds(0, lines)], sems.at[i]).wait()
-    width = out_ref.shape[1]
+    height, width = out_ref.shape
     step = width // 3 if width % 384 == 0 else width
+    block = HD if height % HD == 0 else HALF
 
     def chunk(n, carry):
         cut = pl.ds(pl.multiple_of(n * step, step), step)
-        total = dot_nn(turned_ref[0], rows_ref[0, :, cut])
-        total += dot_nn(turned_ref[1], rows_ref[1, :, cut])
-        out_ref[:, cut] = total.astype(bf16)
+        for low in range(0, height, block):
+            which = (low >= limit).astype(jnp.int32)
+            out_ref[low : low + block, cut] = dot_nn(
+                turned_ref[low : low + block], rows_ref[which, :, cut]
+            ).astype(bf16)
         return carry
 
     lax.fori_loop(0, width // step, chunk, 0)
@@ -636,7 +641,7 @@
             out_specs=pl.BlockSpec(memory_space=pltpu.VMEM),
             scratch_shapes=[
                 pltpu.VMEM((2, half * lines, width), bf16),
-                pltpu.VMEM((2, cols.shape[1], cols.shape[0]), bf16),
+                pltpu.VMEM((cols.shape[1], cols.shape[0]), bf16),
                 pltpu.SemaphoreType.DMA((2 * half,)),
             ],
         ),
@@ -672,30 +677,36 @@
     return [(c, c ^ bit) for c in range(columns)]
 
 
-def column_scatter(parts):
+def column_scatter(parts, beside=None):
     half = parts.shape[-1] // 2
+    ways = ((1, 2, slice(0, half)), (2, 1, slice(half, None)))
+    come = tuple(
+        lax.ppermute(
+            jnp.concatenate([parts[first : first + 1, ..., cut], parts[3:, ..., cut]], axis=0),
+            "seq",
+            partners(4, first),
+        )
+        for first, _, cut in ways
+    )
+    if beside:
+        come = beside(come)
     done = []
-    for first, second, cut in ((1, 2, slice(0, half)), (2, 1, slice(half, None))):
-        low = parts[..., cut]
-        got = lax.ppermute(
-            jnp.concatenate([low[first : first + 1], low[3:]], axis=0), "seq", partners(4, first)
-        )
-        keep = low[0].astype(f32) + got[0].astype(f32)
-        away = low[second].astype(f32) + got[1].astype(f32)
+    for (first, second, cut), got in zip(ways, come):
+        keep = parts[0, ..., cut].astype(f32) + got[0].astype(f32)
+        away = parts[second, ..., cut].astype(f32) + got[1].astype(f32)
         done.append(
             keep + lax.ppermute(away.astype(bf16), "seq", partners(4, second)).astype(f32)
         )
     return jnp.concatenate(done, axis=-1)
 
 
-def column_total(value, column, later):
+def column_total(value, column, beside, later):
     rows, width = value.shape
     step, half = rows // 4, width // 2
     parts = jnp.stack(
         [lax.dynamic_slice_in_dim(value, (column ^ k) * step, step, 0) for k in range(4)]
     )
-    own = column_scatter(parts).astype(bf16)
-    own, *later = lax.optimization_barrier((own, *later))
+    own, *later = beside(column_scatter(parts, beside).astype(bf16), *later)
     pieces = (own[:, :half], own[:, half:])
     near = tuple(lax.ppermute(p, "seq", partners(4, bit)) for p, bit in zip(pieces, (1, 2)))
     near, *later = lax.optimization_barrier((near, *later))
@@ -829,8 +840,9 @@
     chips, ring, _ = ring_tables(shards)
     weight_gate_up, weight_down = ffn_weight[:, :2], ffn_weight[:, 2]
 
-    def pipeline(block, work, aside, before_last):
+    def pipeline(block, work, aside, late):
         held = block
+        pairs = []
         for t in range(chips):
             rows_here = jnp.concatenate([held, lax.ppermute(held, "fsdp", swap)], axis=0)
             if t + 1 < chips:
@@ -838,20 +850,20 @@
             made = work(t, rows_here).astype(bf16)
             got = lax.ppermute(made[own_rows:], "fsdp", swap)
             pair = made[:own_rows].astype(f32) + got.astype(f32)
-            if t == 0:
-                first = pair
-            else:
-                total = pair if t == 1 else total + pair
+            pairs.append(pair)
             if t + 1 < chips:
                 held, made = aside(t, *lax.optimization_barrier((held, made)))
-            if t:
-                total = total.astype(bf16)
+            if t and not late:
+                total = (pair if t == 1 else total + pair).astype(bf16)
                 if t + 1 < chips:
                     held, total = lax.optimization_barrier((held, total))
-                else:
-                    total = before_last(total)
                 total = lax.ppermute(total, "fsdp", ring).astype(f32)
-        return total + first
+        if late:
+            total, _ = lax.optimization_barrier((pairs[1].astype(bf16), held))
+            total = lax.ppermute(total, "fsdp", ring).astype(f32)
+            for pair in pairs[2:]:
+                total = lax.ppermute((total + pair).astype(bf16), "fsdp", ring).astype(f32)
+        return total + pairs[0]
 
     saved = []
 
@@ -863,9 +875,7 @@
         saved.append((rows_here, gate_up, hidden))
         return dot_nn(hidden, weight_down)
 
-    ffn_out = pipeline(
-        normed_ffn, forward, lambda t, held, made: (held, made), lambda total: total
-    )
+    ffn_out = pipeline(normed_ffn, forward, lambda t, held, made: (held, made), False)
     result = residual + rms_scale(ffn_out, gain_rows[3])
     block_out = result.astype(bf16).reshape(tokens.shape)
     grad_ffn, gain_terms = norm_back(ffn_out, gain_rows[3], flat_cot)
@@ -887,16 +897,11 @@
             held, made, kept["lanes"] = lax.optimization_barrier((held, made, kept["lanes"]))
         return held, made
 
-    def units_after(total):
-        total, units = lax.optimization_barrier((total, [part for _, part in back]))
-        kept["units"] = units
-        return total
-
-    grad_normed_ffn = pipeline(grad_ffn.astype(bf16), backward, backward_aside, units_after)
+    grad_normed_ffn = pipeline(grad_ffn.astype(bf16), backward, backward_aside, True)
     ffn_in = jnp.concatenate([rows_here for rows_here, _, _ in saved], axis=0)
     hidden = jnp.concatenate([units for _, _, units in saved], axis=0)
     grad_ffn_all = jnp.concatenate([grads_here for grads_here, _ in back], axis=0)
-    units = jnp.concatenate(kept["units"], axis=0)
+    units = jnp.concatenate([part for _, part in back], axis=0)
     gate_grad, up_grad, down_grad = lax.psum(
         (
             dot_tn(units[:, 0], ffn_in).astype(bf16),
@@ -906,10 +911,12 @@
         "seq",
     )
 
+    other_lanes = lax.ppermute(kept["lanes"], "fsdp", swap)
+    weight_out_all = all_columns(kept["lanes"], other_lanes, per + 2, 2 * per + 2)
+    grad_normed_ffn, weight_out_all = lax.optimization_barrier((grad_normed_ffn, weight_out_all))
+
     def attention_back():
-        other_lanes = lax.ppermute(kept["lanes"], "fsdp", swap)
         weight_in_all = all_columns(kept["lanes"], other_lanes, 0, per + 2)
-        weight_out_all = all_columns(kept["lanes"], other_lanes, per + 2, 2 * per + 2)
         grad_mid, gain_pre_ffn = norm_back(residual, gain_rows[2], grad_normed_ffn)
         grad_residual = flat_cot + grad_mid
         grad_attn, gain_post_attn = norm_back(attn_out, gain_rows[1], grad_residual)
@@ -984,34 +991,44 @@
                 gain_last,
             ]
         )
-        gain_grad = lax.dynamic_slice_in_dim(
-            sum_over(gain_grad, "fsdp", shards),
-            shard * norm_gains.shape[1],
-            norm_gains.shape[1],
-            1,
-        )
         return attn_grad, gain_grad, token_grad
 
     def nothing():
         return (
             jnp.zeros(attn_weight.shape, bf16),
-            jnp.zeros(norm_gains.shape, f32),
+            jnp.zeros((norm_gains.shape[0], width), f32),
             jnp.zeros(tokens.shape, f32),
         )
 
     attn_grad, gain_grad, token_grad = lax.cond(
         shard < 2**20, attention_back, nothing
     )
-    gain_total = sum_over(gain_grad, "seq", columns)
+    gain_grad = lax.dynamic_slice_in_dim(
+        sum_over(gain_grad, "fsdp", shards),
+        shard * norm_gains.shape[1],
+        norm_gains.shape[1],
+        1,
+    )
     if columns == 4:
+
+        def with_gains(*come):
+            nonlocal gain_grad
+            if len(come) == 1:
+                gain_grad = sum_over(gain_grad, "seq", columns)
+                come, gain_grad = lax.optimization_barrier((come[0], gain_grad))
+                return come
+            return lax.optimization_barrier(come)
+
         attn_total, gate_grad, up_grad, down_grad = column_total(
-            attn_grad, column, (gate_grad, up_grad, down_grad)
+            attn_grad, column, with_gains, (gate_grad, up_grad, down_grad)
         )
     else:
         attn_grad, gate_grad, up_grad, down_grad = lax.optimization_barrier(
             (attn_grad, gate_grad, up_grad, down_grad)
         )
         attn_total = lax.psum(attn_grad, "seq").astype(f32)
+        gain_grad = sum_over(gain_grad, "seq", columns)
+    gain_total = gain_grad
     ffn_grad = widen_plane(down_grad, 2, 3, None)
     ffn_grad = widen_plane(gate_grad, 0, 3, ffn_grad)
     ffn_grad = widen_plane(up_grad, 1, 3, ffn_grad)

time: 858 us -> 836 us (0.974)
  starting transfers between devices: 180 us -> 160 us
  waiting for transfers between devices: 234 us -> 245 us
    all_to_all x1, waiting for transfers between devices: 0.01 us -> 24.8 us  [attention_back(): lax.all_to_all(weight_cols.reshape(own_rows, shards, shard_cols).transpos...]
    ppermute x5 -> x7, waiting for transfers between devices: 43.8 us -> 24 us  [the longest x2 18.9 us: pipeline(): total = lax.ppermute((total + pair).astype(bf16), 'fsdp', ring).astype(f32)]
    ppermute x6 -> x4, waiting for transfers between devices: 50.5 us -> 40.4 us  [pipeline(): total = lax.ppermute(total, 'fsdp', ring).astype(f32)]
    ppermute x6, waiting for transfers between devices: 5.54 us -> 15 us  [pipeline(): held = lax.ppermute(held, 'fsdp', ring)]
    unnamed x144 -> x163, local copies, waits for them, and re-layouts: 17.5 us -> 15.9 us
  transfers between devices with their start and end apart: 84 -> 84, of which waited for: 34 -> 37; matrix products, arithmetic and copies ran while one was open for 26% -> 28% of each run, Pallas kernels for 15% -> 15%
where the time goes in v5:
time: 836 us; the launch traced here: 825 us
  waiting for transfers between devices  245 us (29%)
  starting transfers between devices  160 us (19%)
  matrix products  132 us (16%)
  Pallas kernels  122 us (15%)
  local copies, waits for them, and re-layouts  64.3 us (8%)
  other arithmetic  57.6 us (7%)
  between operations  18.2 us (2%)
  blocking collectives  15.7 us (2%)
  loops' own time  10.5 us (1%)
    pallas_call x9, Pallas kernels, pick(): pl.pallas_call(functools.partial(kernel, cands), grid_spec=pltpu.Prefetch...  61.5 us
    ppermute x4, starting transfers between devices, routed_weights(): sources['swapped%d' % number] = lax.ppermute(got, 'fsdp', swap)  52.8 us
    ppermute x4, waiting for transfers between devices, pipeline(): total = lax.ppermute(total, 'fsdp', ring).astype(f32)  40.4 us
    ppermute x3, waiting for transfers between devices, ring_scatter(): lax.ppermute(total.astype(bf16), 'fsdp', pairs).astype(f32)  34.6 us
    dot_general x5, matrix products, dot_nn(): lax.dot_general(a, b, (((1,), (0,)), ((), ())), preferred_element_type=f32)  31.7 us
    ppermute x5, waiting for transfers between devices, sum_over(): lax.ppermute(value, axis, [(c, c ^ bit) for c in range(count)])  30 us
    dot_general x4, matrix products, forward(): jnp.einsum('td,fgd->tgf', rows_here, weight_gate_up, preferred_element_ty...  28.9 us
    all_to_all x1, waiting for transfers between devices, attention_back(): lax.all_to_all(jnp.concatenate([grad_mixed.transpose(2, 0, 1, 3), mixed],...  25.9 us
  transfers between devices with their start and end apart: 84, of which 37 were waited for; matrix products, arithmetic and copies ran while one was open for 28% of the time, Pallas kernels for 15%

profile of v5, /device:TPU:0, one launch (start us, length us, event | category | flops | bytes accessed | tf_op | source)
XLA Modules:
  0.0 824.7 jit_solution(5115681003041768754)
XLA Ops:
  8.0 15.7 %all-gather.2 = bf16[8,288,4]{1,2,0:T(4,128)(2,1)S(1)} all-gather(bf16[1,288,4]{1,2,0:T(4,128)(2,1)} %bitcast.493), channel_id=1, replica_groups=mesh['seq'=4,'fsdp'=8] {'fsdp'}, dimensions={0}, use_global_device_ids=true | all-gather | bytes 20736 | tf_op jit(solution)/shard_map/all_gather | solution.py:771
  102.7 45.3 %collective-permute-start.20 = (bf16[1,256,2304]{2,1,0:T(8,128)(2,1)S(1)}, bf16[1,256,2304]{2,1,0:T(8,128)(2,1)S(1)}, u32[]{:S(2)}, u32[]{:S(2)}) collective-permute-start(bf16[1,256,2304]{2,1,0:T(8,128)(2,1)S(1)} %collective-permute-done.18.refs_8_.refs_11_), channel_id=1, source_target_pairs={{0,1},{1,0},{2,3},{3,2},{4,5},{5,4},{6,7},{7,6},{8,9},{9,8},{10,11... | collective-permute-start | bytes 3538952 | tf_op jit(solution)/shard_map/ppermute | solution.py:476
  158.9 13.0 %attend.1 = (bf16[4,2,64,512]{3,2,1,0:T(8,128)(2,1)S(1)}, f32[4,2,128,128]{3,2,1,0:T(8,128)}) custom-call(s32[1]{0:T(128)} %bitcast.68.shard_ref, bf16[4,2,64,512]{3,2,1,0:T(8,128)(2,1)S(1)} %bitcast.467, bf16[8,4,2,64,512]{4,3,2,1,0:T(8,128)(2,1)} %all-gather.7.cloned.1.call-done.kv_ref), custom_call_target="tpu_custom_call" | custom-call | tf_op jit(solution)/shard_map/attend/pallas_call | solution.py:172
  195.0 9.3 %collective-permute-done.21 = bf16[128,2304]{1,0:T(8,128)(2,1)} collective-permute-done((bf16[128,2304]{1,0:T(8,128)(2,1)}, bf16[128,2304]{1,0:T(8,128)(2,1)}, u32[]{:S(2)}, u32[]{:S(2)}) %collective-permute-start.21) | collective-permute-done | bytes 589856 | tf_op jit(solution)/shard_map/ppermute | solution.py:563
  274.8 8.4 %convolution_bitcast_fusion.5 = f32[256,2,1152]{2,0,1:T(8,128)} fusion(bf16[1152,3,2304]{2,0,1:T(8,128)(2,1)} %param.26, bf16[128,2304]{1,0:T(8,128)(2,1)S(1)} %collective-permute-done.37, bf16[128,2304]{1,0:T(8,128)(2,1)S(1)} %collective-permute-done.33), kind=kOutput, calls=%fused_computation.84 | convolution fusion | flops 2720268288 | bytes 14155776 | tf_op jit(solution)/shard_map/td,fgd->tgf/dot_general | solution.py:871
  289.1 10.9 %collective-permute-done.38 = bf16[128,2304]{1,0:T(8,128)(2,1)S(1)} collective-permute-done((bf16[128,2304]{1,0:T(8,128)(2,1)S(1)}, bf16[128,2304]{1,0:T(8,128)(2,1)S(1)}, u32[]{:S(2)}, u32[]{:S(2)}) %collective-permute-start.38) | collective-permute-done | bytes 589856 | tf_op jit(solution)/shard_map/ppermute | solution.py:860
  302.3 8.4 %convolution_bitcast_fusion.4 = f32[256,2,1152]{2,0,1:T(8,128)} fusion(bf16[1152,3,2304]{2,0,1:T(8,128)(2,1)} %param.26, bf16[128,2304]{1,0:T(8,128)(2,1)S(1)} %collective-permute-done.41, bf16[128,2304]{1,0:T(8,128)(2,1)S(1)} %collective-permute-done.36), kind=kOutput, calls=%fused_computation.83 | convolution fusion | flops 2720268288 | bytes 14155776 | tf_op jit(solution)/shard_map/td,fgd->tgf/dot_general | solution.py:871
  320.8 13.7 %collective-permute-done.43 = bf16[128,2304]{1,0:T(8,128)(2,1)S(1)} collective-permute-done((bf16[128,2304]{1,0:T(8,128)(2,1)S(1)}, bf16[128,2304]{1,0:T(8,128)(2,1)S(1)}, u32[]{:S(2)}, u32[]{:S(2)}) %collective-permute-start.43) | collective-permute-done | bytes 589856 | tf_op jit(solution)/shard_map/ppermute | solution.py:860
  345.8 8.4 %fusion.25 = bf16[256,2304]{1,0:T(8,128)(2,1)} fusion(bf16[1152,3,2304]{2,0,1:T(8,128)(2,1)} %param.26, bf16[256,1,1152]{2,0,1:T(8,128)(2,1)S(1)} %get-tuple-element.410, bf16[256,1,1152]{2,0,1:T(8,128)(2,1)S(1)} %get-tuple-element.409), kind=kOutput, calls=%fused_computation.74 | convolution fusion | flops 2719088640 | bytes 12976128 | tf_op jit(solution)/shard_map/tgf,fgd->td/dot_general | solution.py:893
  428.1 14.6 %collective-permute-done.52 = bf16[128,2304]{1,0:T(8,128)(2,1)} collective-permute-done((bf16[128,2304]{1,0:T(8,128)(2,1)}, bf16[128,2304]{1,0:T(8,128)(2,1)}, u32[]{:S(2)}, u32[]{:S(2)}) %collective-permute-start.52) | collective-permute-done | bytes 589856 | tf_op jit(solution)/shard_map/ppermute | solution.py:863
  461.7 13.1 %collective-permute-done.57 = bf16[128,2304]{1,0:T(8,128)(2,1)S(1)} collective-permute-done((bf16[128,2304]{1,0:T(8,128)(2,1)S(1)}, bf16[128,2304]{1,0:T(8,128)(2,1)S(1)}, u32[]{:S(2)}, u32[]{:S(2)}) %collective-permute-start.57) | collective-permute-done | bytes 589856 | tf_op jit(solution)/shard_map/ppermute | solution.py:865
  475.0 8.6 %pick.11 = bf16[16,128,2304]{2,1,0:T(8,128)(2,1)} custom-call(s32[16]{0:T(128)} %get-tuple-element.436.which_ref, s32[16]{0:T(128)} %get-tuple-element.435.slot_ref, bf16[24,128,2304]{2,1,0:T(8,128)(2,1)} %all-gather.11.cloned.1.call-done, bf16[24,128,2304]{2,1,0:T(8,128)(2,1)} %bitcast.127.refs_1_), custom_call_target="tpu_custom_call" | custom-call | tf_op jit(solution)/shard_map/pick/pallas_call | solution.py:398
  483.7 238.1 %conditional.1 = (bf16[768,2304]{1,0:T(8,128)(2,1)}, f32[4,2304]{1,0:T(4,128)}, f32[2,64,2304]{2,1,0:T(8,128)}) conditional(s32[]{:T(128)} %convert_element_type.461, () %tuple.68, (s32[]{:T(128)}, pred[]{:T(512)}, (), s32[]{:T(128)}, f32[128,2304]{1,0:T(8,128)S(1)}, /*index=5*/f32[128,2304]{1,0:T(8,128)S(1)}, f32[4,2304]{1,0:T(4,128)S(1)}, ...), branch_computations={%region_6.7_spmd, %region_7.18_spmd} | conditional | flops 3653388800 | bytes 193996064 | solution.py:1003
  499.9 25.9 %all-to-all-done = bf16[4,2,64,1024]{3,2,1,0:T(8,128)(2,1)S(1)} async-done(((bf16[4,2,64,1024]{3,2,1,0:T(8,128)(2,1)}), bf16[4,2,64,1024]{3,2,1,0:T(8,128)(2,1)S(1)}, u32[]{:S(2)}, u32[]{:S(2)}) %all-to-all-start) | async-done | bytes 1048608 | tf_op jit(solution)/shard_map/cond/branch_1_fun/all_to_all | solution.py:929
  527.0 21.9 %attend_back.1 = (bf16[4,2,64,512]{3,2,1,0:T(8,128)(2,1)}, bf16[8,4,2,64,512]{4,3,2,1,0:T(8,128)(2,1)}) custom-call(s32[1]{0:T(128)} %get-tuple-element.126.shard_ref, bf16[4,2,64,512]{3,2,1,0:T(8,128)(2,1)S(1)} %copy-done.24, bf16[4,2,64,512]{3,2,1,0:T(8,128)(2,1)} %get-tuple-element.375.do_ref, f32[4,2,128,128]{3,2,1,0:T(8,128)S(1)} %copy-done.48, ...), custom_call_target="tpu_custom_call" | custom-call | tf_op jit(solution)/shard_map/cond/branch_1_fun/attend_back/pallas_call | solution.py:203
  558.8 12.7 %collective-permute-done.4 = bf16[512,512]{1,0:T(8,128)(2,1)S(1)} collective-permute-done((bf16[512,512]{1,0:T(8,128)(2,1)S(1)}, bf16[512,512]{1,0:T(8,128)(2,1)S(1)}, u32[]{:S(2)}, u32[]{:S(2)}) %collective-permute-start.4) | collective-permute-done | bytes 524320 | tf_op jit(solution)/shard_map/cond/branch_1_fun/ppermute | solution.py:672
  575.5 11.5 %collective-permute-done.5 = bf16[512,512]{1,0:T(8,128)(2,1)S(1)} collective-permute-done((bf16[512,512]{1,0:T(8,128)(2,1)S(1)}, bf16[512,512]{1,0:T(8,128)(2,1)S(1)}, u32[]{:S(2)}, u32[]{:S(2)}) %collective-permute-start.5) | collective-permute-done | bytes 524320 | tf_op jit(solution)/shard_map/cond/branch_1_fun/ppermute | solution.py:672
  591.2 10.4 %collective-permute-done.6 = bf16[512,512]{1,0:T(8,128)(2,1)S(1)} collective-permute-done((bf16[512,512]{1,0:T(8,128)(2,1)S(1)}, bf16[512,512]{1,0:T(8,128)(2,1)S(1)}, u32[]{:S(2)}, u32[]{:S(2)}) %collective-permute-start.6) | collective-permute-done | bytes 524320 | tf_op jit(solution)/shard_map/cond/branch_1_fun/ppermute | solution.py:672
  624.3 14.7 %pick.6 = bf16[32,128,2304]{2,1,0:T(8,128)(2,1)} custom-call(s32[32]{0:T(128)} %get-tuple-element.380.which_ref, s32[32]{0:T(128)} %get-tuple-element.379.slot_ref, bf16[24,128,2304]{2,1,0:T(8,128)(2,1)} %bitcast.452, bf16[24,128,2304]{2,1,0:T(8,128)(2,1)} %bitcast.50.refs_1_), custom_call_target="tpu_custom_call" | custom-call | tf_op jit(solution)/shard_map/cond/branch_1_fun/pick/pallas_call | solution.py:398
  646.5 21.4 %all-to-all-start.2 = ((bf16[8,128,768]{1,2,0:T(8,128)(2,1)}), bf16[8,128,768]{1,2,0:T(8,128)(2,1)}, u32[]{:S(2)}, u32[]{:S(2)}) async-start(bf16[8,128,768]{1,2,0:T(8,128)(2,1)} %bitcast.464), calls=%async_computation.2 | async-start | bytes 3145728 | tf_op jit(solution)/shard_map/cond/branch_1_fun/all_to_all | solution.py:977
  668.0 9.9 %multiply_reduce_fusion = (f32[128]{0:T(128)S(1)}, f32[2304]{0:T(1024)S(1)}, f32[128,2304]{1,0:T(8,128)S(1)}) fusion(f32[128,2304]{1,0:T(8,128)S(1)} %get-tuple-element.152, f32[2304]{0:T(1024)S(1)} %get-tuple-element.355, f32[128]{0:T(128)S(1)} %add_rsqrt_fusion, bf16[128,4096]{0,1:T(8,128)(2,1)S(1)} %bitcast.456, bf16[4096,2304]{1,0:T(8,128)(2,1)} %bitcast.449), kind=kOutput, calls=%fused_computation.4 | convolution fusion | flops 2417686272 | bytes 22301696 | tf_op jit(solution)/shard_map/cond/branch_1_fun/dot_general | solution.py:48
  681.1 24.8 %all-to-all-done.2 = bf16[8,128,768]{1,2,0:T(8,128)(2,1)} async-done(((bf16[8,128,768]{1,2,0:T(8,128)(2,1)}), bf16[8,128,768]{1,2,0:T(8,128)(2,1)}, u32[]{:S(2)}, u32[]{:S(2)}) %all-to-all-start.2) | async-done | bytes 1572896 | tf_op jit(solution)/shard_map/cond/branch_1_fun/all_to_all | solution.py:977
  709.3 12.5 %weight_grad.1 = bf16[768,2304]{1,0:T(8,128)(2,1)} custom-call(s32[17]{0:T(128)} %stack.119.place_ref, bf16[1024,768]{1,0:T(8,128)(2,1)} %bitcast.465, bf16[128,2304]{1,0:T(8,128)(2,1)} %get-tuple-element.136.refs_0_, bf16[128,2304]{1,0:T(8,128)(2,1)} %get-tuple-element.137.refs_1_, bf16[128,2304]{1,0:T(8,128)(2,1)} %get-tuple-element.138.refs_2_, ...), custom_call_target="tpu_custom_call" | custom-call | tf_op jit(solution)/shard_map/cond/branch_1_fun/weight_grad/pallas_call | solution.py:634
  742.0 17.4 %collective-permute-done.69 = f32[4,288]{1,0:T(4,128)S(1)} collective-permute-done((f32[4,288]{1,0:T(4,128)S(1)}, f32[4,288]{1,0:T(4,128)S(1)}, u32[]{:S(2)}, u32[]{:S(2)}) %collective-permute-start.69) | collective-permute-done | bytes 4640 | tf_op jit(solution)/shard_map/ppermute | solution.py:729
  (528 shorter events, 443.5 us)
Async XLA Ops:
  7.2 50.2 %all-gather.9.cloned.1.call-start = ((), (), s32[]{:S(2)}) async-start(), calls=%async_computation.4 | async-start | bytes 2949120 | tf_op jit(solution)/shard_map/all_gather | solution.py:770
  7.9 142.3 %all-gather.7.cloned.1.call-start = ((), (), s32[]{:S(2)}) async-start(), calls=%async_computation.3 | async-start | bytes 4718592 | tf_op jit(solution)/shard_map/all_gather | solution.py:795
  85.5 302.5 %all-gather.11.cloned.1.call-start = ((), (), s32[]{:S(2)}) async-start(), calls=%async_computation.5 | async-start | bytes 17694720 | tf_op jit(solution)/shard_map/all_gather | solution.py:836
  99.3 73.7 %collective-permute-start.22 = (bf16[1,256,2304]{2,1,0:T(8,128)(2,1)}, bf16[1,256,2304]{2,1,0:T(8,128)(2,1)}, u32[]{:S(2)}, u32[]{:S(2)}) collective-permute-start(bf16[1,256,2304]{2,1,0:T(8,128)(2,1)} %get-tuple-element.397), channel_id=1, source_target_pairs={{4,6},{27,25}} | collective-permute-start | bytes 3538952 | tf_op jit(solution)/shard_map/ppermute | solution.py:465
  101.0 72.0 %collective-permute-start.23 = (bf16[1,256,2304]{2,1,0:T(8,128)(2,1)}, bf16[1,256,2304]{2,1,0:T(8,128)(2,1)}, u32[]{:S(2)}, u32[]{:S(2)}) collective-permute-start(bf16[1,256,2304]{2,1,0:T(8,128)(2,1)} %get-tuple-element.395), channel_id=1, source_target_pairs={{4,6},{27,25}} | collective-permute-start | bytes 3538952 | tf_op jit(solution)/shard_map/ppermute | solution.py:465
  102.7 48.8 %collective-permute-start.20 = (bf16[1,256,2304]{2,1,0:T(8,128)(2,1)S(1)}, bf16[1,256,2304]{2,1,0:T(8,128)(2,1)S(1)}, u32[]{:S(2)}, u32[]{:S(2)}) collective-permute-start(bf16[1,256,2304]{2,1,0:T(8,128)(2,1)S(1)} %collective-permute-done.18.refs_8_.refs_11_), channel_id=1, source_target_pairs={{0,1},{1,0},{2,3},{3,2},{4,5},{5,4},{6,7},{7,6},{8,9},{9,8},{10,11... | collective-permute-start | bytes 3538952 | tf_op jit(solution)/shard_map/ppermute | solution.py:476
  173.6 30.7 %collective-permute-start.21 = (bf16[128,2304]{1,0:T(8,128)(2,1)}, bf16[128,2304]{1,0:T(8,128)(2,1)}, u32[]{:S(2)}, u32[]{:S(2)}) collective-permute-start(bf16[128,2304]{1,0:T(8,128)(2,1)} %collective-permute-done.17), channel_id=1, source_target_pairs={{0,2},{1,3},{2,6},{3,7},{4,0},{5,1},{6,4},{7,5},{8,10},{9,11},{10,... | collective-permute-start | bytes 1769480 | tf_op jit(solution)/shard_map/ppermute | solution.py:563
  209.9 23.8 %collective-permute-start.26 = (bf16[128,2304]{1,0:T(8,128)(2,1)}, bf16[128,2304]{1,0:T(8,128)(2,1)}, u32[]{:S(2)}, u32[]{:S(2)}) collective-permute-start(bf16[128,2304]{1,0:T(8,128)(2,1)} %collective-permute-done.21), channel_id=1, source_target_pairs={{0,2},{1,3},{2,6},{3,7},{4,0},{5,1},{6,4},{7,5},{8,10},{9,11},{10,... | collective-permute-start | bytes 1769480 | tf_op jit(solution)/shard_map/ppermute | solution.py:563
  240.3 539.3 %all-reduce.3.cloned.1.call-start = ((), (), s32[]{:S(2)}) async-start(), calls=%async_computation.6 | async-start | bytes 31850496 | tf_op jit(solution)/shard_map/psum | solution.py:905
  272.3 27.7 %collective-permute-start.38 = (bf16[128,2304]{1,0:T(8,128)(2,1)S(1)}, bf16[128,2304]{1,0:T(8,128)(2,1)S(1)}, u32[]{:S(2)}, u32[]{:S(2)}) collective-permute-start(bf16[128,2304]{1,0:T(8,128)(2,1)S(1)} %add_convert_fusion.6), channel_id=1, source_target_pairs={{0,2},{1,3},{2,6},{3,7},{4,0},{5,1},{6,4},{7,5},{8,10},{9,11},{10,... | collective-permute-start | bytes 1769480 | tf_op jit(solution)/shard_map/ppermute | solution.py:860
  288.5 32.2 %collective-permute-start.44 = (bf16[128,2304]{1,0:T(8,128)(2,1)S(1)}, bf16[128,2304]{1,0:T(8,128)(2,1)S(1)}, u32[]{:S(2)}, u32[]{:S(2)}) collective-permute-start(bf16[128,2304]{1,0:T(8,128)(2,1)S(1)} %slice.511), channel_id=1, source_target_pairs={{0,1},{1,0},{2,3},{3,2},{4,5},{5,4},{6,7},{7,6},{8,9},{9,8},{10,11... | collective-permute-start | bytes 1769480 | tf_op jit(solution)/shard_map/ppermute | solution.py:851
  390.2 84.8 %collective-permute-start.59 = (bf16[4,6,128,2304]{3,2,1,0:T(8,128)(2,1)}, bf16[4,6,128,2304]{3,2,1,0:T(8,128)(2,1)}, u32[]{:S(2)}, u32[]{:S(2)}) collective-permute-start(bf16[4,6,128,2304]{3,2,1,0:T(8,128)(2,1)} %bitcast.450), channel_id=1, source_target_pairs={{0,1},{1,0},{2,3},{3,2},{4,5},{5,4},{6,7},{7,6},{8,9},{9,8},{10,11... | collective-permute-start | bytes 42467336 | tf_op jit(solution)/shard_map/ppermute | solution.py:914
  496.4 29.5 %all-to-all-start = ((bf16[4,2,64,1024]{3,2,1,0:T(8,128)(2,1)}), bf16[4,2,64,1024]{3,2,1,0:T(8,128)(2,1)S(1)}, u32[]{:S(2)}, u32[]{:S(2)}) async-start(bf16[4,2,64,1024]{3,2,1,0:T(8,128)(2,1)} %pad_maximum_fusion.1), calls=%async_computation | async-start | bytes 2097152 | tf_op jit(solution)/shard_map/cond/branch_1_fun/all_to_all | solution.py:929
  604.1 39.4 %all-to-all-start.1 = ((bf16[4,2,64,1024]{3,2,1,0:T(8,128)(2,1)}), bf16[4,2,64,1024]{3,2,1,0:T(8,128)(2,1)S(1)}, u32[]{:S(2)}, u32[]{:S(2)}) async-start(bf16[4,2,64,1024]{3,2,1,0:T(8,128)(2,1)} %pad_maximum_fusion.2), calls=%async_computation.1 | async-start | bytes 2097152 | tf_op jit(solution)/shard_map/cond/branch_1_fun/all_to_all | solution.py:949
  607.8 35.8 %collective-permute-start = (bf16[128,2304]{1,0:T(8,128)(2,1)}, bf16[128,2304]{1,0:T(8,128)(2,1)}, u32[]{:S(2)}, u32[]{:S(2)}) collective-permute-start(bf16[128,2304]{1,0:T(8,128)(2,1)} %multiply_convert_fusion.refs_8_), channel_id=1, source_target_pairs={{2,4},{3,5},{4,6},{5,7},{10,12},{11,13},{12,14},{13,15},{18,20},{1... | collective-permute-start | bytes 1769480 | tf_op jit(solution)/shard_map/cond/branch_1_fun/ppermute | solution.py:575
  609.3 34.3 %collective-permute-start.1 = (bf16[128,2304]{1,0:T(8,128)(2,1)}, bf16[128,2304]{1,0:T(8,128)(2,1)}, u32[]{:S(2)}, u32[]{:S(2)}) collective-permute-start(bf16[128,2304]{1,0:T(8,128)(2,1)} %multiply_convert_fusion.refs_8_), channel_id=1, source_target_pairs={{0,4},{1,5},{2,6},{3,7},{8,12},{9,13},{10,14},{11,15},{16,20},{17,... | collective-permute-start | bytes 1769480 | tf_op jit(solution)/shard_map/cond/branch_1_fun/ppermute | solution.py:575
  616.5 27.1 %collective-permute-start.2 = (bf16[128,2304]{1,0:T(8,128)(2,1)}, bf16[128,2304]{1,0:T(8,128)(2,1)}, u32[]{:S(2)}, u32[]{:S(2)}) collective-permute-start(bf16[128,2304]{1,0:T(8,128)(2,1)} %multiply_convert_fusion.refs_8_), channel_id=1, source_target_pairs={{0,6},{1,7},{6,4},{7,5},{8,14},{9,15},{14,12},{15,13},{16,22},{17,... | collective-permute-start | bytes 1769480 | tf_op jit(solution)/shard_map/cond/branch_1_fun/ppermute | solution.py:575
  646.5 59.3 %all-to-all-start.2 = ((bf16[8,128,768]{1,2,0:T(8,128)(2,1)}), bf16[8,128,768]{1,2,0:T(8,128)(2,1)}, u32[]{:S(2)}, u32[]{:S(2)}) async-start(bf16[8,128,768]{1,2,0:T(8,128)(2,1)} %bitcast.464), calls=%async_computation.2 | async-start | bytes 3145728 | tf_op jit(solution)/shard_map/cond/branch_1_fun/all_to_all | solution.py:977
  678.0 30.5 %collective-permute-start.10 = (bf16[128,2304]{1,0:T(8,128)(2,1)}, bf16[128,2304]{1,0:T(8,128)(2,1)S(1)}, u32[]{:S(2)}, u32[]{:S(2)}) collective-permute-start(bf16[128,2304]{1,0:T(8,128)(2,1)} %collective-permute-done.2.refs_14_), channel_id=1, source_target_pairs={{0,1},{1,0},{2,3},{3,2},{4,5},{5,4},{6,7},{7,6},{8,9},{9,8},{10,11... | collective-permute-start | bytes 1769480 | tf_op jit(solution)/shard_map/cond/branch_1_fun/ppermute | solution.py:593
  678.5 30.0 %collective-permute-start.7 = (bf16[128,2304]{1,0:T(8,128)(2,1)}, bf16[128,2304]{1,0:T(8,128)(2,1)}, u32[]{:S(2)}, u32[]{:S(2)}) collective-permute-start(bf16[128,2304]{1,0:T(8,128)(2,1)} %multiply_convert_fusion.refs_8_), channel_id=1, source_target_pairs={{0,1},{1,0},{2,3},{3,2},{4,5},{5,4},{6,7},{7,6},{8,9},{9,8},{10,11... | collective-permute-start | bytes 1769480 | tf_op jit(solution)/shard_map/cond/branch_1_fun/ppermute | solution.py:593
  678.6 29.9 %collective-permute-start.8 = (bf16[128,2304]{1,0:T(8,128)(2,1)}, bf16[128,2304]{1,0:T(8,128)(2,1)}, u32[]{:S(2)}, u32[]{:S(2)}) collective-permute-start(bf16[128,2304]{1,0:T(8,128)(2,1)} %collective-permute-done.refs_10_), channel_id=1, source_target_pairs={{0,1},{1,0},{2,3},{3,2},{4,5},{5,4},{6,7},{7,6},{8,9},{9,8},{10,11... | collective-permute-start | bytes 1769480 | tf_op jit(solution)/shard_map/cond/branch_1_fun/ppermute | solution.py:593
  679.0 29.5 %collective-permute-start.9 = (bf16[128,2304]{1,0:T(8,128)(2,1)}, bf16[128,2304]{1,0:T(8,128)(2,1)}, u32[]{:S(2)}, u32[]{:S(2)}) collective-permute-start(bf16[128,2304]{1,0:T(8,128)(2,1)} %collective-permute-done.1.refs_12_), channel_id=1, source_target_pairs={{0,1},{1,0},{2,3},{3,2},{4,5},{5,4},{6,7},{7,6},{8,9},{9,8},{10,11... | collective-permute-start | bytes 1769480 | tf_op jit(solution)/shard_map/cond/branch_1_fun/ppermute | solution.py:593
  724.3 39.3 %collective-permute-start.65 = (bf16[2,192,1152]{2,1,0:T(8,128)(2,1)S(1)}, bf16[2,192,1152]{2,1,0:T(8,128)(2,1)}, u32[]{:S(2)}, u32[]{:S(2)}) collective-permute-start(bf16[2,192,1152]{2,1,0:T(8,128)(2,1)S(1)} %pad_maximum_fusion.7), channel_id=1, source_target_pairs={{0,16},{8,24},{16,0},{24,8},{1,17},{9,25},{17,1},{25,9},{2,18},{10... | collective-permute-start | bytes 2654216 | tf_op jit(solution)/shard_map/ppermute | solution.py:684
  727.1 36.5 %collective-permute-start.64 = (bf16[2,192,1152]{2,1,0:T(8,128)(2,1)}, bf16[2,192,1152]{2,1,0:T(8,128)(2,1)}, u32[]{:S(2)}, u32[]{:S(2)}) collective-permute-start(bf16[2,192,1152]{2,1,0:T(8,128)(2,1)} %pad_maximum_fusion.6), channel_id=1, source_target_pairs={{0,8},{8,0},{16,24},{24,16},{1,9},{9,1},{17,25},{25,17},{2,10},{10... | collective-permute-start | bytes 2654216 | tf_op jit(solution)/shard_map/ppermute | solution.py:684
  (151 other events, 1476.6 us)
Sparse Core Ops, SparseCore 0:
  9.8 40.1 all-gather.8
  85.6 63.7 all-gather.6
  240.4 133.9 all-gather.10
  421.5 332.8 all-reduce.2

commit v6 on v5

--- a/solution.py
+++ b/solution.py
@@ -862,7 +862,9 @@
             total, _ = lax.optimization_barrier((pairs[1].astype(bf16), held))
             total = lax.ppermute(total, "fsdp", ring).astype(f32)
             for pair in pairs[2:]:
-                total = lax.ppermute((total + pair).astype(bf16), "fsdp", ring).astype(f32)
+                total = (total + pair).astype(bf16)
+                total, pairs[-1] = lax.optimization_barrier((total, pairs[-1]))
+                total = lax.ppermute(total, "fsdp", ring).astype(f32)
         return total + pairs[0]
 
     saved = []
@@ -926,15 +928,11 @@
             .astype(bf16)
             .reshape(seqs, rows, columns, per * HD)
         )
-        both = lax.all_to_all(
-            jnp.concatenate([grad_mixed.transpose(2, 0, 1, 3), mixed], axis=-1),
-            "seq",
-            split_axis=0,
-            concat_axis=0,
-            tiled=True,
-        )
-        grad_heads = both[..., : per * HD]
-        mixed_rows = both[..., per * HD :].transpose(1, 2, 0, 3).reshape(own_rows, HQ * HD)
+        grad_heads = lax.all_to_all(
+            grad_mixed.transpose(2, 0, 1, 3), "seq", split_axis=0, concat_axis=0, tiled=True
+        )
+        mixed_rows = lax.all_to_all(mixed, "seq", split_axis=0, concat_axis=0, tiled=True)
+        mixed_rows = mixed_rows.transpose(1, 2, 0, 3).reshape(own_rows, HQ * HD)
         shard_cols = attn_weight.shape[0]
         first_owner = (HQ + 2 * KVH) * HD // shard_cols // 2
         later_pieces = direct_pieces(

time: 836 us -> 831 us (level)
    ppermute x4 -> x6, waiting for transfers between devices: 40.4 us -> 60 us  [pipeline(): total = lax.ppermute(total, 'fsdp', ring).astype(f32)]
    ppermute x2 -> x0, waiting for transfers between devices: 18.9 us -> none  [pipeline(): total = lax.ppermute((total + pair).astype(bf16), 'fsdp', ring).astype(f32)]
    all_to_all x1 -> x2, waiting for transfers between devices: 25.9 us -> 14.7 us  [the longest x1 14.6 us: attention_back(): lax.all_to_all(grad_mixed.transpose(2, 0, 1, 3), 'seq', split_axis=0, con...]
  transfers between devices with their start and end apart: 84 -> 85, of which waited for: 37 -> 37; matrix products, arithmetic and copies ran while one was open for 28% -> 28% of each run, Pallas kernels for 15% -> 15%
where the time goes in v6:
time: 831 us; the launch traced here: 819 us
  waiting for transfers between devices  237 us (29%)
  starting transfers between devices  162 us (19%)
  matrix products  132 us (16%)
  Pallas kernels  122 us (15%)
  local copies, waits for them, and re-layouts  66.6 us (8%)
  other arithmetic  55.2 us (7%)
  between operations  18.2 us (2%)
  blocking collectives  15.7 us (2%)
  loops' own time  10.5 us (1%)
    pallas_call x9, Pallas kernels, pick(): pl.pallas_call(functools.partial(kernel, cands), grid_spec=pltpu.Prefetch...  61.9 us
    ppermute x6, waiting for transfers between devices, pipeline(): total = lax.ppermute(total, 'fsdp', ring).astype(f32)  60 us
    ppermute x4, starting transfers between devices, routed_weights(): sources['swapped%d' % number] = lax.ppermute(got, 'fsdp', swap)  52.8 us
    ppermute x5, waiting for transfers between devices, sum_over(): lax.ppermute(value, axis, [(c, c ^ bit) for c in range(count)])  38.3 us
    dot_general x5, matrix products, dot_nn(): lax.dot_general(a, b, (((1,), (0,)), ((), ())), preferred_element_type=f32)  32 us
    ppermute x3, waiting for transfers between devices, ring_scatter(): lax.ppermute(total.astype(bf16), 'fsdp', pairs).astype(f32)  30.5 us
    dot_general x4, matrix products, forward(): jnp.einsum('td,fgd->tgf', rows_here, weight_gate_up, preferred_element_ty...  28.9 us
    dot_general x5, matrix products, dot_nt(): lax.dot_general(a, b, (((1,), (1,)), ((), ())), preferred_element_type=f32)  25.4 us
  transfers between devices with their start and end apart: 85, of which 37 were waited for; matrix products, arithmetic and copies ran while one was open for 28% of the time, Pallas kernels for 15%

profile of v6, /device:TPU:0, one launch (start us, length us, event | category | flops | bytes accessed | tf_op | source)
XLA Modules:
  0.0 819.3 jit_solution(15230344821878006126)
XLA Ops:
  8.0 15.7 %all-gather.2 = bf16[8,288,4]{1,2,0:T(4,128)(2,1)S(1)} all-gather(bf16[1,288,4]{1,2,0:T(4,128)(2,1)} %bitcast.492), channel_id=1, replica_groups=mesh['seq'=4,'fsdp'=8] {'fsdp'}, dimensions={0}, use_global_device_ids=true | all-gather | bytes 20736 | tf_op jit(solution)/shard_map/all_gather | solution.py:771
  102.7 45.3 %collective-permute-start.20 = (bf16[1,256,2304]{2,1,0:T(8,128)(2,1)S(1)}, bf16[1,256,2304]{2,1,0:T(8,128)(2,1)S(1)}, u32[]{:S(2)}, u32[]{:S(2)}) collective-permute-start(bf16[1,256,2304]{2,1,0:T(8,128)(2,1)S(1)} %collective-permute-done.18.refs_8_.refs_11_), channel_id=1, source_target_pairs={{0,1},{1,0},{2,3},{3,2},{4,5},{5,4},{6,7},{7,6},{8,9},{9,8},{10,11... | collective-permute-start | bytes 3538952 | tf_op jit(solution)/shard_map/ppermute | solution.py:476
  158.9 13.1 %attend.1 = (bf16[4,2,64,512]{3,2,1,0:T(8,128)(2,1)}, f32[4,2,128,128]{3,2,1,0:T(8,128)}) custom-call(s32[1]{0:T(128)} %bitcast.68.shard_ref, bf16[4,2,64,512]{3,2,1,0:T(8,128)(2,1)S(1)} %bitcast.466, bf16[8,4,2,64,512]{4,3,2,1,0:T(8,128)(2,1)} %all-gather.7.cloned.1.call-done.kv_ref), custom_call_target="tpu_custom_call" | custom-call | tf_op jit(solution)/shard_map/attend/pallas_call | solution.py:172
  195.9 8.4 %collective-permute-done.21 = bf16[128,2304]{1,0:T(8,128)(2,1)} collective-permute-done((bf16[128,2304]{1,0:T(8,128)(2,1)}, bf16[128,2304]{1,0:T(8,128)(2,1)}, u32[]{:S(2)}, u32[]{:S(2)}) %collective-permute-start.21) | collective-permute-done | bytes 589856 | tf_op jit(solution)/shard_map/ppermute | solution.py:563
  274.8 8.4 %convolution_bitcast_fusion.5 = f32[256,2,1152]{2,0,1:T(8,128)} fusion(bf16[1152,3,2304]{2,0,1:T(8,128)(2,1)} %param.26, bf16[128,2304]{1,0:T(8,128)(2,1)S(1)} %collective-permute-done.37, bf16[128,2304]{1,0:T(8,128)(2,1)S(1)} %collective-permute-done.33), kind=kOutput, calls=%fused_computation.82 | convolution fusion | flops 2720268288 | bytes 14155776 | tf_op jit(solution)/shard_map/td,fgd->tgf/dot_general | solution.py:873
  289.1 10.8 %collective-permute-done.38 = bf16[128,2304]{1,0:T(8,128)(2,1)S(1)} collective-permute-done((bf16[128,2304]{1,0:T(8,128)(2,1)S(1)}, bf16[128,2304]{1,0:T(8,128)(2,1)S(1)}, u32[]{:S(2)}, u32[]{:S(2)}) %collective-permute-start.38) | collective-permute-done | bytes 589856 | tf_op jit(solution)/shard_map/ppermute | solution.py:860
  302.2 8.4 %convolution_bitcast_fusion.4 = f32[256,2,1152]{2,0,1:T(8,128)} fusion(bf16[1152,3,2304]{2,0,1:T(8,128)(2,1)} %param.26, bf16[128,2304]{1,0:T(8,128)(2,1)S(1)} %collective-permute-done.41, bf16[128,2304]{1,0:T(8,128)(2,1)S(1)} %collective-permute-done.36), kind=kOutput, calls=%fused_computation.81 | convolution fusion | flops 2720268288 | bytes 14155776 | tf_op jit(solution)/shard_map/td,fgd->tgf/dot_general | solution.py:873
  320.7 13.6 %collective-permute-done.43 = bf16[128,2304]{1,0:T(8,128)(2,1)S(1)} collective-permute-done((bf16[128,2304]{1,0:T(8,128)(2,1)S(1)}, bf16[128,2304]{1,0:T(8,128)(2,1)S(1)}, u32[]{:S(2)}, u32[]{:S(2)}) %collective-permute-start.43) | collective-permute-done | bytes 589856 | tf_op jit(solution)/shard_map/ppermute | solution.py:860
  345.7 8.4 %fusion.25 = bf16[256,2304]{1,0:T(8,128)(2,1)} fusion(bf16[1152,3,2304]{2,0,1:T(8,128)(2,1)} %param.26, bf16[256,1,1152]{2,0,1:T(8,128)(2,1)S(1)} %get-tuple-element.440, bf16[256,1,1152]{2,0,1:T(8,128)(2,1)S(1)} %get-tuple-element.439), kind=kOutput, calls=%fused_computation.72 | convolution fusion | flops 2719088640 | bytes 12976128 | tf_op jit(solution)/shard_map/tgf,fgd->td/dot_general | solution.py:895
  446.1 13.3 %collective-permute-done.56 = bf16[128,2304]{1,0:T(8,128)(2,1)S(1)} collective-permute-done((bf16[128,2304]{1,0:T(8,128)(2,1)S(1)}, bf16[128,2304]{1,0:T(8,128)(2,1)S(1)}, u32[]{:S(2)}, u32[]{:S(2)}) %collective-permute-start.56) | collective-permute-done | bytes 589856 | tf_op jit(solution)/shard_map/ppermute | solution.py:867
  461.5 12.9 %collective-permute-done.57 = bf16[128,2304]{1,0:T(8,128)(2,1)S(1)} collective-permute-done((bf16[128,2304]{1,0:T(8,128)(2,1)S(1)}, bf16[128,2304]{1,0:T(8,128)(2,1)S(1)}, u32[]{:S(2)}, u32[]{:S(2)}) %collective-permute-start.57) | collective-permute-done | bytes 589856 | tf_op jit(solution)/shard_map/ppermute | solution.py:867
  474.7 8.6 %pick.11 = bf16[16,128,2304]{2,1,0:T(8,128)(2,1)} custom-call(s32[16]{0:T(128)} %get-tuple-element.466.which_ref, s32[16]{0:T(128)} %get-tuple-element.465.slot_ref, bf16[24,128,2304]{2,1,0:T(8,128)(2,1)} %all-gather.11.cloned.1.call-done, bf16[24,128,2304]{2,1,0:T(8,128)(2,1)} %bitcast.127.refs_1_), custom_call_target="tpu_custom_call" | custom-call | tf_op jit(solution)/shard_map/pick/pallas_call | solution.py:398
  483.4 226.2 %conditional.1 = (bf16[768,2304]{1,0:T(8,128)(2,1)}, f32[4,2304]{1,0:T(4,128)}, f32[2,64,2304]{2,1,0:T(8,128)}) conditional(s32[]{:T(128)} %convert_element_type.461, () %tuple.70, (s32[]{:T(128)}, pred[]{:T(512)}, (), s32[]{:T(128)}, f32[128,2304]{1,0:T(8,128)S(1)}, /*index=5*/f32[128,2304]{1,0:T(8,128)S(1)}, f32[4,2304]{1,0:T(4,128)S(1)}, ...), branch_computations={%region_6.7_spmd, %region_7.18_spmd} | conditional | flops 3651291648 | bytes 191898976 | solution.py:1001
  498.8 14.6 %all-to-all-done.do_ref = bf16[4,2,64,512]{3,2,1,0:T(8,128)(2,1)S(1)} async-done(((bf16[4,2,64,512]{3,2,1,0:T(8,128)(2,1)}), bf16[4,2,64,512]{3,2,1,0:T(8,128)(2,1)S(1)}, u32[]{:S(2)}, u32[]{:S(2)}) %all-to-all-start) | async-done | bytes 524320 | tf_op jit(solution)/shard_map/cond/branch_1_fun/all_to_all | solution.py:931
  514.3 22.0 %attend_back.1 = (bf16[4,2,64,512]{3,2,1,0:T(8,128)(2,1)}, bf16[8,4,2,64,512]{4,3,2,1,0:T(8,128)(2,1)}) custom-call(s32[1]{0:T(128)} %get-tuple-element.126.shard_ref, bf16[4,2,64,512]{3,2,1,0:T(8,128)(2,1)S(1)} %copy-done.24, bf16[4,2,64,512]{3,2,1,0:T(8,128)(2,1)} %copy-done.27, f32[4,2,128,128]{3,2,1,0:T(8,128)S(1)} %copy-done.49, ...), custom_call_target="tpu_custom_call" | custom-call | tf_op jit(solution)/shard_map/cond/branch_1_fun/attend_back/pallas_call | solution.py:203
  546.8 12.1 %collective-permute-done.4 = bf16[512,512]{1,0:T(8,128)(2,1)S(1)} collective-permute-done((bf16[512,512]{1,0:T(8,128)(2,1)S(1)}, bf16[512,512]{1,0:T(8,128)(2,1)S(1)}, u32[]{:S(2)}, u32[]{:S(2)}) %collective-permute-start.4) | collective-permute-done | bytes 524320 | tf_op jit(solution)/shard_map/cond/branch_1_fun/ppermute | solution.py:672
  563.3 11.2 %collective-permute-done.5 = bf16[512,512]{1,0:T(8,128)(2,1)S(1)} collective-permute-done((bf16[512,512]{1,0:T(8,128)(2,1)S(1)}, bf16[512,512]{1,0:T(8,128)(2,1)S(1)}, u32[]{:S(2)}, u32[]{:S(2)}) %collective-permute-start.5) | collective-permute-done | bytes 524320 | tf_op jit(solution)/shard_map/cond/branch_1_fun/ppermute | solution.py:672
  612.1 15.2 %pick.6 = bf16[32,128,2304]{2,1,0:T(8,128)(2,1)} custom-call(s32[32]{0:T(128)} %get-tuple-element.410.which_ref, s32[32]{0:T(128)} %get-tuple-element.409.slot_ref, bf16[24,128,2304]{2,1,0:T(8,128)(2,1)} %bitcast.451, bf16[24,128,2304]{2,1,0:T(8,128)(2,1)} %bitcast.50.refs_1_), custom_call_target="tpu_custom_call" | custom-call | tf_op jit(solution)/shard_map/cond/branch_1_fun/pick/pallas_call | solution.py:398
  634.8 21.2 %all-to-all-start.3 = ((bf16[8,128,768]{1,2,0:T(8,128)(2,1)}), bf16[8,128,768]{1,2,0:T(8,128)(2,1)}, u32[]{:S(2)}, u32[]{:S(2)}) async-start(bf16[8,128,768]{1,2,0:T(8,128)(2,1)} %bitcast.463), calls=%async_computation.3 | async-start | bytes 3145728 | tf_op jit(solution)/shard_map/cond/branch_1_fun/all_to_all | solution.py:975
  656.1 10.2 %multiply_reduce_fusion = (f32[128]{0:T(128)S(1)}, f32[2304]{0:T(1024)S(1)}, f32[128,2304]{1,0:T(8,128)S(1)}) fusion(f32[128,2304]{1,0:T(8,128)S(1)} %get-tuple-element.152, f32[2304]{0:T(1024)S(1)} %get-tuple-element.387, f32[128]{0:T(128)S(1)} %add_rsqrt_fusion, bf16[128,4096]{0,1:T(8,128)(2,1)S(1)} %bitcast.455, bf16[4096,2304]{1,0:T(8,128)(2,1)} %bitcast.448), kind=kOutput, calls=%fused_computation.4 | convolution fusion | flops 2417686272 | bytes 22301696 | tf_op jit(solution)/shard_map/cond/branch_1_fun/dot_general | solution.py:48
  669.4 24.5 %all-to-all-done.3 = bf16[8,128,768]{1,2,0:T(8,128)(2,1)} async-done(((bf16[8,128,768]{1,2,0:T(8,128)(2,1)}), bf16[8,128,768]{1,2,0:T(8,128)(2,1)}, u32[]{:S(2)}, u32[]{:S(2)}) %all-to-all-start.3) | async-done | bytes 1572896 | tf_op jit(solution)/shard_map/cond/branch_1_fun/all_to_all | solution.py:975
  697.3 12.3 %weight_grad.1 = bf16[768,2304]{1,0:T(8,128)(2,1)} custom-call(s32[17]{0:T(128)} %stack.119.place_ref, bf16[1024,768]{1,0:T(8,128)(2,1)} %bitcast.464, bf16[128,2304]{1,0:T(8,128)(2,1)} %get-tuple-element.136.refs_0_, bf16[128,2304]{1,0:T(8,128)(2,1)} %get-tuple-element.137.refs_1_, bf16[128,2304]{1,0:T(8,128)(2,1)} %get-tuple-element.138.refs_2_, ...), custom_call_target="tpu_custom_call" | custom-call | tf_op jit(solution)/shard_map/cond/branch_1_fun/weight_grad/pallas_call | solution.py:634
  729.7 25.6 %collective-permute-done.69 = f32[4,288]{1,0:T(4,128)S(1)} collective-permute-done((f32[4,288]{1,0:T(4,128)S(1)}, f32[4,288]{1,0:T(4,128)S(1)}, u32[]{:S(2)}, u32[]{:S(2)}) %collective-permute-start.69) | collective-permute-done | bytes 4640 | tf_op jit(solution)/shard_map/ppermute | solution.py:729
  776.4 8.2 %collective-permute-done.73 = bf16[192,1152]{1,0:T(8,128)(2,1)S(1)} collective-permute-done((bf16[192,1152]{1,0:T(8,128)(2,1)S(1)}, bf16[192,1152]{1,0:T(8,128)(2,1)S(1)}, u32[]{:S(2)}, u32[]{:S(2)}) %collective-permute-start.73) | collective-permute-done | bytes 442400 | tf_op jit(solution)/shard_map/ppermute | solution.py:711
  (530 shorter events, 446.5 us)
Async XLA Ops:
  7.2 50.2 %all-gather.9.cloned.1.call-start = ((), (), s32[]{:S(2)}) async-start(), calls=%async_computation.5 | async-start | bytes 2949120 | tf_op jit(solution)/shard_map/all_gather | solution.py:770
  7.9 142.3 %all-gather.7.cloned.1.call-start = ((), (), s32[]{:S(2)}) async-start(), calls=%async_computation.4 | async-start | bytes 4718592 | tf_op jit(solution)/shard_map/all_gather | solution.py:795
  85.5 302.3 %all-gather.11.cloned.1.call-start = ((), (), s32[]{:S(2)}) async-start(), calls=%async_computation.6 | async-start | bytes 17694720 | tf_op jit(solution)/shard_map/all_gather | solution.py:836
  99.2 74.8 %collective-permute-start.22 = (bf16[1,256,2304]{2,1,0:T(8,128)(2,1)}, bf16[1,256,2304]{2,1,0:T(8,128)(2,1)}, u32[]{:S(2)}, u32[]{:S(2)}) collective-permute-start(bf16[1,256,2304]{2,1,0:T(8,128)(2,1)} %get-tuple-element.427), channel_id=1, source_target_pairs={{4,6},{27,25}} | collective-permute-start | bytes 3538952 | tf_op jit(solution)/shard_map/ppermute | solution.py:465
  101.0 73.1 %collective-permute-start.23 = (bf16[1,256,2304]{2,1,0:T(8,128)(2,1)}, bf16[1,256,2304]{2,1,0:T(8,128)(2,1)}, u32[]{:S(2)}, u32[]{:S(2)}) collective-permute-start(bf16[1,256,2304]{2,1,0:T(8,128)(2,1)} %get-tuple-element.425), channel_id=1, source_target_pairs={{4,6},{27,25}} | collective-permute-start | bytes 3538952 | tf_op jit(solution)/shard_map/ppermute | solution.py:465
  102.7 48.8 %collective-permute-start.20 = (bf16[1,256,2304]{2,1,0:T(8,128)(2,1)S(1)}, bf16[1,256,2304]{2,1,0:T(8,128)(2,1)S(1)}, u32[]{:S(2)}, u32[]{:S(2)}) collective-permute-start(bf16[1,256,2304]{2,1,0:T(8,128)(2,1)S(1)} %collective-permute-done.18.refs_8_.refs_11_), channel_id=1, source_target_pairs={{0,1},{1,0},{2,3},{3,2},{4,5},{5,4},{6,7},{7,6},{8,9},{9,8},{10,11... | collective-permute-start | bytes 3538952 | tf_op jit(solution)/shard_map/ppermute | solution.py:476
  174.6 29.7 %collective-permute-start.21 = (bf16[128,2304]{1,0:T(8,128)(2,1)}, bf16[128,2304]{1,0:T(8,128)(2,1)}, u32[]{:S(2)}, u32[]{:S(2)}) collective-permute-start(bf16[128,2304]{1,0:T(8,128)(2,1)} %collective-permute-done.17), channel_id=1, source_target_pairs={{0,2},{1,3},{2,6},{3,7},{4,0},{5,1},{6,4},{7,5},{8,10},{9,11},{10,... | collective-permute-start | bytes 1769480 | tf_op jit(solution)/shard_map/ppermute | solution.py:563
  209.8 23.8 %collective-permute-start.26 = (bf16[128,2304]{1,0:T(8,128)(2,1)}, bf16[128,2304]{1,0:T(8,128)(2,1)}, u32[]{:S(2)}, u32[]{:S(2)}) collective-permute-start(bf16[128,2304]{1,0:T(8,128)(2,1)} %collective-permute-done.21), channel_id=1, source_target_pairs={{0,2},{1,3},{2,6},{3,7},{4,0},{5,1},{6,4},{7,5},{8,10},{9,11},{10,... | collective-permute-start | bytes 1769480 | tf_op jit(solution)/shard_map/ppermute | solution.py:563
  240.2 535.1 %all-reduce.3.cloned.1.call-start = ((), (), s32[]{:S(2)}) async-start(), calls=%async_computation.7 | async-start | bytes 31850496 | tf_op jit(solution)/shard_map/psum | solution.py:907
  272.1 27.7 %collective-permute-start.38 = (bf16[128,2304]{1,0:T(8,128)(2,1)S(1)}, bf16[128,2304]{1,0:T(8,128)(2,1)S(1)}, u32[]{:S(2)}, u32[]{:S(2)}) collective-permute-start(bf16[128,2304]{1,0:T(8,128)(2,1)S(1)} %add_convert_fusion.6), channel_id=1, source_target_pairs={{0,2},{1,3},{2,6},{3,7},{4,0},{5,1},{6,4},{7,5},{8,10},{9,11},{10,... | collective-permute-start | bytes 1769480 | tf_op jit(solution)/shard_map/ppermute | solution.py:860
  288.5 32.2 %collective-permute-start.44 = (bf16[128,2304]{1,0:T(8,128)(2,1)S(1)}, bf16[128,2304]{1,0:T(8,128)(2,1)S(1)}, u32[]{:S(2)}, u32[]{:S(2)}) collective-permute-start(bf16[128,2304]{1,0:T(8,128)(2,1)S(1)} %slice.503), channel_id=1, source_target_pairs={{0,1},{1,0},{2,3},{3,2},{4,5},{5,4},{6,7},{7,6},{8,9},{9,8},{10,11... | collective-permute-start | bytes 1769480 | tf_op jit(solution)/shard_map/ppermute | solution.py:851
  390.0 84.7 %collective-permute-start.59 = (bf16[4,6,128,2304]{3,2,1,0:T(8,128)(2,1)}, bf16[4,6,128,2304]{3,2,1,0:T(8,128)(2,1)}, u32[]{:S(2)}, u32[]{:S(2)}) collective-permute-start(bf16[4,6,128,2304]{3,2,1,0:T(8,128)(2,1)} %bitcast.449), channel_id=1, source_target_pairs={{0,1},{1,0},{2,3},{3,2},{4,5},{5,4},{6,7},{7,6},{8,9},{9,8},{10,11... | collective-permute-start | bytes 42467336 | tf_op jit(solution)/shard_map/ppermute | solution.py:916
  591.7 40.1 %all-to-all-start.1 = ((bf16[4,2,64,1024]{3,2,1,0:T(8,128)(2,1)}), bf16[4,2,64,1024]{3,2,1,0:T(8,128)(2,1)S(1)}, u32[]{:S(2)}, u32[]{:S(2)}) async-start(bf16[4,2,64,1024]{3,2,1,0:T(8,128)(2,1)} %pad_maximum_fusion.1), calls=%async_computation.1 | async-start | bytes 2097152 | tf_op jit(solution)/shard_map/cond/branch_1_fun/all_to_all | solution.py:947
  595.4 36.4 %collective-permute-start = (bf16[128,2304]{1,0:T(8,128)(2,1)}, bf16[128,2304]{1,0:T(8,128)(2,1)}, u32[]{:S(2)}, u32[]{:S(2)}) collective-permute-start(bf16[128,2304]{1,0:T(8,128)(2,1)} %multiply_convert_fusion.refs_8_), channel_id=1, source_target_pairs={{2,4},{3,5},{4,6},{5,7},{10,12},{11,13},{12,14},{13,15},{18,20},{1... | collective-permute-start | bytes 1769480 | tf_op jit(solution)/shard_map/cond/branch_1_fun/ppermute | solution.py:575
  596.9 35.0 %collective-permute-start.1 = (bf16[128,2304]{1,0:T(8,128)(2,1)}, bf16[128,2304]{1,0:T(8,128)(2,1)}, u32[]{:S(2)}, u32[]{:S(2)}) collective-permute-start(bf16[128,2304]{1,0:T(8,128)(2,1)} %multiply_convert_fusion.refs_8_), channel_id=1, source_target_pairs={{0,4},{1,5},{2,6},{3,7},{8,12},{9,13},{10,14},{11,15},{16,20},{17,... | collective-permute-start | bytes 1769480 | tf_op jit(solution)/shard_map/cond/branch_1_fun/ppermute | solution.py:575
  604.3 27.5 %collective-permute-start.2 = (bf16[128,2304]{1,0:T(8,128)(2,1)}, bf16[128,2304]{1,0:T(8,128)(2,1)}, u32[]{:S(2)}, u32[]{:S(2)}) collective-permute-start(bf16[128,2304]{1,0:T(8,128)(2,1)} %multiply_convert_fusion.refs_8_), channel_id=1, source_target_pairs={{0,6},{1,7},{6,4},{7,5},{8,14},{9,15},{14,12},{15,13},{16,22},{17,... | collective-permute-start | bytes 1769480 | tf_op jit(solution)/shard_map/cond/branch_1_fun/ppermute | solution.py:575
  634.8 59.1 %all-to-all-start.3 = ((bf16[8,128,768]{1,2,0:T(8,128)(2,1)}), bf16[8,128,768]{1,2,0:T(8,128)(2,1)}, u32[]{:S(2)}, u32[]{:S(2)}) async-start(bf16[8,128,768]{1,2,0:T(8,128)(2,1)} %bitcast.463), calls=%async_computation.3 | async-start | bytes 3145728 | tf_op jit(solution)/shard_map/cond/branch_1_fun/all_to_all | solution.py:975
  666.3 30.2 %collective-permute-start.10 = (bf16[128,2304]{1,0:T(8,128)(2,1)}, bf16[128,2304]{1,0:T(8,128)(2,1)S(1)}, u32[]{:S(2)}, u32[]{:S(2)}) collective-permute-start(bf16[128,2304]{1,0:T(8,128)(2,1)} %collective-permute-done.2.refs_14_), channel_id=1, source_target_pairs={{0,1},{1,0},{2,3},{3,2},{4,5},{5,4},{6,7},{7,6},{8,9},{9,8},{10,11... | collective-permute-start | bytes 1769480 | tf_op jit(solution)/shard_map/cond/branch_1_fun/ppermute | solution.py:593
  666.7 29.8 %collective-permute-start.7 = (bf16[128,2304]{1,0:T(8,128)(2,1)}, bf16[128,2304]{1,0:T(8,128)(2,1)}, u32[]{:S(2)}, u32[]{:S(2)}) collective-permute-start(bf16[128,2304]{1,0:T(8,128)(2,1)} %multiply_convert_fusion.refs_8_), channel_id=1, source_target_pairs={{0,1},{1,0},{2,3},{3,2},{4,5},{5,4},{6,7},{7,6},{8,9},{9,8},{10,11... | collective-permute-start | bytes 1769480 | tf_op jit(solution)/shard_map/cond/branch_1_fun/ppermute | solution.py:593
  666.9 29.6 %collective-permute-start.8 = (bf16[128,2304]{1,0:T(8,128)(2,1)}, bf16[128,2304]{1,0:T(8,128)(2,1)}, u32[]{:S(2)}, u32[]{:S(2)}) collective-permute-start(bf16[128,2304]{1,0:T(8,128)(2,1)} %collective-permute-done.refs_10_), channel_id=1, source_target_pairs={{0,1},{1,0},{2,3},{3,2},{4,5},{5,4},{6,7},{7,6},{8,9},{9,8},{10,11... | collective-permute-start | bytes 1769480 | tf_op jit(solution)/shard_map/cond/branch_1_fun/ppermute | solution.py:593
  667.2 29.3 %collective-permute-start.9 = (bf16[128,2304]{1,0:T(8,128)(2,1)}, bf16[128,2304]{1,0:T(8,128)(2,1)}, u32[]{:S(2)}, u32[]{:S(2)}) collective-permute-start(bf16[128,2304]{1,0:T(8,128)(2,1)} %collective-permute-done.1.refs_12_), channel_id=1, source_target_pairs={{0,1},{1,0},{2,3},{3,2},{4,5},{5,4},{6,7},{7,6},{8,9},{9,8},{10,11... | collective-permute-start | bytes 1769480 | tf_op jit(solution)/shard_map/cond/branch_1_fun/ppermute | solution.py:593
  712.2 47.3 %collective-permute-start.65 = (bf16[2,192,1152]{2,1,0:T(8,128)(2,1)S(1)}, bf16[2,192,1152]{2,1,0:T(8,128)(2,1)}, u32[]{:S(2)}, u32[]{:S(2)}) collective-permute-start(bf16[2,192,1152]{2,1,0:T(8,128)(2,1)S(1)} %pad_maximum_fusion.6), channel_id=1, source_target_pairs={{0,16},{8,24},{16,0},{24,8},{1,17},{9,25},{17,1},{25,9},{2,18},{10... | collective-permute-start | bytes 2654216 | tf_op jit(solution)/shard_map/ppermute | solution.py:684
  714.8 44.7 %collective-permute-start.64 = (bf16[2,192,1152]{2,1,0:T(8,128)(2,1)}, bf16[2,192,1152]{2,1,0:T(8,128)(2,1)}, u32[]{:S(2)}, u32[]{:S(2)}) collective-permute-start(bf16[2,192,1152]{2,1,0:T(8,128)(2,1)} %pad_maximum_fusion.5), channel_id=1, source_target_pairs={{0,8},{8,0},{16,24},{24,16},{1,9},{9,1},{17,25},{25,17},{2,10},{10... | collective-permute-start | bytes 2654216 | tf_op jit(solution)/shard_map/ppermute | solution.py:684
  729.3 26.0 %collective-permute-start.69 = (f32[4,288]{1,0:T(4,128)S(1)}, f32[4,288]{1,0:T(4,128)S(1)}, u32[]{:S(2)}, u32[]{:S(2)}) collective-permute-start(f32[4,288]{1,0:T(4,128)S(1)} %dynamic-slice_add_fusion), channel_id=1, source_target_pairs={{0,8},{8,0},{16,24},{24,16},{1,9},{9,1},{17,25},{25,17},{2,10},{10... | collective-permute-start | bytes 13832 | tf_op jit(solution)/shard_map/ppermute | solution.py:729
  (153 other events, 1508.6 us)
Sparse Core Ops, SparseCore 0:
  9.8 40.1 all-gather.8
  85.6 64.1 all-gather.6
  240.3 134.0 all-gather.10
  421.4 334.2 all-reduce.2

commit v7 on v6

--- a/solution.py
+++ b/solution.py
@@ -934,24 +934,36 @@
         mixed_rows = lax.all_to_all(mixed, "seq", split_axis=0, concat_axis=0, tiled=True)
         mixed_rows = mixed_rows.transpose(1, 2, 0, 3).reshape(own_rows, HQ * HD)
         shard_cols = attn_weight.shape[0]
-        first_owner = (HQ + 2 * KVH) * HD // shard_cols // 2
-        later_pieces = direct_pieces(
-            grad_attn_low, shard, shards, range(first_owner, shards // 2)
-        )
-        grad_queries, grad_kv = attend_back(shard_arg, queries, grad_heads, lse, kv_all)
-        grad_kv_own = (
-            ring_scatter(grad_kv.reshape(shards, columns * own_rows, 2 * HD), shard, shards)
-            .astype(bf16)
-            .reshape(columns, seqs, rows, 2 * HD)
-        )
-        grad_proj = lax.all_to_all(
-            jnp.concatenate([grad_queries, grad_kv_own], axis=-1),
-            "seq",
-            split_axis=0,
-            concat_axis=0,
-            tiled=True,
-        )
-        attn_pieces, grad_proj = later_pieces(grad_proj)
+        made = {"heads": grad_heads}
+
+        def beside_back(step, held):
+            if step == 1:
+                held, made["heads"] = lax.optimization_barrier((held, made["heads"]))
+                made["queries"], made["kv"] = attend_back(
+                    shard_arg, queries, made["heads"], lse, kv_all
+                )
+            if step == 2:
+                held, made["kv"] = lax.optimization_barrier((held, made["kv"]))
+                grad_kv_own = (
+                    ring_scatter(
+                        made["kv"].reshape(shards, columns * own_rows, 2 * HD), shard, shards
+                    )
+                    .astype(bf16)
+                    .reshape(columns, seqs, rows, 2 * HD)
+                )
+                made["proj"] = lax.all_to_all(
+                    jnp.concatenate([made["queries"], grad_kv_own], axis=-1),
+                    "seq",
+                    split_axis=0,
+                    concat_axis=0,
+                    tiled=True,
+                )
+            if step == 3:
+                held, made["proj"] = lax.optimization_barrier((held, made["proj"]))
+            return held
+
+        attn_pieces = ring_pieces(grad_attn_low, shard, shards, beside_back)
+        grad_proj = made["proj"]
         grad_rows = grad_proj.reshape(columns, own_rows, (per + 2) * HD).transpose(1, 0, 2)
         grad_normed = dot_nn(grad_rows.reshape(own_rows, -1), weight_in_all)
         grad_tokens, gain_pre_attn = norm_back(flat_tokens, gain_rows[0], grad_normed)

time: 831 us -> 827 us (level)
  starting transfers between devices: 162 us -> 137 us
  blocking collectives: 15.7 us -> 33.7 us
    all_to_all x0 -> x1, blocking collectives: none -> 18 us  [attention_back(): lax.all_to_all(grad_mixed.transpose(2, 0, 1, 3), 'seq', split_axis=0, con...]
    all_to_all x1, starting transfers between devices: 21.2 us -> 4.54 us  [attention_back(): lax.all_to_all(weight_cols.reshape(own_rows, shards, shard_cols).transpos...]
    all_to_all x2 -> x1, waiting for transfers between devices: 14.7 us -> 0.01 us  [beside_back(): lax.all_to_all(jnp.concatenate([made['queries'], grad_kv_own], axis=-1),...]
    ppermute x7 -> x0, starting transfers between devices: 12.2 us -> none  [the longest x3 11.1 us: direct_pieces(): lax.ppermute(block, 'fsdp', [(f, (f + 2 * hop) % shards) for f in range(s...]
    ppermute x4, waiting for transfers between devices: 12.9 us -> 24.6 us  [column_scatter(): lax.ppermute(away.astype(bf16), 'seq', partners(4, second)).astype(f32)]
  transfers between devices with their start and end apart: 85 -> 84, of which waited for: 37 -> 37; matrix products, arithmetic and copies ran while one was open for 28% -> 28% of each run, Pallas kernels for 15% -> 15%
where the time goes in v7:
time: 827 us; the launch traced here: 816 us
  waiting for transfers between devices  243 us (29%)
  starting transfers between devices  137 us (17%)
  matrix products  131 us (16%)
  Pallas kernels  123 us (15%)
  local copies, waits for them, and re-layouts  62.3 us (8%)
  other arithmetic  55.2 us (7%)
  blocking collectives  33.7 us (4%)
  between operations  18.2 us (2%)
  loops' own time  12.8 us (2%)
    pallas_call x9, Pallas kernels, pick(): pl.pallas_call(functools.partial(kernel, cands), grid_spec=pltpu.Prefetch...  61.6 us
    ppermute x6, waiting for transfers between devices, pipeline(): total = lax.ppermute(total, 'fsdp', ring).astype(f32)  60 us
    ppermute x4, starting transfers between devices, routed_weights(): sources['swapped%d' % number] = lax.ppermute(got, 'fsdp', swap)  52.8 us
    ppermute x5, waiting for transfers between devices, sum_over(): lax.ppermute(value, axis, [(c, c ^ bit) for c in range(count)])  40.2 us
    dot_general x5, matrix products, dot_nn(): lax.dot_general(a, b, (((1,), (0,)), ((), ())), preferred_element_type=f32)  31.1 us
    ppermute x3, waiting for transfers between devices, ring_scatter(): lax.ppermute(total.astype(bf16), 'fsdp', pairs).astype(f32)  30.4 us
    dot_general x4, matrix products, forward(): jnp.einsum('td,fgd->tgf', rows_here, weight_gate_up, preferred_element_ty...  28.9 us
    dot_general x5, matrix products, dot_nt(): lax.dot_general(a, b, (((1,), (1,)), ((), ())), preferred_element_type=f32)  25.3 us
  transfers between devices with their start and end apart: 84, of which 37 were waited for; matrix products, arithmetic and copies ran while one was open for 28% of the time, Pallas kernels for 15%

profile of v7, /device:TPU:0, one launch (start us, length us, event | category | flops | bytes accessed | tf_op | source)
XLA Modules:
  0.0 815.8 jit_solution(4135855611370536247)
XLA Ops:
  8.0 15.7 %all-gather.2 = bf16[8,288,4]{1,2,0:T(4,128)(2,1)S(1)} all-gather(bf16[1,288,4]{1,2,0:T(4,128)(2,1)} %bitcast.497), channel_id=1, replica_groups=mesh['seq'=4,'fsdp'=8] {'fsdp'}, dimensions={0}, use_global_device_ids=true | all-gather | bytes 20736 | tf_op jit(solution)/shard_map/all_gather | solution.py:771
  102.8 45.3 %collective-permute-start.20 = (bf16[1,256,2304]{2,1,0:T(8,128)(2,1)S(1)}, bf16[1,256,2304]{2,1,0:T(8,128)(2,1)S(1)}, u32[]{:S(2)}, u32[]{:S(2)}) collective-permute-start(bf16[1,256,2304]{2,1,0:T(8,128)(2,1)S(1)} %collective-permute-done.18.refs_8_.refs_11_), channel_id=1, source_target_pairs={{0,1},{1,0},{2,3},{3,2},{4,5},{5,4},{6,7},{7,6},{8,9},{9,8},{10,11... | collective-permute-start | bytes 3538952 | tf_op jit(solution)/shard_map/ppermute | solution.py:476
  159.0 13.1 %attend.1 = (bf16[4,2,64,512]{3,2,1,0:T(8,128)(2,1)}, f32[4,2,128,128]{3,2,1,0:T(8,128)}) custom-call(s32[1]{0:T(128)} %bitcast.72.shard_ref, bf16[4,2,64,512]{3,2,1,0:T(8,128)(2,1)S(1)} %bitcast.470, bf16[8,4,2,64,512]{4,3,2,1,0:T(8,128)(2,1)} %all-gather.7.cloned.1.call-done.kv_ref), custom_call_target="tpu_custom_call" | custom-call | tf_op jit(solution)/shard_map/attend/pallas_call | solution.py:172
  195.9 8.4 %collective-permute-done.21 = bf16[128,2304]{1,0:T(8,128)(2,1)} collective-permute-done((bf16[128,2304]{1,0:T(8,128)(2,1)}, bf16[128,2304]{1,0:T(8,128)(2,1)}, u32[]{:S(2)}, u32[]{:S(2)}) %collective-permute-start.21) | collective-permute-done | bytes 589856 | tf_op jit(solution)/shard_map/ppermute | solution.py:563
  274.9 8.4 %convolution_bitcast_fusion.5 = f32[256,2,1152]{2,0,1:T(8,128)} fusion(bf16[1152,3,2304]{2,0,1:T(8,128)(2,1)} %param.27, bf16[128,2304]{1,0:T(8,128)(2,1)S(1)} %collective-permute-done.37, bf16[128,2304]{1,0:T(8,128)(2,1)S(1)} %collective-permute-done.33), kind=kOutput, calls=%fused_computation.82 | convolution fusion | flops 2720268288 | bytes 14155776 | tf_op jit(solution)/shard_map/td,fgd->tgf/dot_general | solution.py:873
  289.2 10.8 %collective-permute-done.38 = bf16[128,2304]{1,0:T(8,128)(2,1)S(1)} collective-permute-done((bf16[128,2304]{1,0:T(8,128)(2,1)S(1)}, bf16[128,2304]{1,0:T(8,128)(2,1)S(1)}, u32[]{:S(2)}, u32[]{:S(2)}) %collective-permute-start.38) | collective-permute-done | bytes 589856 | tf_op jit(solution)/shard_map/ppermute | solution.py:860
  302.3 8.4 %convolution_bitcast_fusion.4 = f32[256,2,1152]{2,0,1:T(8,128)} fusion(bf16[1152,3,2304]{2,0,1:T(8,128)(2,1)} %param.27, bf16[128,2304]{1,0:T(8,128)(2,1)S(1)} %collective-permute-done.41, bf16[128,2304]{1,0:T(8,128)(2,1)S(1)} %collective-permute-done.36), kind=kOutput, calls=%fused_computation.81 | convolution fusion | flops 2720268288 | bytes 14155776 | tf_op jit(solution)/shard_map/td,fgd->tgf/dot_general | solution.py:873
  320.8 13.6 %collective-permute-done.43 = bf16[128,2304]{1,0:T(8,128)(2,1)S(1)} collective-permute-done((bf16[128,2304]{1,0:T(8,128)(2,1)S(1)}, bf16[128,2304]{1,0:T(8,128)(2,1)S(1)}, u32[]{:S(2)}, u32[]{:S(2)}) %collective-permute-start.43) | collective-permute-done | bytes 589856 | tf_op jit(solution)/shard_map/ppermute | solution.py:860
  345.8 8.4 %fusion.25 = bf16[256,2304]{1,0:T(8,128)(2,1)} fusion(bf16[1152,3,2304]{2,0,1:T(8,128)(2,1)} %param.27, bf16[256,1,1152]{2,0,1:T(8,128)(2,1)S(1)} %get-tuple-element.446, bf16[256,1,1152]{2,0,1:T(8,128)(2,1)S(1)} %get-tuple-element.445), kind=kOutput, calls=%fused_computation.72 | convolution fusion | flops 2719088640 | bytes 12976128 | tf_op jit(solution)/shard_map/tgf,fgd->td/dot_general | solution.py:895
  446.2 13.4 %collective-permute-done.56 = bf16[128,2304]{1,0:T(8,128)(2,1)S(1)} collective-permute-done((bf16[128,2304]{1,0:T(8,128)(2,1)S(1)}, bf16[128,2304]{1,0:T(8,128)(2,1)S(1)}, u32[]{:S(2)}, u32[]{:S(2)}) %collective-permute-start.56) | collective-permute-done | bytes 589856 | tf_op jit(solution)/shard_map/ppermute | solution.py:867
  461.6 13.0 %collective-permute-done.57 = bf16[128,2304]{1,0:T(8,128)(2,1)S(1)} collective-permute-done((bf16[128,2304]{1,0:T(8,128)(2,1)S(1)}, bf16[128,2304]{1,0:T(8,128)(2,1)S(1)}, u32[]{:S(2)}, u32[]{:S(2)}) %collective-permute-start.57) | collective-permute-done | bytes 589856 | tf_op jit(solution)/shard_map/ppermute | solution.py:867
  474.8 8.5 %pick.11 = bf16[16,128,2304]{2,1,0:T(8,128)(2,1)} custom-call(s32[16]{0:T(128)} %get-tuple-element.472.which_ref, s32[16]{0:T(128)} %get-tuple-element.471.slot_ref, bf16[24,128,2304]{2,1,0:T(8,128)(2,1)} %all-gather.11.cloned.1.call-done, bf16[24,128,2304]{2,1,0:T(8,128)(2,1)} %bitcast.131.refs_1_), custom_call_target="tpu_custom_call" | custom-call | tf_op jit(solution)/shard_map/pick/pallas_call | solution.py:398
  483.4 202.9 %conditional.1 = (bf16[768,2304]{1,0:T(8,128)(2,1)}, f32[4,2304]{1,0:T(4,128)}, f32[2,64,2304]{2,1,0:T(8,128)}) conditional(s32[]{:T(128)} %convert_element_type.461, () %tuple.72, (s32[]{:T(128)}, pred[]{:T(512)}, (), s32[]{:T(128)}, (), /*index=5*/f32[128,2304]{1,0:T(8,128)S(1)}, f32[128,2304]{1,0:T(8,128)S(1)}, f32[4,2304]{1,0:T(4,128)S(1)}, ...), branch_computations={%region_6.7_spmd, %region_7.18_spmd} | conditional | flops 3651291648 | bytes 189276960 | solution.py:1013
  494.6 18.0 %all_to_all.16.do_ref = bf16[4,2,64,512]{3,2,1,0:T(8,128)(2,1)} all-to-all(bf16[4,2,64,512]{3,2,1,0:T(8,128)(2,1)S(1)} %bitcast.480), channel_id=1, replica_groups=mesh['seq'=4,'fsdp'=8] {'seq'}, dimensions={0} | all-to-all | bytes 1048576 | tf_op jit(solution)/shard_map/cond/branch_1_fun/all_to_all | solution.py:931
  514.8 22.0 %attend_back.1 = (bf16[4,2,64,512]{3,2,1,0:T(8,128)(2,1)}, bf16[8,4,2,64,512]{4,3,2,1,0:T(8,128)(2,1)}) custom-call(s32[1]{0:T(128)} %get-tuple-element.131.shard_ref, bf16[4,2,64,512]{3,2,1,0:T(8,128)(2,1)S(1)} %copy-done.24, bf16[4,2,64,512]{3,2,1,0:T(8,128)(2,1)} %all_to_all.16.do_ref, f32[4,2,128,128]{3,2,1,0:T(8,128)S(1)} %copy-done.48, ...), custom_call_target="tpu_custom_call" | custom-call | tf_op jit(solution)/shard_map/cond/branch_1_fun/attend_back/pallas_call | solution.py:203
  548.4 11.1 %collective-permute-done.4 = bf16[512,512]{1,0:T(8,128)(2,1)S(1)} collective-permute-done((bf16[512,512]{1,0:T(8,128)(2,1)S(1)}, bf16[512,512]{1,0:T(8,128)(2,1)S(1)}, u32[]{:S(2)}, u32[]{:S(2)}) %collective-permute-start.4) | collective-permute-done | bytes 524320 | tf_op jit(solution)/shard_map/cond/branch_1_fun/ppermute | solution.py:672
  563.6 11.6 %collective-permute-done.5 = bf16[512,512]{1,0:T(8,128)(2,1)S(1)} collective-permute-done((bf16[512,512]{1,0:T(8,128)(2,1)S(1)}, bf16[512,512]{1,0:T(8,128)(2,1)S(1)}, u32[]{:S(2)}, u32[]{:S(2)}) %collective-permute-start.5) | collective-permute-done | bytes 524320 | tf_op jit(solution)/shard_map/cond/branch_1_fun/ppermute | solution.py:672
  605.6 14.9 %pick.6 = bf16[32,128,2304]{2,1,0:T(8,128)(2,1)} custom-call(s32[32]{0:T(128)} %get-tuple-element.415.which_ref, s32[32]{0:T(128)} %get-tuple-element.414.slot_ref, bf16[24,128,2304]{2,1,0:T(8,128)(2,1)} %bitcast.455, bf16[24,128,2304]{2,1,0:T(8,128)(2,1)} %bitcast.54.refs_1_), custom_call_target="tpu_custom_call" | custom-call | tf_op jit(solution)/shard_map/cond/branch_1_fun/pick/pallas_call | solution.py:398
  633.3 9.3 %multiply_reduce_fusion = (f32[128]{0:T(128)S(1)}, f32[2304]{0:T(1024)S(1)}, f32[128,2304]{1,0:T(8,128)S(1)}) fusion(f32[128,2304]{1,0:T(8,128)S(1)} %get-tuple-element.156, f32[2304]{0:T(1024)S(1)} %get-tuple-element.392, f32[128]{0:T(128)S(1)} %add_rsqrt_fusion, bf16[128,4096]{0,1:T(8,128)(2,1)S(1)} %bitcast.459, bf16[4096,2304]{1,0:T(8,128)(2,1)} %bitcast.452), kind=kOutput, calls=%fused_computation.4 | convolution fusion | flops 2417686272 | bytes 22301696 | tf_op jit(solution)/shard_map/cond/branch_1_fun/dot_general | solution.py:48
  645.2 25.3 %all-to-all-done.3 = bf16[8,128,768]{1,2,0:T(8,128)(2,1)} async-done(((bf16[8,128,768]{1,2,0:T(8,128)(2,1)}), bf16[8,128,768]{1,2,0:T(8,128)(2,1)}, u32[]{:S(2)}, u32[]{:S(2)}) %all-to-all-start.3) | async-done | bytes 1572896 | tf_op jit(solution)/shard_map/cond/branch_1_fun/all_to_all | solution.py:987
  673.9 12.4 %weight_grad.1 = bf16[768,2304]{1,0:T(8,128)(2,1)} custom-call(s32[17]{0:T(128)} %stack.119.place_ref, bf16[1024,768]{1,0:T(8,128)(2,1)} %bitcast.468, bf16[128,2304]{1,0:T(8,128)(2,1)} %get-tuple-element.143.refs_0_, bf16[128,2304]{1,0:T(8,128)(2,1)} %get-tuple-element.144.refs_1_, bf16[128,2304]{1,0:T(8,128)(2,1)} %get-tuple-element.145.refs_2_, ...), custom_call_target="tpu_custom_call" | custom-call | tf_op jit(solution)/shard_map/cond/branch_1_fun/weight_grad/pallas_call | solution.py:634
  706.6 26.5 %collective-permute-done.69 = f32[4,288]{1,0:T(4,128)S(1)} collective-permute-done((f32[4,288]{1,0:T(4,128)S(1)}, f32[4,288]{1,0:T(4,128)S(1)}, u32[]{:S(2)}, u32[]{:S(2)}) %collective-permute-start.69) | collective-permute-done | bytes 4640 | tf_op jit(solution)/shard_map/ppermute | solution.py:729
  742.2 17.9 %collective-permute-done.72 = bf16[192,1152]{1,0:T(8,128)(2,1)S(1)} collective-permute-done((bf16[192,1152]{1,0:T(8,128)(2,1)S(1)}, bf16[192,1152]{1,0:T(8,128)(2,1)S(1)}, u32[]{:S(2)}, u32[]{:S(2)}) %collective-permute-start.72) | collective-permute-done | bytes 442400 | tf_op jit(solution)/shard_map/ppermute | solution.py:698
  768.3 8.5 %collective-permute-done.73 = bf16[192,1152]{1,0:T(8,128)(2,1)S(1)} collective-permute-done((bf16[192,1152]{1,0:T(8,128)(2,1)S(1)}, bf16[192,1152]{1,0:T(8,128)(2,1)S(1)}, u32[]{:S(2)}, u32[]{:S(2)}) %collective-permute-start.73) | collective-permute-done | bytes 442400 | tf_op jit(solution)/shard_map/ppermute | solution.py:711
  (527 shorter events, 440.1 us)
Async XLA Ops:
  7.2 50.2 %all-gather.9.cloned.1.call-start = ((), (), s32[]{:S(2)}) async-start(), calls=%async_computation.5 | async-start | bytes 2949120 | tf_op jit(solution)/shard_map/all_gather | solution.py:770
  7.9 142.3 %all-gather.7.cloned.1.call-start = ((), (), s32[]{:S(2)}) async-start(), calls=%async_computation.4 | async-start | bytes 4718592 | tf_op jit(solution)/shard_map/all_gather | solution.py:795
  85.5 302.4 %all-gather.11.cloned.1.call-start = ((), (), s32[]{:S(2)}) async-start(), calls=%async_computation.6 | async-start | bytes 17694720 | tf_op jit(solution)/shard_map/all_gather | solution.py:836
  99.3 74.7 %collective-permute-start.22 = (bf16[1,256,2304]{2,1,0:T(8,128)(2,1)}, bf16[1,256,2304]{2,1,0:T(8,128)(2,1)}, u32[]{:S(2)}, u32[]{:S(2)}) collective-permute-start(bf16[1,256,2304]{2,1,0:T(8,128)(2,1)} %get-tuple-element.433), channel_id=1, source_target_pairs={{4,6},{27,25}} | collective-permute-start | bytes 3538952 | tf_op jit(solution)/shard_map/ppermute | solution.py:465
  101.1 73.0 %collective-permute-start.23 = (bf16[1,256,2304]{2,1,0:T(8,128)(2,1)}, bf16[1,256,2304]{2,1,0:T(8,128)(2,1)}, u32[]{:S(2)}, u32[]{:S(2)}) collective-permute-start(bf16[1,256,2304]{2,1,0:T(8,128)(2,1)} %get-tuple-element.431), channel_id=1, source_target_pairs={{4,6},{27,25}} | collective-permute-start | bytes 3538952 | tf_op jit(solution)/shard_map/ppermute | solution.py:465
  102.8 48.7 %collective-permute-start.20 = (bf16[1,256,2304]{2,1,0:T(8,128)(2,1)S(1)}, bf16[1,256,2304]{2,1,0:T(8,128)(2,1)S(1)}, u32[]{:S(2)}, u32[]{:S(2)}) collective-permute-start(bf16[1,256,2304]{2,1,0:T(8,128)(2,1)S(1)} %collective-permute-done.18.refs_8_.refs_11_), channel_id=1, source_target_pairs={{0,1},{1,0},{2,3},{3,2},{4,5},{5,4},{6,7},{7,6},{8,9},{9,8},{10,11... | collective-permute-start | bytes 3538952 | tf_op jit(solution)/shard_map/ppermute | solution.py:476
  174.7 29.7 %collective-permute-start.21 = (bf16[128,2304]{1,0:T(8,128)(2,1)}, bf16[128,2304]{1,0:T(8,128)(2,1)}, u32[]{:S(2)}, u32[]{:S(2)}) collective-permute-start(bf16[128,2304]{1,0:T(8,128)(2,1)} %collective-permute-done.17), channel_id=1, source_target_pairs={{0,2},{1,3},{2,6},{3,7},{4,0},{5,1},{6,4},{7,5},{8,10},{9,11},{10,... | collective-permute-start | bytes 1769480 | tf_op jit(solution)/shard_map/ppermute | solution.py:563
  209.9 23.8 %collective-permute-start.26 = (bf16[128,2304]{1,0:T(8,128)(2,1)}, bf16[128,2304]{1,0:T(8,128)(2,1)}, u32[]{:S(2)}, u32[]{:S(2)}) collective-permute-start(bf16[128,2304]{1,0:T(8,128)(2,1)} %collective-permute-done.21), channel_id=1, source_target_pairs={{0,2},{1,3},{2,6},{3,7},{4,0},{5,1},{6,4},{7,5},{8,10},{9,11},{10,... | collective-permute-start | bytes 1769480 | tf_op jit(solution)/shard_map/ppermute | solution.py:563
  240.3 524.4 %all-reduce.3.cloned.1.call-start = ((), (), s32[]{:S(2)}) async-start(), calls=%async_computation.7 | async-start | bytes 31850496 | tf_op jit(solution)/shard_map/psum | solution.py:907
  272.2 27.7 %collective-permute-start.38 = (bf16[128,2304]{1,0:T(8,128)(2,1)S(1)}, bf16[128,2304]{1,0:T(8,128)(2,1)S(1)}, u32[]{:S(2)}, u32[]{:S(2)}) collective-permute-start(bf16[128,2304]{1,0:T(8,128)(2,1)S(1)} %add_convert_fusion.6), channel_id=1, source_target_pairs={{0,2},{1,3},{2,6},{3,7},{4,0},{5,1},{6,4},{7,5},{8,10},{9,11},{10,... | collective-permute-start | bytes 1769480 | tf_op jit(solution)/shard_map/ppermute | solution.py:860
  288.6 32.2 %collective-permute-start.44 = (bf16[128,2304]{1,0:T(8,128)(2,1)S(1)}, bf16[128,2304]{1,0:T(8,128)(2,1)S(1)}, u32[]{:S(2)}, u32[]{:S(2)}) collective-permute-start(bf16[128,2304]{1,0:T(8,128)(2,1)S(1)} %slice.523), channel_id=1, source_target_pairs={{0,1},{1,0},{2,3},{3,2},{4,5},{5,4},{6,7},{7,6},{8,9},{9,8},{10,11... | collective-permute-start | bytes 1769480 | tf_op jit(solution)/shard_map/ppermute | solution.py:851
  390.1 84.6 %collective-permute-start.59 = (bf16[4,6,128,2304]{3,2,1,0:T(8,128)(2,1)}, bf16[4,6,128,2304]{3,2,1,0:T(8,128)(2,1)}, u32[]{:S(2)}, u32[]{:S(2)}) collective-permute-start(bf16[4,6,128,2304]{3,2,1,0:T(8,128)(2,1)} %bitcast.453), channel_id=1, source_target_pairs={{0,1},{1,0},{2,3},{3,2},{4,5},{5,4},{6,7},{7,6},{8,9},{9,8},{10,11... | collective-permute-start | bytes 42467336 | tf_op jit(solution)/shard_map/ppermute | solution.py:916
  487.6 25.0 %collective-permute-start = (bf16[128,2304]{1,0:T(8,128)(2,1)}, bf16[128,2304]{1,0:T(8,128)(2,1)}, u32[]{:S(2)}, u32[]{:S(2)}) collective-permute-start(bf16[128,2304]{1,0:T(8,128)(2,1)} %multiply_convert_fusion.refs_8_), channel_id=1, source_target_pairs={{0,2},{1,3},{2,6},{3,7},{4,0},{5,1},{6,4},{7,5},{8,10},{9,11},{10,... | collective-permute-start | bytes 1769480 | tf_op jit(solution)/shard_map/cond/branch_1_fun/ppermute | solution.py:563
  512.6 24.2 %collective-permute-start.1 = (bf16[128,2304]{1,0:T(8,128)(2,1)}, bf16[128,2304]{1,0:T(8,128)(2,1)}, u32[]{:S(2)}, u32[]{:S(2)}) collective-permute-start(bf16[128,2304]{1,0:T(8,128)(2,1)} %collective-permute-done.refs_10_), channel_id=1, source_target_pairs={{0,2},{1,3},{2,6},{3,7},{4,0},{5,1},{6,4},{7,5},{8,10},{9,11},{10,... | collective-permute-start | bytes 1769480 | tf_op jit(solution)/shard_map/cond/branch_1_fun/ppermute | solution.py:563
  592.5 32.6 %all-to-all-start.1 = ((bf16[4,2,64,1024]{3,2,1,0:T(8,128)(2,1)}), bf16[4,2,64,1024]{3,2,1,0:T(8,128)(2,1)S(1)}, u32[]{:S(2)}, u32[]{:S(2)}) async-start(bf16[4,2,64,1024]{3,2,1,0:T(8,128)(2,1)} %pad_maximum_fusion.1), calls=%async_computation.1 | async-start | bytes 2097152 | tf_op jit(solution)/shard_map/cond/branch_1_fun/all_to_all | solution.py:954
  596.2 28.9 %collective-permute-start.2 = (bf16[128,2304]{1,0:T(8,128)(2,1)}, bf16[128,2304]{1,0:T(8,128)(2,1)}, u32[]{:S(2)}, u32[]{:S(2)}) collective-permute-start(bf16[128,2304]{1,0:T(8,128)(2,1)} %collective-permute-done.1.refs_12_), channel_id=1, source_target_pairs={{0,2},{1,3},{2,6},{3,7},{4,0},{5,1},{6,4},{7,5},{8,10},{9,11},{10,... | collective-permute-start | bytes 1769480 | tf_op jit(solution)/shard_map/cond/branch_1_fun/ppermute | solution.py:563
  597.4 75.6 %collective-permute-start.7 = (bf16[128,2304]{1,0:T(8,128)(2,1)}, bf16[128,2304]{1,0:T(8,128)(2,1)}, u32[]{:S(2)}, u32[]{:S(2)}) collective-permute-start(bf16[128,2304]{1,0:T(8,128)(2,1)} %multiply_convert_fusion.refs_8_), channel_id=1, source_target_pairs={{0,1},{1,0},{2,3},{3,2},{4,5},{5,4},{6,7},{7,6},{8,9},{9,8},{10,11... | collective-permute-start | bytes 1769480 | tf_op jit(solution)/shard_map/cond/branch_1_fun/ppermute | solution.py:566
  628.1 42.4 %all-to-all-start.3 = ((bf16[8,128,768]{1,2,0:T(8,128)(2,1)}), bf16[8,128,768]{1,2,0:T(8,128)(2,1)}, u32[]{:S(2)}, u32[]{:S(2)}) async-start(bf16[8,128,768]{1,2,0:T(8,128)(2,1)} %bitcast.467), calls=%async_computation.3 | async-start | bytes 3145728 | tf_op jit(solution)/shard_map/cond/branch_1_fun/all_to_all | solution.py:987
  632.6 40.4 %collective-permute-start.8 = (bf16[128,2304]{1,0:T(8,128)(2,1)}, bf16[128,2304]{1,0:T(8,128)(2,1)}, u32[]{:S(2)}, u32[]{:S(2)}) collective-permute-start(bf16[128,2304]{1,0:T(8,128)(2,1)} %collective-permute-done.refs_10_), channel_id=1, source_target_pairs={{0,1},{1,0},{2,3},{3,2},{4,5},{5,4},{6,7},{7,6},{8,9},{9,8},{10,11... | collective-permute-start | bytes 1769480 | tf_op jit(solution)/shard_map/cond/branch_1_fun/ppermute | solution.py:566
  633.2 39.9 %collective-permute-start.9 = (bf16[128,2304]{1,0:T(8,128)(2,1)}, bf16[128,2304]{1,0:T(8,128)(2,1)}, u32[]{:S(2)}, u32[]{:S(2)}) collective-permute-start(bf16[128,2304]{1,0:T(8,128)(2,1)} %collective-permute-done.1.refs_12_), channel_id=1, source_target_pairs={{0,1},{1,0},{2,3},{3,2},{4,5},{5,4},{6,7},{7,6},{8,9},{9,8},{10,11... | collective-permute-start | bytes 1769480 | tf_op jit(solution)/shard_map/cond/branch_1_fun/ppermute | solution.py:566
  642.6 30.4 %collective-permute-start.10 = (bf16[128,2304]{1,0:T(8,128)(2,1)}, bf16[128,2304]{1,0:T(8,128)(2,1)S(1)}, u32[]{:S(2)}, u32[]{:S(2)}) collective-permute-start(bf16[128,2304]{1,0:T(8,128)(2,1)} %collective-permute-done.2.refs_14_), channel_id=1, source_target_pairs={{0,1},{1,0},{2,3},{3,2},{4,5},{5,4},{6,7},{7,6},{8,9},{9,8},{10,11... | collective-permute-start | bytes 1769480 | tf_op jit(solution)/shard_map/cond/branch_1_fun/ppermute | solution.py:566
  688.9 48.6 %collective-permute-start.65 = (bf16[2,192,1152]{2,1,0:T(8,128)(2,1)S(1)}, bf16[2,192,1152]{2,1,0:T(8,128)(2,1)}, u32[]{:S(2)}, u32[]{:S(2)}) collective-permute-start(bf16[2,192,1152]{2,1,0:T(8,128)(2,1)S(1)} %pad_maximum_fusion.6), channel_id=1, source_target_pairs={{0,16},{8,24},{16,0},{24,8},{1,17},{9,25},{17,1},{25,9},{2,18},{10... | collective-permute-start | bytes 2654216 | tf_op jit(solution)/shard_map/ppermute | solution.py:684
  691.8 45.7 %collective-permute-start.64 = (bf16[2,192,1152]{2,1,0:T(8,128)(2,1)}, bf16[2,192,1152]{2,1,0:T(8,128)(2,1)}, u32[]{:S(2)}, u32[]{:S(2)}) collective-permute-start(bf16[2,192,1152]{2,1,0:T(8,128)(2,1)} %pad_maximum_fusion.5), channel_id=1, source_target_pairs={{0,8},{8,0},{16,24},{24,16},{1,9},{9,1},{17,25},{25,17},{2,10},{10... | collective-permute-start | bytes 2654216 | tf_op jit(solution)/shard_map/ppermute | solution.py:684
  706.0 27.1 %collective-permute-start.69 = (f32[4,288]{1,0:T(4,128)S(1)}, f32[4,288]{1,0:T(4,128)S(1)}, u32[]{:S(2)}, u32[]{:S(2)}) collective-permute-start(f32[4,288]{1,0:T(4,128)S(1)} %dynamic-slice_add_fusion), channel_id=1, source_target_pairs={{0,8},{8,0},{16,24},{24,16},{1,9},{9,1},{17,25},{25,17},{2,10},{10... | collective-permute-start | bytes 13832 | tf_op jit(solution)/shard_map/ppermute | solution.py:729
  (151 other events, 1502.0 us)
Sparse Core Ops, SparseCore 0:
  9.8 40.2 all-gather.8
  85.7 63.6 all-gather.6
  240.4 134.0 all-gather.10
  421.5 343.1 all-reduce.2
